TPU v7x, 32 devices: a whole 2x2x4 slice. The times are simulated.
32 devices in a mesh: shot: 4 (over z), space: 8 (over y, x, core).
Axes of the slice: x: 2, y: 2, z: 4, core: 2. Of those that a mesh axis runs over, the one named last changes fastest.
Arguments:
- courant: float32 [64, 64, 256], P('space'), may hold values from 0.2 to 0.45
- field_old: float32 [4, 64, 64, 256], P('shot', 'space'), may hold values from -0.9 to 0.9
- field_now: float32 [4, 64, 64, 256], P('shot', 'space'), may hold values from -0.9 to 0.9
- adjoint_late: float32 [4, 64, 64, 256], P('shot', 'space'), may hold values from -0.9 to 0.9
- adjoint_now: float32 [4, 64, 64, 256], P('shot', 'space'), may hold values from -0.9 to 0.9
- source_x: int32 [4], P('shot'), may hold values from 0 to 63
- source_yz: int32 [4], P('shot'), may hold values from 0 to 16383
- wavelet: float32 [4, 2], P('shot'), may hold values from -18 to 18
- receiver_x: int32 [4, 256], P('shot'), may hold values from 0 to 63
- receiver_yz: int32 [4, 256], P('shot'), may hold values from 0 to 16383
- residual_trace: float32 [4, 256, 2], P('shot'), may hold values from -18 to 18
Outputs:
- speed_gradient: float32 [64, 64, 256], P('space', 'shot')
All inputs are finite; a program needn't handle non-finite values.
Results may differ from a plain program's by a relative error of at most 0.00002.
Values sent between devices are 32-bit elements; how exact they have to be, the bound alone decides.
No kernel may reach another device: no remote copies, remote signals or barrier semaphores. Data moves between devices by JAX's collectives and lax.ppermute only.
A program may use at most 64 MiB of HBM per device.

v0:
```python
import jax
import jax.numpy as jnp
from jax import lax
from jax.sharding import PartitionSpec as P

STENCIL_MIDDLE = -205.0 / 72.0
STENCIL_SIDE = (8.0 / 5.0, -1.0 / 5.0, 8.0 / 315.0, -1.0 / 560.0)


def with_halo(block, sides, width):
    for axis, dim in sides:
        count = lax.axis_size(axis)
        forward = [(i, i + 1) for i in range(count - 1)]
        backward = [(target, source) for source, target in forward]
        low = lax.ppermute(
            lax.slice_in_dim(block, block.shape[dim] - width, None, axis=dim), axis, forward
        )
        high = lax.ppermute(lax.slice_in_dim(block, 0, width, axis=dim), axis, backward)
        block = jnp.concatenate([low, block, high], axis=dim)
    return block


def laplace_x(widened):
    length = widened.shape[1] - 8
    size_y, size_z = (widened.shape[2], widened.shape[3])
    padded = jnp.pad(widened, ((0, 0), (0, 0), (4, 4), (4, 4)))

    def window(shift_x, shift_y, shift_z):
        return padded[
            :,
            4 + shift_x : 4 + shift_x + length,
            4 + shift_y : 4 + shift_y + size_y,
            4 + shift_z : 4 + shift_z + size_z,
        ]

    summed = 3.0 * STENCIL_MIDDLE * window(0, 0, 0)
    for offset in range(1, 5):
        weight = STENCIL_SIDE[offset - 1]
        summed = summed + weight * (
            window(offset, 0, 0)
            + window(-offset, 0, 0)
            + window(0, offset, 0)
            + window(0, -offset, 0)
            + window(0, 0, offset)
            + window(0, 0, -offset)
        )
    return summed


def inject(wavefield, cells_x, cells_yz, amounts, lower_x):
    shot_count, length = (wavefield.shape[0], wavefield.shape[1])
    local_x = cells_x - lower_x
    inside = (local_x >= 0) & (local_x < length)
    local_x = jnp.where(inside, local_x, length)
    shot_rows = jnp.broadcast_to(
        jnp.arange(shot_count, dtype=jnp.int32).reshape((shot_count,) + (1,) * (local_x.ndim - 1)),
        local_x.shape,
    )
    flattened = wavefield.reshape(shot_count, length, -1)
    flattened = flattened.at[shot_rows, local_x, cells_yz].add(amounts, mode="drop")
    return flattened.reshape(wavefield.shape)


def face_layers(wavefield):
    return with_halo(wavefield, (("space", 1),), 4)


def on_device(
    courant,
    field_old,
    field_now,
    adjoint_late,
    adjoint_now,
    source_x,
    source_yz,
    wavelet,
    receiver_x,
    receiver_yz,
    residual_trace,
):
    slab_cells = courant.shape[0]
    first_x = lax.axis_index("space") * slab_cells
    speed_sq = (courant * courant)[None]
    accel_one = inject(
        laplace_x(face_layers(field_now)), source_x, source_yz, wavelet[:, 0], first_x
    )
    field_mid = 2.0 * field_now - field_old + speed_sq * accel_one
    accel_two = inject(
        laplace_x(face_layers(field_mid)), source_x, source_yz, wavelet[:, 1], first_x
    )
    adjoint_mid = 2.0 * adjoint_now - adjoint_late + laplace_x(face_layers(speed_sq * adjoint_now))
    adjoint_mid = inject(adjoint_mid, receiver_x, receiver_yz, residual_trace[:, :, 0], first_x)
    adjoint_early = 2.0 * adjoint_mid - adjoint_now + laplace_x(face_layers(speed_sq * adjoint_mid))
    adjoint_early = inject(adjoint_early, receiver_x, receiver_yz, residual_trace[:, :, 1], first_x)
    gradient_terms = jnp.sum(
        2.0 * courant[None] * (adjoint_early * accel_one + adjoint_mid * accel_two), axis=0
    )
    summed_all = lax.psum(gradient_terms, "shot")
    part_rows = summed_all.shape[1] // lax.axis_size("shot")
    return lax.dynamic_slice_in_dim(summed_all, lax.axis_index("shot") * part_rows, part_rows, 1)


def solution(mesh):
    placed = (
        P("space", None, None),
        P("shot", "space", None, None),
        P("shot", "space", None, None),
        P("shot", "space", None, None),
        P("shot", "space", None, None),
        P("shot"),
        P("shot"),
        P("shot", None),
        P("shot", None),
        P("shot", None),
        P("shot", None, None),
    )
    return jax.shard_map(
        on_device, mesh=mesh, in_specs=placed, out_specs=P("space", "shot", None), check_vma=False
    )
```

profile of v0, /device:TPU:0, one launch (start us, length us, event | category | flops | bytes accessed | tf_op | source)
XLA Modules:
  0.0 142.0 jit_solution(15168053447562948703)
XLA Ops:
  6.5 0.0 all-reduce.6.cloned.1.call-start
  6.5 1.1 fusion.116
  7.7 2.4 %collective-permute-start.5 = (f32[1,4,64,256]{3,2,1,0:T(8,128)S(1)}, f32[1,4,64,256]{3,2,1,0:T(8,128)S(1)}, u32[]{:S(2)}, u32[]{:S(2)}) collective-permute-start(f32[1,4,64,256]{3,2,1,0:T(8,128)S(1)} %get-tuple-element.39), channel_id=1, source_target_pairs={{0,1},{1,2},{2,3},{3,4},{4,5},{5,6},{6,7},{8,9},{9,10},{10,11},{11... | collective-permute-start | bytes 786440 | tf_op jit(solution)/shard_map/ppermute | solution.py:15
  10.1 1.3 collective-permute-start.4
  11.4 0.7 fusion.111
  12.1 0.1 add_bitcast_fusion
  13.5 1.5 %and_reduce_fusion = pred[]{:T(512)} fusion(s32[3]{0:T(128)} %constant.82.clone.1, s32[1]{0:T(128)} %select_n.34, s32[1]{0:T(128)} %select_n.33, s32[1]{0:T(128)} %constant.79.clone.1), kind=kLoop, calls=%fused_computation.216 | loop fusion | flops 17 | bytes 25 | tf_op jit(solution)/shard_map/reduce.2
  14.9 1.4 fusion.118
  16.3 0.0 collective-permute-done.5
  16.3 0.0 copy-done
  16.4 0.1 constant_dynamic-update-slice_fusion.1
  16.5 0.0 collective-permute-done.4
  16.5 0.6 select_maximum_fusion.2
  17.1 0.0 copy-start.1
  17.1 0.0 copy-start.2
  17.1 0.0 copy-start.6
  17.1 2.1 %fusion.98 = f32[1,8,64,256]{3,2,1,0:T(8,128)S(1)} fusion(f32[1,16,72,264]{3,2,1,0:T(8,128)S(1)} %select_maximum_fusion.2, f32[1,12,64,256]{3,2,1,0:T(8,128)S(1)} %get-tuple-element.38, f32[1,12,64,256]{3,2,1,0:T(8,128)S(1)} %constant_dynamic-update-slice_fusion, f32[1,8,64,256]{3,2,1,0:T(8,128)S(1)} %copy-done), kind=kLoop, calls=%fused_computation.158 | loop fusion | flops 3801088 | bytes 13631488 | tf_op jit(solution)/shard_map/add | solution.py:39
  19.2 0.1 reshape.132
  19.3 1.3 fusion.119
  22.5 0.1 scatter-add.26
  22.6 0.0 copy-done.1
  22.6 0.0 copy-done.2
  22.7 0.0 copy-done.6
  22.7 0.0 copy-start.8
  22.7 0.3 bitcast_multiply_fusion.3
  23.1 1.3 collective-permute-start
  24.4 6.5 %collective-permute-start.1 = (f32[1,4,64,256]{3,2,1,0:T(8,128)S(1)}, f32[1,4,64,256]{3,2,1,0:T(8,128)S(1)}, u32[]{:S(2)}, u32[]{:S(2)}) collective-permute-start(f32[1,4,64,256]{3,2,1,0:T(8,128)S(1)} %get-tuple-element.32), channel_id=1, source_target_pairs={{0,1},{1,2},{2,3},{3,4},{4,5},{5,6},{6,7},{8,9},{9,10},{10,11},{11... | collective-permute-start | bytes 786440 | tf_op jit(solution)/shard_map/ppermute | solution.py:15
  30.9 0.0 copy-start.7
  30.9 0.9 fusion.115
  31.7 1.3 collective-permute-start.6
  33.0 5.0 %collective-permute-start.7 = (f32[1,4,64,256]{3,2,1,0:T(8,128)}, f32[1,4,64,256]{3,2,1,0:T(8,128)}, u32[]{:S(2)}, u32[]{:S(2)}) collective-permute-start(f32[1,4,64,256]{3,2,1,0:T(8,128)} %get-tuple-element.36), channel_id=1, source_target_pairs={{0,1},{1,2},{2,3},{3,4},{4,5},{5,6},{6,7},{8,9},{9,10},{10,11},{11... | collective-permute-start | bytes 786440 | tf_op jit(solution)/shard_map/ppermute | solution.py:15
  38.0 0.0 collective-permute-done
  38.0 0.0 collective-permute-done.1
  38.0 0.6 select_maximum_fusion.6
  38.5 0.0 copy-done.7
  38.6 2.1 %fusion.71 = f32[1,8,64,256]{3,2,1,0:T(8,128)S(1)} fusion(f32[1,8,64,256]{3,2,1,0:T(8,128)S(1)} %get-tuple-element.33, f32[1,4,64,256]{3,2,1,0:T(8,128)S(1)} %collective-permute-done.1, f32[1,4,64,256]{3,2,1,0:T(8,128)S(1)} %collective-permute-done, f32[1,16,72,264]{3,2,1,0:T(8,128)S(1)} %select_maximum_fusion.6, f32[1,8,64,256]{3,2,1,0:T(8,128)S(1)} %copy-done.7, ...), kind=kLoop, calls=%fused_computation.121 | loop fusion | flops 5242880 | bytes 11010048
  40.7 0.3 copy.20
  41.0 12.3 %scatter_fusion = f32[8,16384]{1,0:T(8,128)S(1)} fusion(f32[8,16384]{1,0:T(8,128)S(1)} %bitcast.62, s32[256]{0:T(256)S(1)} %bitcast.60, f32[256]{0:T(256)S(1)} %bitcast.73), kind=kCustom, calls=%fused_computation | custom fusion | flops 256 | bytes 5120 | tf_op jit(solution)/shard_map/scatter-add | solution.py:60
  53.3 0.8 broadcast_multiply_fusion
  54.2 0.2 fusion.109
  54.4 0.9 fusion.113
  55.2 1.3 collective-permute-start.2
  56.5 4.3 %collective-permute-start.3 = (f32[1,4,64,256]{3,2,1,0:T(8,128)}, f32[1,4,64,256]{3,2,1,0:T(8,128)}, u32[]{:S(2)}, u32[]{:S(2)}) collective-permute-start(f32[1,4,64,256]{3,2,1,0:T(8,128)} %get-tuple-element.30), channel_id=1, source_target_pairs={{0,1},{1,2},{2,3},{3,4},{4,5},{5,6},{6,7},{8,9},{9,10},{10,11},{11... | collective-permute-start | bytes 786440 | tf_op jit(solution)/shard_map/ppermute | solution.py:15
  60.9 0.0 collective-permute-done.6
  60.9 0.0 collective-permute-done.7
  60.9 1.5 %select_maximum_fusion = f32[1,16,72,264]{3,2,1,0:T(8,128)S(1)} fusion(f32[1,4,64,256]{3,2,1,0:T(8,128)S(1)} %collective-permute-done.6, f32[1,8,64,256]{3,2,1,0:T(8,128)S(1)} %get-tuple-element.34, f32[1,4,64,256]{3,2,1,0:T(8,128)} %collective-permute-done.7), kind=kLoop, calls=%fused_computation.6 | loop fusion | flops 4561920 | bytes 2265088 | tf_op jit(solution)/shard_map/concatenate | solution.py:19
  62.4 4.1 %fusion.11 = f32[1,8,64,256]{3,2,1,0:T(8,128)} fusion(f32[1,8,64,256]{3,2,1,0:T(8,128)S(1)} %get-tuple-element.34, f32[1,4,64,256]{3,2,1,0:T(8,128)} %collective-permute-done.7, f32[1,4,64,256]{3,2,1,0:T(8,128)S(1)} %collective-permute-done.6, f32[1,16,72,264]{3,2,1,0:T(8,128)S(1)} %select_maximum_fusion), kind=kLoop, calls=%fused_computation.61 | loop fusion | flops 4849664 | bytes 9961472 | tf_op jit(solution)/shard_map/add | solution.py:39
  66.5 1.1 reshape.138
  67.6 1.3 fusion.120
  70.8 0.3 scatter-add.27
  71.2 0.0 copy-start.3
  71.2 0.0 copy-start.5
  71.2 0.0 collective-permute-done.2
  71.2 0.0 collective-permute-done.3
  71.2 1.8 %select_maximum_fusion.4 = f32[1,16,72,264]{3,2,1,0:T(8,128)S(1)} fusion(f32[1,4,64,256]{3,2,1,0:T(8,128)} %collective-permute-done.2, f32[1,8,64,256]{3,2,1,0:T(8,128)S(1)} %fusion.109, f32[1,4,64,256]{3,2,1,0:T(8,128)} %collective-permute-done.3), kind=kLoop, calls=%fused_computation.10 | loop fusion | flops 4561920 | bytes 2265088 | tf_op jit(solution)/shard_map/concatenate | solution.py:19
  73.0 0.0 copy-done.3
  73.0 0.0 copy-done.5
  73.0 3.5 %fusion.41 = f32[1,8,64,256]{3,2,1,0:T(8,128)S(1)} fusion(f32[1,8,64,256]{3,2,1,0:T(8,128)S(1)} %fusion.109, f32[1,4,64,256]{3,2,1,0:T(8,128)} %collective-permute-done.3, f32[1,4,64,256]{3,2,1,0:T(8,128)} %collective-permute-done.2, f32[1,16,72,264]{3,2,1,0:T(8,128)S(1)} %select_maximum_fusion.4, f32[1,8,64,256]{3,2,1,0:T(8,128)S(1)} %copy-done.2, ...), kind=kLoop, calls=%fused_computation.91 | loop fusion | flops 5373952 | bytes 12058624
  76.6 0.3 copy.21
  76.9 12.3 %scatter_fusion.1 = f32[8,16384]{1,0:T(8,128)S(1)} fusion(f32[8,16384]{1,0:T(8,128)S(1)} %bitcast.66, s32[256]{0:T(256)S(1)} %bitcast.61, f32[256]{0:T(256)S(1)} %bitcast.72), kind=kCustom, calls=%fused_computation.1 | custom fusion | flops 256 | bytes 5120 | tf_op jit(solution)/shard_map/scatter-add | solution.py:60
  89.2 1.5 %fusion.92 = f32[8,64,256]{2,1,0:T(8,128)} fusion(f32[1,8,64,256]{3,1,2,0:T(8,128)S(1)} %bitcast.70, f32[8,64,256]{2,0,1:T(8,128)S(1)} %bitcast.67, f32[8,64,256]{2,1,0:T(8,128)S(1)} %copy-done.1, f32[1,8,64,256]{3,1,2,0:T(8,128)S(1)} %bitcast.69, f32[8,64,256]{2,0,1:T(8,128)S(1)} %bitcast.65), kind=kLoop, calls=%fused_computation.143 | loop fusion | flops 655360 | bytes 3145728 | tf_op jit(solution)/shard_map/mul | solution.py:96
  90.7 0.0 all-reduce.6.cloned.1.call-update
  90.7 42.8 %all-reduce.6.cloned.1.call-done = f32[8,64,256]{2,1,0:T(8,128)} async-done(((f32[8,64,256]{2,1,0:T(8,128)}), f32[8,64,256]{2,1,0:T(8,128)}) %all-reduce.6.cloned.1.call-update) | async-done | bytes 524304 | tf_op jit(solution)/shard_map/psum | solution.py:98
  133.5 1.6 %constant_dynamic-slice_fusion = f32[8,16,256]{2,1,0:T(8,128)} fusion(f32[8,64,256]{2,1,0:T(8,128)} %all-reduce.6.cloned.1.call-done, s32[]{:T(128)S(6)} %select_n.35), kind=kLoop, calls=%fused_computation.222 | loop fusion | bytes 262148 | tf_op jit(solution)/shard_map/dynamic_slice | solution.py:100
  (10 shorter events, 0.1 us)
Async XLA Ops:
  6.5 9.8 %copy-start = (f32[1,8,64,256]{3,2,1,0:T(8,128)S(1)}, f32[1,8,64,256]{3,2,1,0:T(8,128)}, u32[]{:S(2)}) copy-start(f32[1,8,64,256]{3,2,1,0:T(8,128)} %param.17) | copy-start | bytes 1572868
  6.5 127.0 %all-reduce.6.cloned.1.call-start = ((), (), s32[]{:S(2)}) async-start(), calls=%async_computation | async-start | bytes 1048576 | tf_op jit(solution)/shard_map/psum | solution.py:98
  7.7 8.6 %collective-permute-start.5 = (f32[1,4,64,256]{3,2,1,0:T(8,128)S(1)}, f32[1,4,64,256]{3,2,1,0:T(8,128)S(1)}, u32[]{:S(2)}, u32[]{:S(2)}) collective-permute-start(f32[1,4,64,256]{3,2,1,0:T(8,128)S(1)} %get-tuple-element.39), channel_id=1, source_target_pairs={{0,1},{1,2},{2,3},{3,4},{4,5},{5,6},{6,7},{8,9},{9,10},{10,11},{11... | collective-permute-start | bytes 786440 | tf_op jit(solution)/shard_map/ppermute | solution.py:15
  10.1 6.4 %collective-permute-start.4 = (f32[1,4,64,256]{3,2,1,0:T(8,128)S(1)}, f32[1,4,64,256]{3,2,1,0:T(8,128)S(1)}, u32[]{:S(2)}, u32[]{:S(2)}) collective-permute-start(f32[1,4,64,256]{3,2,1,0:T(8,128)S(1)} %get-tuple-element.40), channel_id=1, source_target_pairs={{1,0},{2,1},{3,2},{4,3},{5,4},{6,5},{7,6},{9,8},{10,9},{11,10},{12... | collective-permute-start | bytes 786440 | tf_op jit(solution)/shard_map/ppermute | solution.py:18
  17.1 5.6 %copy-start.1 = (f32[8,64,256]{2,1,0:T(8,128)S(1)}, f32[8,64,256]{2,1,0:T(8,128)}, u32[]{:S(2)}) copy-start(f32[8,64,256]{2,1,0:T(8,128)} %param.15) | copy-start | bytes 1572868
  17.1 5.6 %copy-start.2 = (f32[1,8,64,256]{3,2,1,0:T(8,128)S(1)}, f32[1,8,64,256]{3,2,1,0:T(8,128)}, u32[]{:S(2)}) copy-start(f32[1,8,64,256]{3,2,1,0:T(8,128)} %param.19) | copy-start | bytes 1572868
  17.1 5.6 %copy-start.6 = (f32[1,8,64,256]{3,2,1,0:T(8,128)S(1)}, f32[1,8,64,256]{3,2,1,0:T(8,128)}, u32[]{:S(2)}) copy-start(f32[1,8,64,256]{3,2,1,0:T(8,128)} %param.16) | copy-start | bytes 1572868
  22.7 8.2 %copy-start.8 = (f32[1,256,2]{1,2,0:T(2,128)S(1)}, f32[1,256,2]{1,2,0:T(2,128)}, u32[]{:S(2)}) copy-start(f32[1,256,2]{1,2,0:T(2,128)} %param.25) | copy-start | bytes 6148
  23.1 14.9 %collective-permute-start = (f32[1,4,64,256]{3,2,1,0:T(8,128)S(1)}, f32[1,4,64,256]{3,2,1,0:T(8,128)S(1)}, u32[]{:S(2)}, u32[]{:S(2)}) collective-permute-start(f32[1,4,64,256]{3,2,1,0:T(8,128)S(1)} %get-tuple-element.31), channel_id=1, source_target_pairs={{1,0},{2,1},{3,2},{4,3},{5,4},{6,5},{7,6},{9,8},{10,9},{11,10},{12... | collective-permute-start | bytes 786440 | tf_op jit(solution)/shard_map/ppermute | solution.py:18
  24.4 13.6 %collective-permute-start.1 = (f32[1,4,64,256]{3,2,1,0:T(8,128)S(1)}, f32[1,4,64,256]{3,2,1,0:T(8,128)S(1)}, u32[]{:S(2)}, u32[]{:S(2)}) collective-permute-start(f32[1,4,64,256]{3,2,1,0:T(8,128)S(1)} %get-tuple-element.32), channel_id=1, source_target_pairs={{0,1},{1,2},{2,3},{3,4},{4,5},{5,6},{6,7},{8,9},{9,10},{10,11},{11... | collective-permute-start | bytes 786440 | tf_op jit(solution)/shard_map/ppermute | solution.py:15
  30.9 7.7 %copy-start.7 = (f32[1,8,64,256]{3,2,1,0:T(8,128)S(1)}, f32[1,8,64,256]{3,2,1,0:T(8,128)}, u32[]{:S(2)}) copy-start(f32[1,8,64,256]{3,2,1,0:T(8,128)} %param.18) | copy-start | bytes 1572868
  31.7 29.1 %collective-permute-start.6 = (f32[1,4,64,256]{3,2,1,0:T(8,128)}, f32[1,4,64,256]{3,2,1,0:T(8,128)S(1)}, u32[]{:S(2)}, u32[]{:S(2)}) collective-permute-start(f32[1,4,64,256]{3,2,1,0:T(8,128)} %get-tuple-element.35), channel_id=1, source_target_pairs={{1,0},{2,1},{3,2},{4,3},{5,4},{6,5},{7,6},{9,8},{10,9},{11,10},{12... | collective-permute-start | bytes 786440 | tf_op jit(solution)/shard_map/ppermute | solution.py:18
  33.0 27.8 %collective-permute-start.7 = (f32[1,4,64,256]{3,2,1,0:T(8,128)}, f32[1,4,64,256]{3,2,1,0:T(8,128)}, u32[]{:S(2)}, u32[]{:S(2)}) collective-permute-start(f32[1,4,64,256]{3,2,1,0:T(8,128)} %get-tuple-element.36), channel_id=1, source_target_pairs={{0,1},{1,2},{2,3},{3,4},{4,5},{5,6},{6,7},{8,9},{9,10},{10,11},{11... | collective-permute-start | bytes 786440 | tf_op jit(solution)/shard_map/ppermute | solution.py:15
  55.2 16.0 %collective-permute-start.2 = (f32[1,4,64,256]{3,2,1,0:T(8,128)}, f32[1,4,64,256]{3,2,1,0:T(8,128)}, u32[]{:S(2)}, u32[]{:S(2)}) collective-permute-start(f32[1,4,64,256]{3,2,1,0:T(8,128)} %get-tuple-element.29), channel_id=1, source_target_pairs={{1,0},{2,1},{3,2},{4,3},{5,4},{6,5},{7,6},{9,8},{10,9},{11,10},{12... | collective-permute-start | bytes 786440 | tf_op jit(solution)/shard_map/ppermute | solution.py:18
  56.5 14.7 %collective-permute-start.3 = (f32[1,4,64,256]{3,2,1,0:T(8,128)}, f32[1,4,64,256]{3,2,1,0:T(8,128)}, u32[]{:S(2)}, u32[]{:S(2)}) collective-permute-start(f32[1,4,64,256]{3,2,1,0:T(8,128)} %get-tuple-element.30), channel_id=1, source_target_pairs={{0,1},{1,2},{2,3},{3,4},{4,5},{5,6},{6,7},{8,9},{9,10},{10,11},{11... | collective-permute-start | bytes 786440 | tf_op jit(solution)/shard_map/ppermute | solution.py:15
  71.2 1.8 %copy-start.3 = (f32[1,8,16384]{2,1,0:T(8,128)}, f32[1,8,16384]{2,1,0:T(8,128)S(1)}, u32[]{:S(2)}) copy-start(f32[1,8,16384]{2,1,0:T(8,128)S(1)} %scatter-add.27) | copy-start | bytes 1572868
  71.2 1.8 %copy-start.5 = (f32[8,16384]{1,0:T(8,128)S(1)}, f32[8,16384]{1,0:T(8,128)}, u32[]{:S(2)}) copy-start(f32[8,16384]{1,0:T(8,128)} %broadcast_multiply_fusion) | copy-start | bytes 1572868
  76.6 12.7 %copy-start.4 = (f32[1,8,16384]{2,1,0:T(8,128)S(1)}, f32[1,8,16384]{2,1,0:T(8,128)}, u32[]{:S(2)}) copy-start(f32[1,8,16384]{2,1,0:T(8,128)} %copy-done.3) | copy-start | bytes 1572868
Sparse Core Ops, SparseCore 0:
  90.8 42.6 all-reduce.5
where the time goes:
time: 143 us; the launch traced here: 142 us
  other arithmetic  48.6 us (34%)
  waiting for transfers between devices  42.9 us (30%)
  starting transfers between devices  23.3 us (16%)
  between operations  18.9 us (13%)
  local copies, waits for them, and re-layouts  8.36 us (6%)
    psum x1, waiting for transfers between devices, on_device(): summed_all = lax.psum(gradient_terms, 'shot')  42.8 us
    scatter-add x2, other arithmetic, inject(): flattened.at[shot_rows, local_x, cells_yz].add(amounts, mode='drop')  24.6 us
    ppermute x4, starting transfers between devices, with_halo(): lax.ppermute(lax.slice_in_dim(block, block.shape[dim] - width, None, axis...  18.1 us
    add x2, other arithmetic, laplace_x(): summed + weight * (window(offset, 0, 0) + window(-offset, 0, 0) + window(...  6.23 us
    unnamed x2, other arithmetic  5.64 us
    ppermute x4, starting transfers between devices, with_halo(): lax.ppermute(lax.slice_in_dim(block, 0, width, axis=dim), axis, backward)  5.14 us
    concatenate x4, other arithmetic, with_halo(): block = jnp.concatenate([low, block, high], axis=dim)  4.41 us
  transfers between devices with their start and end apart: 9, of which 1 were waited for; matrix products, arithmetic and copies ran while one was open for 21% of the time, Pallas kernels for 0%

commit v1 on v0

v1 whole, which is shorter than its diff:
```python
import functools
import jax
import jax.numpy as jnp
from jax import lax
from jax.experimental import pallas as pl
from jax.experimental.pallas import tpu as pltpu
from jax.sharding import PartitionSpec as P

MIDDLE = 3.0 * (-205.0 / 72.0)
SIDE = (8.0 / 5.0, -1.0 / 5.0, 8.0 / 315.0, -1.0 / 560.0)
REACH = 4
F32 = jnp.float32
BF16 = jnp.bfloat16
VMEM_LIMIT = 48 * 1024 * 1024


def placed(layer, odd, slab):
    return layer + odd * (slab - 1 - 2 * layer)


def grids(size_y, size_z):
    rows = lax.broadcasted_iota(jnp.int32, (size_y, size_z), 0)
    columns = lax.broadcasted_iota(jnp.int32, (size_y, size_z), 1)
    return rows, columns


def own_laplace(layers, at, slab, rows, columns):
    centre = layers[at]
    size_y, size_z = centre.shape
    total = MIDDLE * centre
    for offset in range(1, REACH + 1):
        near = jnp.where(rows >= offset, pltpu.roll(centre, offset, 0), 0.0)
        near += jnp.where(rows < size_y - offset, pltpu.roll(centre, size_y - offset, 0), 0.0)
        near += jnp.where(columns >= offset, pltpu.roll(centre, offset, 1), 0.0)
        near += jnp.where(columns < size_z - offset, pltpu.roll(centre, size_z - offset, 1), 0.0)
        if at - offset >= 0:
            near += layers[at - offset]
        if at + offset < slab:
            near += layers[at + offset]
        total += SIDE[offset - 1] * near
    return total


def across(depth, layers):
    total = None
    for beyond in range(REACH - depth):
        term = SIDE[depth + beyond] * layers(beyond)
        total = term if total is None else total + term
    return total


def early_kernel(slab, courant, now, adjoint, packet, c_part, n_part, a_part, sems):
    odd = lax.rem(lax.axis_index("space"), 2)
    start = odd * (slab - REACH)
    copies = [
        pltpu.make_async_copy(source.at[pl.ds(start, REACH)], target, sems.at[number])
        for number, (source, target) in enumerate(
            ((courant, c_part), (now, n_part), (adjoint, a_part))
        )
    ]
    for copy in copies:
        copy.start()
    for copy in copies:
        copy.wait()
    for layer in range(REACH):
        at = placed(layer, odd, REACH)
        packet[layer] = n_part[at]
        speed = c_part[at]
        packet[REACH + layer] = speed * speed * a_part[at]


def local_kernel(
    slab,
    source_x,
    source_yz,
    wavelet,
    courant,
    old,
    now,
    late,
    adjoint,
    receiver_x,
    receiver_yz,
    residual,
    accel_one,
    field_mid,
    adjoint_mid,
    early_rest,
    packet_in,
    packet_out,
    scaled,
    marks,
    added,
):
    space = lax.axis_index("space")
    odd = lax.rem(space, 2)
    first_x = space * slab
    size_y, size_z = courant.shape[1:]
    z_bits = size_z.bit_length() - 1
    rows, columns = grids(size_y, size_z)

    local_x = receiver_x[...] - first_x
    cells = receiver_yz[...]
    inside = (local_x >= 0) & (local_x < slab)
    wanted = jnp.where(inside, local_x * size_y + jnp.right_shift(cells, z_bits), -1)
    count = wanted.shape[1]
    line = lax.broadcasted_iota(jnp.int32, (slab * size_y, count), 0)
    marks[...] = jnp.where(line == wanted, 1.0, 0.0).astype(BF16)
    depth = lax.broadcasted_iota(jnp.int32, (size_z, count), 0)
    hit = depth == jnp.bitwise_and(cells, size_z - 1)
    for step in range(2):
        rest = residual[pl.ds(step, 1), :]
        total = None
        for _ in range(3):
            part = rest.astype(BF16).astype(F32)
            rest = rest - part
            spread = jnp.where(hit, part, 0.0).astype(BF16)
            term = lax.dot_general(
                marks[...], spread, (((1,), (1,)), ((), ())), preferred_element_type=F32
            )
            total = term if total is None else total + term
        added[step] = total

    for at in range(slab):
        scaled[at] = courant[at] * courant[at] * adjoint[at]
    cell = rows * size_z + columns
    source_layer = source_x[0] - first_x
    for at in range(slab):
        to = placed(at, odd, slab)
        speed_sq = courant[at] * courant[at]
        spot = jnp.where(source_layer == at, source_yz[0], -1)
        laplace = own_laplace(now, at, slab, rows, columns)
        laplace += jnp.where(cell == spot, wavelet[0, 0], 0.0)
        accel_one[to] = laplace
        field_mid[to] = 2.0 * now[at] - old[at] + speed_sq * laplace
        mine = pl.ds(at * size_y, size_y)
        adjoint_mid[to] = (
            2.0 * adjoint[at]
            - late[at]
            + own_laplace(scaled, at, slab, rows, columns)
            + added[0, mine, :]
        )
        early_rest[to] = added[1, mine, :] - adjoint[at]
    for layer in range(REACH):
        inner = slab - 1 - layer
        at = placed(inner, odd, slab)
        speed = courant[at]
        packet_in[layer] = now[at]
        packet_in[REACH + layer] = scaled[at]
        packet_in[2 * REACH + layer] = speed
        packet_in[3 * REACH + layer] = field_mid[inner]
        packet_in[4 * REACH + layer] = speed * speed * adjoint_mid[inner]
        speed = courant[placed(layer, odd, slab)]
        packet_out[layer] = speed
        packet_out[REACH + layer] = field_mid[layer]
        packet_out[2 * REACH + layer] = speed * speed * adjoint_mid[layer]


def finished_halo(speeds, partial, own):
    return [
        partial(layer) + speeds(layer) * speeds(layer) * across(layer, own)
        for layer in range(REACH)
    ]


def scatter_rows(gradient, outputs, shots):
    rows = gradient.shape[1] // shots
    me = lax.axis_index("shot")
    for shift in range(shots):
        first = pl.multiple_of(lax.rem(me + shift, shots) * rows, rows)
        outputs[shift][...] = gradient[:, pl.ds(first, rows), :]


def inner_kernel(
    slab,
    shots,
    source_x,
    source_yz,
    wavelet,
    courant,
    accel_one,
    field_mid,
    adjoint_mid,
    early_rest,
    own_in,
    halo_in,
    halo_early,
    *rest,
):
    outer, outputs = rest[0], rest[1 : 1 + shots]
    accel, adjoint, mid, scaled, next_mid, next_scaled, gradient = rest[1 + shots :]
    space = lax.axis_index("space")
    odd = lax.rem(space, 2)
    size_y, size_z = courant.shape[1:]
    rows, columns = grids(size_y, size_z)

    for layer in range(REACH):
        speed = halo_in[2 * REACH + layer]
        speed_sq = speed * speed
        next_mid[layer] = halo_in[3 * REACH + layer] + speed_sq * across(
            layer, lambda beyond: own_in[beyond]
        )
        next_scaled[layer] = halo_in[4 * REACH + layer] + speed_sq * across(
            layer, lambda beyond: own_in[REACH + beyond]
        )

    def beyond_faces(at, out_layers, in_layers):
        total = None
        if at < REACH:
            total = across(at, out_layers)
        if slab - 1 - at < REACH:
            other = across(slab - 1 - at, in_layers)
            total = other if total is None else total + other
        return total

    for at in range(slab):
        speed = courant[placed(at, odd, slab)]
        speed_sq = speed * speed
        extra = beyond_faces(
            at, lambda beyond: halo_early[beyond], lambda beyond: halo_in[beyond]
        )
        accel[at] = accel_one[at] if extra is None else accel_one[at] + extra
        mid[at] = field_mid[at] if extra is None else field_mid[at] + speed_sq * extra
        extra = beyond_faces(
            at, lambda beyond: halo_early[REACH + beyond], lambda beyond: halo_in[REACH + beyond]
        )
        adjoint[at] = adjoint_mid[at] if extra is None else adjoint_mid[at] + extra
        scaled[at] = speed_sq * adjoint[at]

    cell = rows * size_z + columns
    source_layer = placed(source_x[0] - space * slab, odd, slab)
    for at in range(slab):
        spot = jnp.where(source_layer == at, source_yz[0], -1)
        accel_two = own_laplace(mid, at, slab, rows, columns)
        accel_two += jnp.where(cell == spot, wavelet[0, 1], 0.0)
        early = 2.0 * adjoint[at] + early_rest[at]
        early += own_laplace(scaled, at, slab, rows, columns)
        depth = slab - 1 - at
        if depth < REACH:
            accel_two += across(depth, lambda beyond: next_mid[beyond])
            early += across(depth, lambda beyond: next_scaled[beyond])
        if at < REACH:
            outer[at] = accel[at]
            outer[REACH + at] = adjoint[at]
            outer[2 * REACH + at] = accel_two
            outer[3 * REACH + at] = early
        else:
            speed = courant[placed(at, odd, slab)]
            gradient[at - REACH] = (
                2.0 * speed * (early * accel[at] + adjoint[at] * accel_two)
            )
    scatter_rows(gradient, outputs, shots)


def outer_kernel(slab, shots, courant, outer, own_early, halo_late, *rest):
    outputs, (next_mid, next_scaled, gradient) = rest[:shots], rest[shots:]
    odd = lax.rem(lax.axis_index("space"), 2)
    for layer in range(REACH):
        speed = halo_late[layer]
        speed_sq = speed * speed
        next_mid[layer] = halo_late[REACH + layer] + speed_sq * across(
            layer, lambda beyond: own_early[beyond]
        )
        next_scaled[layer] = halo_late[2 * REACH + layer] + speed_sq * across(
            layer, lambda beyond: own_early[REACH + beyond]
        )
    for at in range(REACH):
        accel_two = outer[2 * REACH + at] + across(at, lambda beyond: next_mid[beyond])
        early = outer[3 * REACH + at] + across(at, lambda beyond: next_scaled[beyond])
        speed = courant[placed(at, odd, slab)]
        gradient[at] = 2.0 * speed * (early * outer[at] + outer[REACH + at] * accel_two)
    scatter_rows(gradient, outputs, shots)


def sum_kernel(slab, shots, *refs):
    outers, inners, out = refs[:shots], refs[shots : 2 * shots], refs[2 * shots]
    odd = lax.rem(lax.axis_index("space"), 2)
    for at in range(slab):
        parts = [ref[at] for ref in outers] if at < REACH else [ref[at - REACH] for ref in inners]
        out[placed(at, odd, slab)] = functools.reduce(lambda a, b: a + b, parts)


def call(kernel, shapes, in_spaces, scratch, flops, moved):
    many = isinstance(shapes, list)
    return pl.pallas_call(
        kernel,
        out_shape=[jax.ShapeDtypeStruct(s, F32) for s in shapes]
        if many
        else jax.ShapeDtypeStruct(shapes, F32),
        in_specs=[pl.BlockSpec(memory_space=space) for space in in_spaces],
        out_specs=[pl.BlockSpec(memory_space=pltpu.VMEM) for _ in shapes]
        if many
        else pl.BlockSpec(memory_space=pltpu.VMEM),
        scratch_shapes=scratch,
        compiler_params=pltpu.CompilerParams(vmem_limit_bytes=VMEM_LIMIT),
        cost_estimate=pl.CostEstimate(flops=flops, bytes_accessed=moved, transcendentals=0),
    )


def on_device(
    courant,
    field_old,
    field_now,
    adjoint_late,
    adjoint_now,
    source_x,
    source_yz,
    wavelet,
    receiver_x,
    receiver_yz,
    residual_trace,
):
    slab, size_y, size_z = courant.shape
    shots = lax.axis_size("shot")
    devices = lax.axis_size("space")
    plane = (size_y, size_z)
    layer_bytes = 4 * size_y * size_z
    inner_layers = slab - REACH
    part_rows = size_y // shots
    V, S, A = pltpu.VMEM, pltpu.SMEM, pl.ANY
    out_pairs = [(i, i + 1) for i in range(1, devices - 1, 2)]
    out_pairs += [(b, a) for a, b in out_pairs]
    in_pairs = [(i, i ^ 1) for i in range(devices)]
    old, now, late, adjoint = (
        field[0] for field in (field_old, field_now, adjoint_late, adjoint_now)
    )
    residual = residual_trace[0].T

    own_early = call(
        functools.partial(early_kernel, slab),
        (2 * REACH,) + plane,
        [A, A, A],
        [pltpu.VMEM((REACH,) + plane, F32)] * 3 + [pltpu.SemaphoreType.DMA((3,))],
        3 * REACH * size_y * size_z,
        20 * layer_bytes,
    )(courant, now, adjoint)
    halo_early = lax.ppermute(own_early, "space", out_pairs)

    whole = (slab,) + plane
    accel_one, field_mid, adjoint_mid, early_rest, own_in, own_late = call(
        functools.partial(local_kernel, slab),
        [whole] * 4 + [(5 * REACH,) + plane, (3 * REACH,) + plane],
        [S, S, S, V, V, V, V, V, V, V, V],
        [
            pltpu.VMEM(whole, F32),
            pltpu.VMEM((slab * size_y, receiver_x.shape[1]), BF16),
            pltpu.VMEM((2, slab * size_y, size_z), F32),
        ],
        100 * slab * size_y * size_z,
        13 * slab * layer_bytes,
    )(
        source_x,
        source_yz,
        wavelet,
        courant,
        old,
        now,
        late,
        adjoint,
        receiver_x,
        receiver_yz,
        residual,
    )
    halo_in = lax.ppermute(own_in, "space", in_pairs)
    halo_late = lax.ppermute(own_late, "space", out_pairs)

    outer, *inner_parts = call(
        functools.partial(inner_kernel, slab, shots),
        [(4 * REACH,) + plane] + [(inner_layers, part_rows, size_z)] * shots,
        [S, S, S, V, V, V, V, V, V, V, V],
        [
            pltpu.VMEM(whole, F32),
            pltpu.VMEM(whole, F32),
            pltpu.VMEM(whole, F32),
            pltpu.VMEM(whole, F32),
            pltpu.VMEM((REACH,) + plane, F32),
            pltpu.VMEM((REACH,) + plane, F32),
            pltpu.VMEM((inner_layers,) + plane, F32),
        ],
        100 * slab * size_y * size_z,
        13 * slab * layer_bytes,
    )(
        source_x,
        source_yz,
        wavelet,
        courant,
        accel_one,
        field_mid,
        adjoint_mid,
        early_rest,
        own_in,
        halo_in,
        halo_early,
    )
    shifts = [[(i, (i + k) % shots) for i in range(shots)] for k in range(shots)]
    inner_parts = inner_parts[:1] + [
        lax.ppermute(inner_parts[k], "shot", shifts[k]) for k in range(1, shots)
    ]
    outer_parts = call(
        functools.partial(outer_kernel, slab, shots),
        [(REACH, part_rows, size_z)] * shots,
        [V, V, V, V],
        [
            pltpu.VMEM((REACH,) + plane, F32),
            pltpu.VMEM((REACH,) + plane, F32),
            pltpu.VMEM((REACH,) + plane, F32),
        ],
        50 * REACH * size_y * size_z,
        48 * layer_bytes,
    )(courant, outer, own_early, halo_late)
    outer_parts = list(outer_parts[:1]) + [
        lax.ppermute(outer_parts[k], "shot", shifts[k]) for k in range(1, shots)
    ]
    return call(
        functools.partial(sum_kernel, slab, shots),
        (slab, part_rows, size_z),
        [V] * (2 * shots),
        [],
        slab * size_y * size_z,
        2 * slab * layer_bytes,
    )(*outer_parts, *inner_parts)


def solution(mesh):
    field = P("shot", "space", None, None)
    specs = (
        P("space", None, None),
        field,
        field,
        field,
        field,
        P("shot"),
        P("shot"),
        P("shot", None),
        P("shot", None),
        P("shot", None),
        P("shot", None, None),
    )
    return jax.shard_map(
        on_device, mesh=mesh, in_specs=specs, out_specs=P("space", "shot", None), check_vma=False
    )
```

time: 143 us -> 68.5 us (0.48)
  the two profiles are of different devices: /device:TPU:0 before, /device:TPU:3 now
where the time goes in v1:
time: 68.5 us; the launch traced here: 68 us
  waiting for transfers between devices  32.5 us (47%)
  starting transfers between devices  14.6 us (21%)
  Pallas kernels  10.6 us (15%)
  local copies, waits for them, and re-layouts  8.97 us (13%)
  between operations  1.38 us (2%)
    ppermute x1, waiting for transfers between devices, on_device(): halo_early = lax.ppermute(own_early, 'space', out_pairs)  26.7 us
    unnamed x26, local copies, waits for them, and re-layouts  8.97 us
    ppermute x3, waiting for transfers between devices, on_device(): lax.ppermute(inner_parts[k], 'shot', shifts[k])  5.19 us
    pallas_call x1, Pallas kernels, on_device(): call(functools.partial(local_kernel, slab), [whole] * 4 + [(5 * REACH,) +...  5.05 us
    ppermute x3, starting transfers between devices, on_device(): lax.ppermute(outer_parts[k], 'shot', shifts[k])  4.73 us
    pallas_call x1, Pallas kernels, on_device(): call(functools.partial(inner_kernel, slab, shots), [(4 * REACH,) + plane]...  4.38 us
    ppermute x1, starting transfers between devices, on_device(): halo_early = lax.ppermute(own_early, 'space', out_pairs)  3.32 us
    ppermute x1, starting transfers between devices, on_device(): halo_late = lax.ppermute(own_late, 'space', out_pairs)  3.13 us
  transfers between devices with their start and end apart: 9, of which 4 were waited for; matrix products, arithmetic and copies ran while one was open for 0% of the time, Pallas kernels for 7%

profile of v1, /device:TPU:3, one launch (start us, length us, event | category | flops | bytes accessed | tf_op | source)
XLA Modules:
  0.0 68.0 jit_solution(5153258367158720411)
XLA Ops:
  1.3 0.0 copy-start
  1.3 1.0 %copy-done = f32[8,64,256]{2,1,0:T(8,128)S(1)} copy-done((f32[8,64,256]{2,1,0:T(8,128)S(1)}, f32[8,64,256]{2,1,0:T(8,128)}, u32[]{:S(2)}) %copy-start) | copy-done | bytes 524312
  2.3 0.0 copy-start.2
  2.3 1.0 %copy-done.2 = f32[1,8,64,256]{3,2,1,0:T(8,128)S(1)} copy-done((f32[1,8,64,256]{3,2,1,0:T(8,128)S(1)}, f32[1,8,64,256]{3,2,1,0:T(8,128)}, u32[]{:S(2)}) %copy-start.2) | copy-done | bytes 524312
  3.4 0.0 copy-start.4
  3.4 1.0 %copy-done.4 = f32[1,8,64,256]{3,2,1,0:T(8,128)S(1)} copy-done((f32[1,8,64,256]{3,2,1,0:T(8,128)S(1)}, f32[1,8,64,256]{3,2,1,0:T(8,128)}, u32[]{:S(2)}) %copy-start.4) | copy-done | bytes 524312
  4.4 0.0 copy-start.6
  4.4 1.0 %copy-done.6 = f32[1,8,64,256]{3,2,1,0:T(8,128)S(1)} copy-done((f32[1,8,64,256]{3,2,1,0:T(8,128)S(1)}, f32[1,8,64,256]{3,2,1,0:T(8,128)}, u32[]{:S(2)}) %copy-start.6) | copy-done | bytes 524312
  5.5 0.0 copy-start.7
  5.5 1.0 %copy-done.7 = f32[1,8,64,256]{3,2,1,0:T(8,128)S(1)} copy-done((f32[1,8,64,256]{3,2,1,0:T(8,128)S(1)}, f32[1,8,64,256]{3,2,1,0:T(8,128)}, u32[]{:S(2)}) %copy-start.7) | copy-done | bytes 524312
  6.5 0.0 copy-start.8
  6.5 0.7 copy-done.8
  7.2 0.0 copy-start.9
  7.2 0.7 copy-done.9
  7.8 0.0 copy-start.10
  7.8 0.7 copy-done.10
  8.5 0.0 copy-start.11
  8.5 0.7 copy-done.11
  9.2 0.0 copy-start.1
  9.2 0.0 copy-start.3
  9.2 5.1 %shard_map.109 = (f32[8,64,256]{2,1,0:T(8,128)S(1)}, f32[8,64,256]{2,1,0:T(8,128)S(1)}, f32[8,64,256]{2,1,0:T(8,128)S(1)}, f32[8,64,256]{2,1,0:T(8,128)S(1)}, f3...) custom-call(s32[1]{0:T(128)S(6)} %copy.12.source_x, s32[1]{0:T(128)S(6)} %copy.13.source_yz, f32[1,2]{1,0:T(1,128)S(1)} %copy-done.9, ...), custom_call_target="tpu_custom_call" | custom-call | flops 13107200 | bytes 6815744 | tf_op jit(solution)/shard_map/pallas_call | solution.py:340
  14.3 0.0 copy-start.5
  14.3 0.7 %collective-permute-start = (f32[20,64,256]{2,1,0:T(8,128)}, f32[20,64,256]{2,1,0:T(8,128)S(1)}, u32[]{:S(2)}, u32[]{:S(2)}) collective-permute-start(f32[20,64,256]{2,1,0:T(8,128)} %get-tuple-element.24.own_in), channel_id=1, source_target_pairs={{0,1},{1,0},{2,3},{3,2},{4,5},{5,4},{6,7},{7,6},{8,9},{9,8},{10,11... | collective-permute-start | bytes 3932168 | tf_op jit(solution)/shard_map/ppermute | solution.py:364
  15.0 3.1 %collective-permute-start.2 = (f32[12,64,256]{2,1,0:T(8,128)S(1)}, f32[12,64,256]{2,1,0:T(8,128)S(1)}, u32[]{:S(2)}, u32[]{:S(2)}) collective-permute-start(f32[12,64,256]{2,1,0:T(8,128)S(1)} %get-tuple-element.26), channel_id=1, source_target_pairs={{1,2},{3,4},{5,6},{2,1},{4,3},{6,5},{9,10},{11,12},{13,14},{10,9},... | collective-permute-start | bytes 2359304 | tf_op jit(solution)/shard_map/ppermute | solution.py:365
  18.1 0.0 copy-done.1
  18.1 0.0 copy-done.3
  18.1 0.1 shard_map.110.own_early
  18.3 3.3 %collective-permute-start.1 = (f32[8,64,256]{2,1,0:T(8,128)S(1)}, f32[8,64,256]{2,1,0:T(8,128)S(1)}, u32[]{:S(2)}, u32[]{:S(2)}) collective-permute-start(f32[8,64,256]{2,1,0:T(8,128)S(1)} %shard_map.110.own_early), channel_id=1, source_target_pairs={{1,2},{3,4},{5,6},{2,1},{4,3},{6,5},{9,10},{11,12},{13,14},{10,9},... | collective-permute-start | bytes 1572872 | tf_op jit(solution)/shard_map/ppermute | solution.py:337
  21.6 26.7 %collective-permute-done.1.halo_early = f32[8,64,256]{2,1,0:T(8,128)S(1)} collective-permute-done((f32[8,64,256]{2,1,0:T(8,128)S(1)}, f32[8,64,256]{2,1,0:T(8,128)S(1)}, u32[]{:S(2)}, u32[]{:S(2)}) %collective-permute-start.1) | collective-permute-done | bytes 524320 | tf_op jit(solution)/shard_map/ppermute | solution.py:337
  48.3 0.0 collective-permute-done.halo_in
  48.3 0.0 copy-start.12
  48.3 1.1 %copy-done.12 = f32[20,64,256]{2,1,0:T(8,128)} copy-done((f32[20,64,256]{2,1,0:T(8,128)}, f32[20,64,256]{2,1,0:T(8,128)S(1)}, u32[]{:S(2)}) %copy-start.12) | copy-done | bytes 1310744
  49.4 0.0 copy-done.5
  49.4 4.4 %shard_map.111 = (f32[16,64,256]{2,1,0:T(8,128)S(1)}, f32[4,16,256]{2,1,0:T(8,128)S(1)}, f32[4,16,256]{2,1,0:T(8,128)S(1)}, f32[4,16,256]{2,1,0:T(8,128)S(1)}, f32[4,16,256]{2,1,0:T(8,128)S(1)}) custom-call(s32[1]{0:T(128)S(6)} %copy.12.source_x, s32[1]{0:T(128)S(6)} %copy.13.source_yz, f32[1,2]{1,0:T(1,128)S(1)} %copy-done.9, f32[8,64,256]{2,1,0:T(8,128)S(1)} %copy-done.1, ...), custom_call_target="tpu_custom_call" | custom-call | flops 13107200 | bytes 6815744 | tf_op jit(solution)/shard_map/pallas_call | solution.py:367
  53.8 0.0 collective-permute-done.2.halo_late
  53.8 0.4 shard_map.112
  54.2 1.4 %collective-permute-start.3 = (f32[4,16,256]{2,1,0:T(8,128)S(1)}, f32[4,16,256]{2,1,0:T(8,128)S(1)}, u32[]{:S(2)}, u32[]{:S(2)}) collective-permute-start(f32[4,16,256]{2,1,0:T(8,128)S(1)} %get-tuple-element.28), channel_id=1, source_target_pairs={{0,8},{8,16},{16,24},{24,0},{1,9},{9,17},{17,25},{25,1},{2,10},{10... | collective-permute-start | bytes 196616 | tf_op jit(solution)/shard_map/ppermute | solution.py:412
  55.5 2.3 %collective-permute-start.4 = (f32[4,16,256]{2,1,0:T(8,128)S(1)}, f32[4,16,256]{2,1,0:T(8,128)S(1)}, u32[]{:S(2)}, u32[]{:S(2)}) collective-permute-start(f32[4,16,256]{2,1,0:T(8,128)S(1)} %get-tuple-element.29), channel_id=1, source_target_pairs={{0,16},{8,24},{16,0},{24,8},{1,17},{9,25},{17,1},{25,9},{2,18},{10... | collective-permute-start | bytes 196616 | tf_op jit(solution)/shard_map/ppermute | solution.py:412
  57.8 1.1 %collective-permute-start.5 = (f32[4,16,256]{2,1,0:T(8,128)S(1)}, f32[4,16,256]{2,1,0:T(8,128)S(1)}, u32[]{:S(2)}, u32[]{:S(2)}) collective-permute-start(f32[4,16,256]{2,1,0:T(8,128)S(1)} %get-tuple-element.30), channel_id=1, source_target_pairs={{0,24},{8,0},{16,8},{24,16},{1,25},{9,1},{17,9},{25,17},{2,26},{10... | collective-permute-start | bytes 196616 | tf_op jit(solution)/shard_map/ppermute | solution.py:412
  58.9 0.4 collective-permute-start.6
  59.3 0.1 collective-permute-start.7
  59.3 0.5 collective-permute-done.3.refs_1_
  59.9 2.3 %collective-permute-start.8 = (f32[4,16,256]{2,1,0:T(8,128)S(1)}, f32[4,16,256]{2,1,0:T(8,128)S(1)}, u32[]{:S(2)}, u32[]{:S(2)}) collective-permute-start(f32[4,16,256]{2,1,0:T(8,128)S(1)} %get-tuple-element.34), channel_id=1, source_target_pairs={{0,24},{8,0},{16,8},{24,16},{1,25},{9,1},{17,9},{25,17},{2,26},{10... | collective-permute-start | bytes 196616 | tf_op jit(solution)/shard_map/ppermute | solution.py:397
  62.2 0.0 collective-permute-done.4.refs_2_
  62.2 0.0 collective-permute-done.5.refs_3_
  62.2 2.4 %collective-permute-done.6.refs_5_ = f32[4,16,256]{2,1,0:T(8,128)S(1)} collective-permute-done((f32[4,16,256]{2,1,0:T(8,128)S(1)}, f32[4,16,256]{2,1,0:T(8,128)S(1)}, u32[]{:S(2)}, u32[]{:S(2)}) %collective-permute-start.6) | collective-permute-done | bytes 65568 | tf_op jit(solution)/shard_map/ppermute | solution.py:397
  64.6 2.8 %collective-permute-done.7.refs_6_ = f32[4,16,256]{2,1,0:T(8,128)S(1)} collective-permute-done((f32[4,16,256]{2,1,0:T(8,128)S(1)}, f32[4,16,256]{2,1,0:T(8,128)S(1)}, u32[]{:S(2)}, u32[]{:S(2)}) %collective-permute-start.7) | collective-permute-done | bytes 65568 | tf_op jit(solution)/shard_map/ppermute | solution.py:397
  67.4 0.0 collective-permute-done.8.refs_7_
  67.4 0.7 %shard_map.113 = f32[8,16,256]{2,1,0:T(8,128)} custom-call(f32[4,16,256]{2,1,0:T(8,128)S(1)} %get-tuple-element.27.refs_0_, f32[4,16,256]{2,1,0:T(8,128)S(1)} %collective-permute-done.3.refs_1_, f32[4,16,256]{2,1,0:T(8,128)S(1)} %collective-permute-done.4.refs_2_, f32[4,16,256]{2,1,0:T(8,128)S(1)} %collective-permute-done.5.refs_3_, ...), custom_call_target="tpu_custom_call" | custom-call | flops 131072 | bytes 1048576 | tf_op jit(solution)/shard_map/pallas_call | solution.py:414
Async XLA Ops:
  1.3 1.0 %copy-start = (f32[8,64,256]{2,1,0:T(8,128)S(1)}, f32[8,64,256]{2,1,0:T(8,128)}, u32[]{:S(2)}) copy-start(f32[8,64,256]{2,1,0:T(8,128)} %courant.7) | copy-start | bytes 1572868
  2.3 1.0 %copy-start.2 = (f32[1,8,64,256]{3,2,1,0:T(8,128)S(1)}, f32[1,8,64,256]{3,2,1,0:T(8,128)}, u32[]{:S(2)}) copy-start(f32[1,8,64,256]{3,2,1,0:T(8,128)} %param.13) | copy-start | bytes 1572868
  3.4 1.0 %copy-start.4 = (f32[1,8,64,256]{3,2,1,0:T(8,128)S(1)}, f32[1,8,64,256]{3,2,1,0:T(8,128)}, u32[]{:S(2)}) copy-start(f32[1,8,64,256]{3,2,1,0:T(8,128)} %param.15) | copy-start | bytes 1572868
  4.4 1.0 %copy-start.6 = (f32[1,8,64,256]{3,2,1,0:T(8,128)S(1)}, f32[1,8,64,256]{3,2,1,0:T(8,128)}, u32[]{:S(2)}) copy-start(f32[1,8,64,256]{3,2,1,0:T(8,128)} %param.12) | copy-start | bytes 1572868
  5.5 1.0 %copy-start.7 = (f32[1,8,64,256]{3,2,1,0:T(8,128)S(1)}, f32[1,8,64,256]{3,2,1,0:T(8,128)}, u32[]{:S(2)}) copy-start(f32[1,8,64,256]{3,2,1,0:T(8,128)} %param.14) | copy-start | bytes 1572868
  6.5 0.7 %copy-start.8 = (f32[1,256,2]{1,2,0:T(2,128)S(1)}, f32[1,256,2]{1,2,0:T(2,128)}, u32[]{:S(2)}) copy-start(f32[1,256,2]{1,2,0:T(2,128)} %param.21) | copy-start | bytes 6148
  7.2 0.7 copy-start.9
  7.8 0.7 copy-start.10
  8.5 0.7 copy-start.11
  9.2 8.9 %copy-start.1 = (f32[8,64,256]{2,1,0:T(8,128)S(1)}, f32[8,64,256]{2,1,0:T(8,128)}, u32[]{:S(2)}) copy-start(f32[8,64,256]{2,1,0:T(8,128)} %courant.7) | copy-start | bytes 1572868
  9.2 8.9 %copy-start.3 = (f32[1,8,64,256]{3,2,1,0:T(8,128)S(1)}, f32[1,8,64,256]{3,2,1,0:T(8,128)}, u32[]{:S(2)}) copy-start(f32[1,8,64,256]{3,2,1,0:T(8,128)} %param.13) | copy-start | bytes 1572868
  14.3 35.1 %copy-start.5 = (f32[20,64,256]{2,1,0:T(8,128)S(1)}, f32[20,64,256]{2,1,0:T(8,128)}, u32[]{:S(2)}) copy-start(f32[20,64,256]{2,1,0:T(8,128)} %get-tuple-element.24.own_in) | copy-start | bytes 3932164
  14.3 34.1 %collective-permute-start = (f32[20,64,256]{2,1,0:T(8,128)}, f32[20,64,256]{2,1,0:T(8,128)S(1)}, u32[]{:S(2)}, u32[]{:S(2)}) collective-permute-start(f32[20,64,256]{2,1,0:T(8,128)} %get-tuple-element.24.own_in), channel_id=1, source_target_pairs={{0,1},{1,0},{2,3},{3,2},{4,5},{5,4},{6,7},{7,6},{8,9},{9,8},{10,11... | collective-permute-start | bytes 3932168 | tf_op jit(solution)/shard_map/ppermute | solution.py:364
  15.0 38.8 %collective-permute-start.2 = (f32[12,64,256]{2,1,0:T(8,128)S(1)}, f32[12,64,256]{2,1,0:T(8,128)S(1)}, u32[]{:S(2)}, u32[]{:S(2)}) collective-permute-start(f32[12,64,256]{2,1,0:T(8,128)S(1)} %get-tuple-element.26), channel_id=1, source_target_pairs={{1,2},{3,4},{5,6},{2,1},{4,3},{6,5},{9,10},{11,12},{13,14},{10,9},... | collective-permute-start | bytes 2359304 | tf_op jit(solution)/shard_map/ppermute | solution.py:365
  18.3 30.1 %collective-permute-start.1 = (f32[8,64,256]{2,1,0:T(8,128)S(1)}, f32[8,64,256]{2,1,0:T(8,128)S(1)}, u32[]{:S(2)}, u32[]{:S(2)}) collective-permute-start(f32[8,64,256]{2,1,0:T(8,128)S(1)} %shard_map.110.own_early), channel_id=1, source_target_pairs={{1,2},{3,4},{5,6},{2,1},{4,3},{6,5},{9,10},{11,12},{13,14},{10,9},... | collective-permute-start | bytes 1572872 | tf_op jit(solution)/shard_map/ppermute | solution.py:337
  48.3 1.1 %copy-start.12 = (f32[20,64,256]{2,1,0:T(8,128)}, f32[20,64,256]{2,1,0:T(8,128)S(1)}, u32[]{:S(2)}) copy-start(f32[20,64,256]{2,1,0:T(8,128)S(1)} %collective-permute-done.halo_in) | copy-start | bytes 3932164
  54.2 5.7 %collective-permute-start.3 = (f32[4,16,256]{2,1,0:T(8,128)S(1)}, f32[4,16,256]{2,1,0:T(8,128)S(1)}, u32[]{:S(2)}, u32[]{:S(2)}) collective-permute-start(f32[4,16,256]{2,1,0:T(8,128)S(1)} %get-tuple-element.28), channel_id=1, source_target_pairs={{0,8},{8,16},{16,24},{24,0},{1,9},{9,17},{17,25},{25,1},{2,10},{10... | collective-permute-start | bytes 196616 | tf_op jit(solution)/shard_map/ppermute | solution.py:412
  55.5 6.7 %collective-permute-start.4 = (f32[4,16,256]{2,1,0:T(8,128)S(1)}, f32[4,16,256]{2,1,0:T(8,128)S(1)}, u32[]{:S(2)}, u32[]{:S(2)}) collective-permute-start(f32[4,16,256]{2,1,0:T(8,128)S(1)} %get-tuple-element.29), channel_id=1, source_target_pairs={{0,16},{8,24},{16,0},{24,8},{1,17},{9,25},{17,1},{25,9},{2,18},{10... | collective-permute-start | bytes 196616 | tf_op jit(solution)/shard_map/ppermute | solution.py:412
  57.8 4.3 %collective-permute-start.5 = (f32[4,16,256]{2,1,0:T(8,128)S(1)}, f32[4,16,256]{2,1,0:T(8,128)S(1)}, u32[]{:S(2)}, u32[]{:S(2)}) collective-permute-start(f32[4,16,256]{2,1,0:T(8,128)S(1)} %get-tuple-element.30), channel_id=1, source_target_pairs={{0,24},{8,0},{16,8},{24,16},{1,25},{9,1},{17,9},{25,17},{2,26},{10... | collective-permute-start | bytes 196616 | tf_op jit(solution)/shard_map/ppermute | solution.py:412
  58.9 5.7 %collective-permute-start.6 = (f32[4,16,256]{2,1,0:T(8,128)S(1)}, f32[4,16,256]{2,1,0:T(8,128)S(1)}, u32[]{:S(2)}, u32[]{:S(2)}) collective-permute-start(f32[4,16,256]{2,1,0:T(8,128)S(1)} %get-tuple-element.32), channel_id=1, source_target_pairs={{0,8},{8,16},{16,24},{24,0},{1,9},{9,17},{17,25},{25,1},{2,10},{10... | collective-permute-start | bytes 196616 | tf_op jit(solution)/shard_map/ppermute | solution.py:397
  59.3 8.1 %collective-permute-start.7 = (f32[4,16,256]{2,1,0:T(8,128)S(1)}, f32[4,16,256]{2,1,0:T(8,128)S(1)}, u32[]{:S(2)}, u32[]{:S(2)}) collective-permute-start(f32[4,16,256]{2,1,0:T(8,128)S(1)} %get-tuple-element.33), channel_id=1, source_target_pairs={{0,16},{8,24},{16,0},{24,8},{1,17},{9,25},{17,1},{25,9},{2,18},{10... | collective-permute-start | bytes 196616 | tf_op jit(solution)/shard_map/ppermute | solution.py:397
  59.9 7.5 %collective-permute-start.8 = (f32[4,16,256]{2,1,0:T(8,128)S(1)}, f32[4,16,256]{2,1,0:T(8,128)S(1)}, u32[]{:S(2)}, u32[]{:S(2)}) collective-permute-start(f32[4,16,256]{2,1,0:T(8,128)S(1)} %get-tuple-element.34), channel_id=1, source_target_pairs={{0,24},{8,0},{16,8},{24,16},{1,25},{9,1},{17,9},{25,17},{2,26},{10... | collective-permute-start | bytes 196616 | tf_op jit(solution)/shard_map/ppermute | solution.py:397

commit v2 on v0

v2 whole, which is shorter than its diff:
```python
import functools
import jax
import jax.numpy as jnp
from jax import lax
from jax.experimental import pallas as pl
from jax.experimental.pallas import tpu as pltpu
from jax.sharding import PartitionSpec as P

MIDDLE = 3.0 * (-205.0 / 72.0)
SIDE = (8.0 / 5.0, -1.0 / 5.0, 8.0 / 315.0, -1.0 / 560.0)
REACH = 4
F32 = jnp.float32
BF16 = jnp.bfloat16
VMEM_LIMIT = 32 * 1024 * 1024
SMALL, LARGE = 10**6, 10**10


def placed(layer, outward, odd):
    layer = layer if outward else 2 * REACH - 1 - layer
    return layer + odd * (2 * REACH - 1 - 2 * layer)


def grids(size_y, size_z):
    rows = lax.broadcasted_iota(jnp.int32, (size_y, size_z), 0)
    columns = lax.broadcasted_iota(jnp.int32, (size_y, size_z), 1)
    return rows, columns


def three_parts(values):
    high = values.astype(BF16)
    rest = values - high.astype(F32)
    middle = rest.astype(BF16)
    return high, middle, (rest - middle.astype(F32)).astype(BF16)


def exact_dot(left, right):
    def dot(a, b):
        return jnp.dot(left[a], right[b], preferred_element_type=F32)

    return dot(0, 0) + (dot(0, 1) + dot(1, 0)) + (dot(1, 1) + dot(0, 2) + dot(2, 0))


def band(size, block, middle):
    rows, columns = grids(size, size)
    distance = jnp.abs(rows - columns)
    weights = jnp.where(distance == 0, middle, 0.0)
    for offset in range(1, REACH + 1):
        weights = jnp.where(distance == offset, SIDE[offset - 1], weights)
    bits = block.bit_length() - 1
    return jnp.where(jnp.right_shift(rows, bits) == jnp.right_shift(columns, bits), weights, 0.0)


def plane_laplace(layers, along_y, along_z):
    shape = (len(layers),) + layers[0].shape
    parts = three_parts(jnp.concatenate(layers, axis=0))
    return (exact_dot(parts, along_z) + exact_dot(along_y, parts)).reshape(shape)


def weighted(terms):
    total = None
    for distance in range(1, REACH + 1):
        found = [layer() for at, layer in terms if at == distance]
        if found:
            term = SIDE[distance - 1] * functools.reduce(lambda a, b: a + b, found)
            total = term if total is None else total + term
    return total


def within(at, layers):
    return weighted([(abs(at - i), lambda i=i: layers(i)) for i in range(REACH) if i != at])


def from_other(at, layers):
    last = 2 * REACH - 1
    return weighted([(last - i - at, lambda i=i: layers(i)) for i in range(REACH)])


def across(at, layers):
    return weighted([(at + 1 + i, lambda i=i: layers(i)) for i in range(REACH)])


def add(*values):
    return functools.reduce(lambda a, b: a + b, [v for v in values if v is not None])


def early_kernel(courant, now, adjoint, *refs):
    packets, adjoints, sems = refs[:2], refs[2:4], refs[4]
    odd = lax.rem(lax.axis_index("space"), 2)
    copies = []
    for half in range(2):
        for layer in range(REACH):
            at = placed(layer, half == 0, odd)
            for source, target in (
                (courant.at[at], packets[half].at[2 * REACH + layer]),
                (adjoint.at[at], adjoints[half].at[layer]),
                (now.at[at], packets[half].at[layer]),
            ):
                copies.append(pltpu.make_async_copy(source, target, sems.at[len(copies)]))
                copies[-1].start()
    for copy in copies:
        copy.wait()
    for half in range(2):
        for layer in range(REACH):
            speed = packets[half][2 * REACH + layer]
            packets[half][REACH + layer] = speed * speed * adjoints[half][layer]


def half_kernel(outward, mine, other, adjoint_now, old, late, *refs):
    if outward:
        accel, adjoint, packet, bands = refs[:4]
    else:
        bands, accel, adjoint, packet = refs[:4]
    old_half, late_half, sems = refs[4:]
    size_y, size_z = mine.shape[1:]
    odd = lax.rem(lax.axis_index("space"), 2)
    copies = []
    for layer in range(REACH):
        at = placed(layer, outward, odd)
        for source, target in ((old.at[at], old_half), (late.at[at], late_half)):
            copies.append(
                pltpu.make_async_copy(source, target.at[layer], sems.at[len(copies)])
            )
            copies[-1].start()
    if outward:
        along_y = three_parts(band(REACH * size_y, size_y, 0.0))
        along_z = three_parts(band(size_z, size_z, MIDDLE))
        for number in range(3):
            bands[number] = along_y[number]
            bands[3 + number] = along_z[number]
    else:
        along_y, along_z = bands[0:3], bands[3:6]
    flat = [
        plane_laplace([mine[first + at] for at in range(REACH)], along_y, along_z)
        for first in (0, REACH)
    ]
    for copy in copies:
        copy.wait()
    for at in range(REACH):
        speed = mine[2 * REACH + at]
        speed_sq = speed * speed
        laplace = add(
            flat[0][at],
            within(at, lambda i: mine[i]),
            from_other(at, lambda i: other[i]),
        )
        accel[at] = laplace
        packet[at] = 2.0 * mine[at] - old_half[at] + speed_sq * laplace
        laplace = add(
            flat[1][at],
            within(at, lambda i: mine[REACH + i]),
            from_other(at, lambda i: other[REACH + i]),
        )
        field = 2.0 * adjoint_now[at] - late_half[at] + laplace
        adjoint[at] = field
        packet[REACH + at] = speed_sq * field


def next_halo(at, speed, late, own, points):
    speed_sq = speed * speed
    mid = late[at] + speed_sq * (across(at, lambda i: own[i]) + points[at])
    scaled = late[REACH + at] + speed_sq * (
        across(at, lambda i: own[REACH + i]) + points[REACH + at]
    )
    return mid, scaled


def scatter_rows(gradient, outputs, shots):
    rows = gradient.shape[1] // shots
    me = lax.axis_index("shot")
    for shift in range(shots):
        first = pl.multiple_of(jnp.bitwise_xor(me, shift) * rows, rows)
        outputs[shift][...] = gradient[:, pl.ds(first, rows), :]


def inner_kernel(
    pulse,
    receiver_x,
    receiver_yz,
    residual,
    own_in,
    own_out,
    accel_in,
    accel_out,
    adjoint_in,
    adjoint_out,
    late_in,
    late_out,
    now_in,
    now_out,
    bands,
    halo_early,
    halo_late,
    inner,
    outer,
    forward,
    backward,
    points_out,
    marks,
    added,
    points_in,
    mid,
    scaled,
    next_mid,
    next_scaled,
):
    slab = 2 * REACH
    space = lax.axis_index("space")
    odd = lax.rem(space, 2)
    size_y, size_z = own_in.shape[1:]
    along_y, along_z = bands[0:3], bands[3:6]
    z_bits = size_z.bit_length() - 1

    def counted(x):
        local = x - space * slab
        return REACH + local + odd * (slab - 1 - 2 * local)

    cells = receiver_yz[...]
    layer = counted(receiver_x[...])
    inside = (layer >= 0) & (layer < 2 * slab)
    wanted = jnp.where(inside, layer * size_y + jnp.right_shift(cells, z_bits), -1)
    count = wanted.shape[1]
    line = lax.broadcasted_iota(jnp.int32, (2 * slab * size_y, count), 0)
    marks[...] = jnp.where(line == wanted, 1.0, 0.0).astype(BF16)
    depth = lax.broadcasted_iota(jnp.int32, (size_z, count), 0)
    hit = depth == jnp.bitwise_and(cells, size_z - 1)

    def received(step, first, last):
        total = None
        for part in three_parts(residual[pl.ds(step, 1), :]):
            spread = jnp.where(hit, part.astype(F32), 0.0).astype(BF16)
            term = lax.dot_general(
                marks[first * size_y : last * size_y],
                spread,
                (((1,), (1,)), ((), ())),
                preferred_element_type=F32,
            )
            total = term if total is None else total + term
        return total.reshape(last - first, size_y, size_z)

    added[0 : 2 * slab] = received(0, 0, 2 * slab)
    added[2 * slab :] = received(1, REACH, REACH + slab)

    rows, columns = grids(size_y, size_z)
    cell = rows * size_z + columns
    source_layer = counted(pulse[:, 2:3].astype(jnp.int32))
    source_cell = pulse[:, 3:4].astype(jnp.int32)

    def fired(step, at):
        spot = jnp.where(source_layer == at, source_cell, -1)
        return jnp.where(cell == spot, pulse[:, step : step + 1], 0.0)

    for at in range(REACH):
        points_out[at] = fired(0, REACH - 1 - at)
        points_out[REACH + at] = added[REACH - 1 - at]
        points_in[at] = fired(0, REACH + slab + at)
        points_in[REACH + at] = added[REACH + slab + at]
        speed = own_out[2 * REACH + at]
        fire = fired(0, REACH + at)
        outer[at] = accel_out[at] + fire
        outer[REACH + at] = adjoint_out[at] + added[REACH + at]
        outer[2 * REACH + at] = late_out[at] + speed * speed * fire
    for at in range(REACH):
        next_mid[at], next_scaled[at] = next_halo(
            at, halo_early[2 * REACH + at], halo_late, own_in, points_in
        )
    for at in range(REACH):
        to = REACH + slab - 1 - at
        speed = own_in[2 * REACH + at]
        speed_sq = speed * speed
        extra = across(at, lambda i: halo_early[i]) + fired(0, to)
        adjoint = adjoint_in[at] + across(at, lambda i: halo_early[REACH + i]) + added[to]
        inner[at] = accel_in[at] + extra
        inner[REACH + at] = adjoint
        mid[at] = late_in[at] + speed_sq * extra
        scaled[at] = speed_sq * adjoint
    flat_mid = plane_laplace([mid[at] for at in range(REACH)], along_y, along_z)
    flat_scaled = plane_laplace([scaled[at] for at in range(REACH)], along_y, along_z)
    for at in range(REACH):
        to = REACH + at
        forward[at] = add(fired(1, to), from_other(at, lambda i: mid[i]))
        backward[at] = add(
            added[2 * slab + at] - now_out[at],
            from_other(at, lambda i: scaled[i]),
        )
        to = REACH + slab - 1 - at
        forward[REACH + at] = add(
            flat_mid[at],
            fired(1, to),
            within(at, lambda i: mid[i]),
            across(at, lambda i: next_mid[i]),
        )
        backward[REACH + at] = add(
            flat_scaled[at],
            added[2 * slab + slab - 1 - at] - now_in[at],
            2.0 * inner[REACH + at],
            within(at, lambda i: scaled[i]),
            across(at, lambda i: next_scaled[i]),
        )


def middle_kernel(
    shots, own_in, own_out, bands, halo, inner, outer_part, forward, backward, outer, *rest
):
    outputs, (mid, scaled, gradient) = rest[:shots], rest[shots:]
    along_y, along_z = bands[0:3], bands[3:6]
    for at in range(REACH):
        speed = own_out[2 * REACH + at]
        speed_sq = speed * speed
        extra = across(at, lambda i: halo[i])
        adjoint = outer_part[REACH + at] + across(at, lambda i: halo[REACH + i])
        outer[at] = outer_part[at] + extra
        outer[REACH + at] = adjoint
        mid[at] = outer_part[2 * REACH + at] + speed_sq * extra
        scaled[at] = speed_sq * adjoint
    for at in range(REACH):
        ahead = add(forward[REACH + at], from_other(at, lambda i: mid[i]))
        back = add(backward[REACH + at], from_other(at, lambda i: scaled[i]))
        speed = own_in[2 * REACH + at]
        gradient[at] = 2.0 * speed * (back * inner[at] + inner[REACH + at] * ahead)
    scatter_rows(gradient, outputs, shots)
    flat_mid = plane_laplace([mid[at] for at in range(REACH)], along_y, along_z)
    flat_scaled = plane_laplace([scaled[at] for at in range(REACH)], along_y, along_z)
    for at in range(REACH):
        outer[2 * REACH + at] = add(forward[at], flat_mid[at], within(at, lambda i: mid[i]))
        outer[3 * REACH + at] = add(
            backward[at],
            2.0 * outer[REACH + at],
            flat_scaled[at],
            within(at, lambda i: scaled[i]),
        )


def outer_kernel(shots, relayed, own_out, outer, halo_early, points_out, *rest):
    lates, rest = rest[: 1 + relayed], rest[1 + relayed :]
    outputs, (late, next_mid, next_scaled, gradient) = rest[:shots], rest[shots:]
    if relayed:
        for layer in range(2 * REACH):
            late[layer] = lates[0][layer] + lates[1][layer]
    else:
        late = lates[0]
    for at in range(REACH):
        next_mid[at], next_scaled[at] = next_halo(
            at, halo_early[2 * REACH + at], late, own_out, points_out
        )
    for at in range(REACH):
        ahead = outer[2 * REACH + at] + across(at, lambda i: next_mid[i])
        back = outer[3 * REACH + at] + across(at, lambda i: next_scaled[i])
        speed = own_out[2 * REACH + at]
        gradient[at] = 2.0 * speed * (back * outer[at] + outer[REACH + at] * ahead)
    scatter_rows(gradient, outputs, shots)


def add_kernel(*refs):
    refs[-1][...] = functools.reduce(lambda a, b: a + b, [ref[...] for ref in refs[:-1]])


def sum_kernel(inner, *refs):
    outers, out = refs[:-1], refs[-1]
    odd = lax.rem(lax.axis_index("space"), 2)
    for at in range(REACH):
        out[placed(at, True, odd)] = functools.reduce(lambda a, b: a + b, [r[at] for r in outers])
        out[placed(at, False, odd)] = inner[at]


def call(kernel, shapes, in_spaces, scratch, flops, moved):
    def shape(given):
        return jax.ShapeDtypeStruct(given, F32) if isinstance(given, tuple) else given

    many = isinstance(shapes, list)
    return pl.pallas_call(
        kernel,
        out_shape=[shape(s) for s in shapes] if many else shape(shapes),
        in_specs=[pl.BlockSpec(memory_space=space) for space in in_spaces],
        out_specs=[pl.BlockSpec(memory_space=pltpu.VMEM) for _ in shapes]
        if many
        else pl.BlockSpec(memory_space=pltpu.VMEM),
        scratch_shapes=scratch,
        compiler_params=pltpu.CompilerParams(vmem_limit_bytes=VMEM_LIMIT),
        cost_estimate=pl.CostEstimate(flops=flops, bytes_accessed=moved, transcendentals=0),
    )


def both_ways(pairs):
    return pairs + [(b, a) for a, b in pairs]


def on_device(
    courant,
    field_old,
    field_now,
    adjoint_late,
    adjoint_now,
    source_x,
    source_yz,
    wavelet,
    receiver_x,
    receiver_yz,
    residual_trace,
):
    slab, size_y, size_z = courant.shape
    if slab != 2 * REACH:
        raise ValueError("unsupported slab")
    shots = lax.axis_size("shot")
    devices = lax.axis_size("space")
    plane = size_y * size_z
    part_rows = size_y // shots
    V, H = pltpu.VMEM, pltpu.HBM

    def stack(layers):
        return (layers, size_y, size_z)

    def held(layers):
        return pltpu.VMEM(stack(layers), F32)

    def in_hbm(values):
        return pltpu.with_memory_space_constraint(values, pltpu.HBM)

    out_pairs = both_ways([(i, i + 1) for i in range(1, devices - 1, 2)])
    in_pairs = [(i, i ^ 1) for i in range(devices)]
    relayed = devices == 8
    fields = [courant] + [f[0] for f in (adjoint_now, field_now, adjoint_late, field_old)]
    courant, adjoint, now, late, old = [in_hbm(f) for f in fields]
    place = [source_x.astype(F32), source_yz.astype(F32)]
    pulse = jnp.concatenate([wavelet[0]] + place).reshape(1, 4)

    own_out, own_in, now_out, now_in = call(
        early_kernel,
        [stack(3 * REACH)] * 2 + [stack(REACH)] * 2,
        [H] * 3,
        [pltpu.SemaphoreType.DMA((6 * REACH,))],
        SMALL,
        SMALL,
    )(courant, now, adjoint)
    halo_out = lax.ppermute(own_out, "space", out_pairs)
    halo_in = lax.ppermute(own_in, "space", in_pairs)

    bands = jax.ShapeDtypeStruct((6, size_z, size_z), BF16)

    def half(outward, *given):
        return call(
            functools.partial(half_kernel, outward),
            [stack(REACH)] * 2 + [stack(2 * REACH)] + [bands] * outward,
            [V] * 3 + [H] * 2 + [V] * (not outward),
            [held(REACH)] * 2 + [pltpu.SemaphoreType.DMA((2 * REACH,))],
            LARGE,
            SMALL,
        )(*given)

    accel_out, adjoint_out, late_out, bands = half(True, own_out, own_in, now_out, old, late)
    if relayed:
        first_hop = lax.ppermute(late_out, "space", [(3, 7), (4, 0)])
        halo_lates = [
            lax.ppermute(late_out, "space", both_ways([(1, 2), (5, 6)])),
            lax.ppermute(first_hop, "space", [(7, 4), (0, 3)]),
        ]
    else:
        halo_lates = [lax.ppermute(late_out, "space", out_pairs)]
    accel_in, adjoint_in, late_in = half(False, own_in, own_out, now_in, old, late, bands)
    halo_late_in = lax.ppermute(late_in, "space", in_pairs)

    inner, outer_part, forward, backward, points_out = call(
        inner_kernel,
        [stack(2 * REACH), stack(3 * REACH)] + [stack(2 * REACH)] * 3,
        [V] * 17,
        [
            pltpu.VMEM((2 * slab * size_y, receiver_x.shape[1]), BF16),
            held(3 * slab),
            held(2 * REACH),
        ]
        + [held(REACH)] * 4,
        SMALL,
        SMALL,
    )(
        pulse,
        receiver_x,
        receiver_yz,
        residual_trace[0].T,
        own_in,
        own_out,
        accel_in,
        accel_out,
        adjoint_in,
        adjoint_out,
        late_in,
        late_out,
        now_in,
        now_out,
        bands,
        halo_in,
        halo_late_in,
    )
    outer, *inner_parts = call(
        functools.partial(middle_kernel, shots),
        [stack(4 * REACH)] + [(REACH, part_rows, size_z)] * shots,
        [V] * 8,
        [held(REACH)] * 3,
        LARGE,
        SMALL,
    )(own_in, own_out, bands, halo_out, inner, outer_part, forward, backward)
    shifts = [[(i, i ^ k) for i in range(shots)] for k in range(shots)]
    inner_parts = inner_parts[:1] + [
        lax.ppermute(inner_parts[k], "shot", shifts[k]) for k in range(1, shots)
    ]
    inner_sum = call(add_kernel, (REACH, part_rows, size_z), [V] * shots, [], LARGE, SMALL)(
        *inner_parts
    )
    outer_parts = call(
        functools.partial(outer_kernel, shots, relayed),
        [(REACH, part_rows, size_z)] * shots,
        [V] * (4 + len(halo_lates)),
        [held(2 * REACH)] + [held(REACH)] * 3,
        SMALL,
        SMALL,
    )(own_out, outer, halo_out, points_out, *halo_lates)
    outer_parts = list(outer_parts[:1]) + [
        lax.ppermute(outer_parts[k], "shot", shifts[k]) for k in range(1, shots)
    ]
    return call(sum_kernel, (slab, part_rows, size_z), [V] * (1 + shots), [], SMALL, SMALL)(
        inner_sum, *outer_parts
    )


def solution(mesh):
    field = P("shot", "space", None, None)
    specs = (
        P("space", None, None),
        field,
        field,
        field,
        field,
        P("shot"),
        P("shot"),
        P("shot", None),
        P("shot", None),
        P("shot", None),
        P("shot", None, None),
    )
    return jax.shard_map(
        on_device, mesh=mesh, in_specs=specs, out_specs=P("space", "shot", None), check_vma=False
    )
```

time: 143 us -> 41.1 us (0.29)
  other arithmetic: 48.6 us -> 0.08 us
  waiting for transfers between devices: 42.9 us -> 10.8 us
  between operations: 18.9 us -> 1.45 us
  Pallas kernels: 0 us -> 10.5 us
  local copies, waits for them, and re-layouts: 8.36 us -> 1.33 us
  starting transfers between devices: 23.3 us -> 16.5 us
    psum x1 -> x0, waiting for transfers between devices: 42.8 us -> none  [on_device(): summed_all = lax.psum(gradient_terms, 'shot')]
    scatter-add x2 -> x0, other arithmetic: 24.6 us -> none  [inject(): flattened.at[shot_rows, local_x, cells_yz].add(amounts, mode='drop')]
    ppermute x8 -> x12, waiting for transfers between devices: 0.02 us -> 10.8 us  [the longest x3 5.06 us: on_device(): lax.ppermute(outer_parts[k], 'shot', shifts[k])]
    pallas_call x0 -> x8, Pallas kernels: none -> 10.5 us  [the longest x2 4.52 us: half(): call(functools.partial(half_kernel, outward), [stack(REACH)] * 2 + [stack...]
    add x4 -> x0, other arithmetic: 8.81 us -> none  [the longest x2 6.23 us: laplace_x(): summed + weight * (window(offset, 0, 0) + window(-offset, 0, 0) + window(...]
    ppermute x8 -> x12, starting transfers between devices: 23.3 us -> 16.5 us  [the longest x3 4.45 us: on_device(): lax.ppermute(inner_parts[k], 'shot', shifts[k])]
    unnamed x2 -> x0, other arithmetic: 5.64 us -> none
    concatenate x6 -> x0, other arithmetic: 4.5 us -> none  [the longest x4 4.41 us: with_halo(): block = jnp.concatenate([low, block, high], axis=dim)]
  transfers between devices with their start and end apart: 9 -> 12, of which waited for: 1 -> 3; matrix products, arithmetic and copies ran while one was open for 21% -> 0% of each run, Pallas kernels for 0% -> 20%
where the time goes in v2:
time: 41.1 us; the launch traced here: 40.7 us
  starting transfers between devices  16.5 us (40%)
  waiting for transfers between devices  10.8 us (26%)
  Pallas kernels  10.5 us (26%)
  between operations  1.45 us (4%)
  local copies, waits for them, and re-layouts  1.33 us (3%)
    ppermute x3, waiting for transfers between devices, on_device(): lax.ppermute(outer_parts[k], 'shot', shifts[k])  5.06 us
    pallas_call x2, Pallas kernels, half(): call(functools.partial(half_kernel, outward), [stack(REACH)] * 2 + [stack...  4.52 us
    ppermute x3, starting transfers between devices, on_device(): lax.ppermute(inner_parts[k], 'shot', shifts[k])  4.45 us
    ppermute x3, starting transfers between devices, on_device(): lax.ppermute(outer_parts[k], 'shot', shifts[k])  4.24 us
    ppermute x1, waiting for transfers between devices, on_device(): first_hop = lax.ppermute(late_out, 'space', [(3, 7), (4, 0)])  4.19 us
    ppermute x1, starting transfers between devices, on_device(): halo_late_in = lax.ppermute(late_in, 'space', in_pairs)  3.29 us
    pallas_call x1, Pallas kernels, on_device(): call(inner_kernel, [stack(2 * REACH), stack(3 * REACH)] + [stack(2 * REAC...  2.07 us
    pallas_call x1, Pallas kernels, on_device(): call(early_kernel, [stack(3 * REACH)] * 2 + [stack(REACH)] * 2, [H] * 3,...  1.65 us
  transfers between devices with their start and end apart: 12, of which 3 were waited for; matrix products, arithmetic and copies ran while one was open for 0% of the time, Pallas kernels for 20%

profile of v2, /device:TPU:0, one launch (start us, length us, event | category | flops | bytes accessed | tf_op | source)
XLA Modules:
  0.0 40.7 jit_solution(12676317113779602077)
XLA Ops:
  0.0 1.7 %shard_map.109 = (f32[12,64,256]{2,1,0:T(8,128)S(1)}, f32[12,64,256]{2,1,0:T(8,128)S(1)}, f32[4,64,256]{2,1,0:T(8,128)S(1)}, f32[4,64,256]{2,1,0:T(8,128)S(1)}) custom-call(f32[8,64,256]{2,1,0:T(8,128)} %courant.1, f32[8,64,256]{2,1,0:T(8,128)} %bitcast.11, f32[8,64,256]{2,1,0:T(8,128)} %bitcast.12), custom_call_target="tpu_custom_call" | custom-call | flops 1000000 | bytes 1000000 | tf_op jit(solution)/shard_map/pallas_call | solution.py:426
  1.7 0.5 %collective-permute-start.1 = (f32[12,64,256]{2,1,0:T(8,128)S(1)}, f32[12,64,256]{2,1,0:T(8,128)S(1)}, u32[]{:S(2)}, u32[]{:S(2)}) collective-permute-start(f32[12,64,256]{2,1,0:T(8,128)S(1)} %get-tuple-element.30.other.mine.own_in), channel_id=1, source_target_pairs={{0,1},{1,0},{2,3},{3,2},{4,5},{5,4},{6,7},{7,6},{8,9},{9,8},{10,11... | collective-permute-start | bytes 2359304 | tf_op jit(solution)/shard_map/ppermute | solution.py:435
  2.2 0.7 %collective-permute-start = (f32[12,64,256]{2,1,0:T(8,128)S(1)}, f32[12,64,256]{2,1,0:T(8,128)S(1)}, u32[]{:S(2)}, u32[]{:S(2)}) collective-permute-start(f32[12,64,256]{2,1,0:T(8,128)S(1)} %get-tuple-element.31.mine.other.own_out), channel_id=1, source_target_pairs={{1,2},{3,4},{5,6},{2,1},{4,3},{6,5},{9,10},{11,12},{13,14},{10,9},... | collective-permute-start | bytes 2359304 | tf_op jit(solution)/shard_map/ppermute | solution.py:434
  2.9 2.3 %shard_map.110 = (f32[4,64,256]{2,1,0:T(8,128)S(1)}, f32[4,64,256]{2,1,0:T(8,128)S(1)}, f32[8,64,256]{2,1,0:T(8,128)S(1)}, bf16[6,256,256]{2,1,0:T(8,128)(2,1)S(1)}) custom-call(f32[12,64,256]{2,1,0:T(8,128)S(1)} %get-tuple-element.31.mine.other.own_out, f32[12,64,256]{2,1,0:T(8,128)S(1)} %get-tuple-element.30.other.mine.own_in, ...), custom_call_target="tpu_custom_call" | custom-call | flops 10000000000 | bytes 1000000 | tf_op jit(solution)/shard_map/pallas_call | solution.py:440
  5.2 1.3 %collective-permute-start.7 = (f32[8,64,256]{2,1,0:T(8,128)S(1)}, f32[8,64,256]{2,1,0:T(8,128)S(1)}, u32[]{:S(2)}, u32[]{:S(2)}) collective-permute-start(f32[8,64,256]{2,1,0:T(8,128)S(1)} %get-tuple-element.40.late_out), channel_id=1, source_target_pairs={{3,7},{4,0},{11,15},{12,8},{19,23},{20,16},{27,31},{28,24}} | collective-permute-start | bytes 1572872 | tf_op jit(solution)/shard_map/ppermute | solution.py:451
  6.5 0.0 copy-start.2
  6.5 2.2 %shard_map.111 = (f32[4,64,256]{2,1,0:T(8,128)S(1)}, f32[4,64,256]{2,1,0:T(8,128)S(1)}, f32[8,64,256]{2,1,0:T(8,128)S(1)}) custom-call(f32[12,64,256]{2,1,0:T(8,128)S(1)} %get-tuple-element.30.other.mine.own_in, f32[12,64,256]{2,1,0:T(8,128)S(1)} %get-tuple-element.31.mine.other.own_out, f32[4,64,256]{2,1,0:T(8,128)S(1)} %get-tuple-element.34.adjoint_now.now_in, ...), custom_call_target="tpu_custom_call" | custom-call | flops 10000000000 | bytes 1000000 | tf_op jit(solution)/shard_map/pallas_call | solution.py:440
  8.7 3.3 %collective-permute-start.2 = (f32[8,64,256]{2,1,0:T(8,128)S(1)}, f32[8,64,256]{2,1,0:T(8,128)S(1)}, u32[]{:S(2)}, u32[]{:S(2)}) collective-permute-start(f32[8,64,256]{2,1,0:T(8,128)S(1)} %get-tuple-element.39.late_in), channel_id=1, source_target_pairs={{0,1},{1,0},{2,3},{3,2},{4,5},{5,4},{6,7},{7,6},{8,9},{9,8},{10,11... | collective-permute-start | bytes 1572872 | tf_op jit(solution)/shard_map/ppermute | solution.py:459
  12.0 0.7 %collective-permute-start.6 = (f32[8,64,256]{2,1,0:T(8,128)S(1)}, f32[8,64,256]{2,1,0:T(8,128)S(1)}, u32[]{:S(2)}, u32[]{:S(2)}) collective-permute-start(f32[8,64,256]{2,1,0:T(8,128)S(1)} %get-tuple-element.40.late_out), channel_id=1, source_target_pairs={{1,2},{5,6},{2,1},{6,5},{9,10},{13,14},{10,9},{14,13},{17,18},{21,... | collective-permute-start | bytes 1572872 | tf_op jit(solution)/shard_map/ppermute | solution.py:453
  14.0 0.0 copy-start.3
  14.0 0.6 %copy-done.3 = f32[1,2]{1,0:T(1,128)S(1)} copy-done((f32[1,2]{1,0:T(1,128)S(1)}, f32[1,2]{1,0:T(1,128)}, u32[]{:S(2)}) %copy-start.3) | copy-done | bytes 32
  14.7 0.1 maximum_bitcast_fusion.pulse
  14.7 4.2 %collective-permute-done.7 = f32[8,64,256]{2,1,0:T(8,128)S(1)} collective-permute-done((f32[8,64,256]{2,1,0:T(8,128)S(1)}, f32[8,64,256]{2,1,0:T(8,128)S(1)}, u32[]{:S(2)}, u32[]{:S(2)}) %collective-permute-start.7) | collective-permute-done | bytes 524320 | tf_op jit(solution)/shard_map/ppermute | solution.py:451
  18.9 1.3 %collective-permute-start.8 = (f32[8,64,256]{2,1,0:T(8,128)S(1)}, f32[8,64,256]{2,1,0:T(8,128)S(1)}, u32[]{:S(2)}, u32[]{:S(2)}) collective-permute-start(f32[8,64,256]{2,1,0:T(8,128)S(1)} %collective-permute-done.7), channel_id=1, source_target_pairs={{7,4},{0,3},{15,12},{8,11},{23,20},{16,19},{31,28},{24,27}} | collective-permute-start | bytes 1572872 | tf_op jit(solution)/shard_map/ppermute | solution.py:454
  20.3 0.0 collective-permute-done.2.halo_late
  20.3 0.0 collective-permute-done.1.halo_early
  20.3 0.0 copy-start
  20.3 0.0 copy-start.1
  20.3 0.0 copy-done.2
  20.3 0.7 %copy-done = f32[1,256,2]{1,2,0:T(2,128)S(1)} copy-done((f32[1,256,2]{1,2,0:T(2,128)S(1)}, f32[1,256,2]{1,2,0:T(2,128)}, u32[]{:S(2)}) %copy-start) | copy-done | bytes 2072
  21.0 0.0 copy-done.1
  21.0 2.1 %shard_map.112 = (f32[8,64,256]{2,1,0:T(8,128)S(1)}, f32[12,64,256]{2,1,0:T(8,128)S(1)}, f32[8,64,256]{2,1,0:T(8,128)S(1)}, f32[8,64,256]{2,1,0:T(8,128)S(1)}, f32[8,64,256]{2,1,0:T(8,128)S(1)}) custom-call(f32[1,4]{1,0:T(1,128)S(1)} %maximum_bitcast_fusion.pulse, s32[1,256]{1,0:T(1,128)S(1)} %copy-done.1, s32[1,256]{1,0:T(1,128)S(1)} %copy-done.2, ...), custom_call_target="tpu_custom_call" | custom-call | flops 1000000 | bytes 1000000 | tf_op jit(solution)/shard_map/pallas_call | solution.py:461
  23.1 0.0 collective-permute-done.halo.halo_early
  23.1 1.2 %shard_map.113 = (f32[16,64,256]{2,1,0:T(8,128)S(1)}, f32[4,16,256]{2,1,0:T(8,128)S(1)}, f32[4,16,256]{2,1,0:T(8,128)S(1)}, f32[4,16,256]{2,1,0:T(8,128)S(1)}, f32[4,16,256]{2,1,0:T(8,128)S(1)}) custom-call(f32[12,64,256]{2,1,0:T(8,128)S(1)} %get-tuple-element.30.other.mine.own_in, f32[12,64,256]{2,1,0:T(8,128)S(1)} %get-tuple-element.31.mine.other.own_out, ...), custom_call_target="tpu_custom_call" | custom-call | flops 10000000000 | bytes 1000000 | tf_op jit(solution)/shard_map/pallas_call | solution.py:492
  24.3 1.6 %collective-permute-start.3 = (f32[4,16,256]{2,1,0:T(8,128)S(1)}, f32[4,16,256]{2,1,0:T(8,128)S(1)}, u32[]{:S(2)}, u32[]{:S(2)}) collective-permute-start(f32[4,16,256]{2,1,0:T(8,128)S(1)} %get-tuple-element.46), channel_id=1, source_target_pairs={{0,8},{8,0},{16,24},{24,16},{1,9},{9,1},{17,25},{25,17},{2,10},{10... | collective-permute-start | bytes 196616 | tf_op jit(solution)/shard_map/ppermute | solution.py:502
  25.9 2.6 %collective-permute-start.4 = (f32[4,16,256]{2,1,0:T(8,128)S(1)}, f32[4,16,256]{2,1,0:T(8,128)S(1)}, u32[]{:S(2)}, u32[]{:S(2)}) collective-permute-start(f32[4,16,256]{2,1,0:T(8,128)S(1)} %get-tuple-element.47), channel_id=1, source_target_pairs={{0,16},{8,24},{16,0},{24,8},{1,17},{9,25},{17,1},{25,9},{2,18},{10... | collective-permute-start | bytes 196616 | tf_op jit(solution)/shard_map/ppermute | solution.py:502
  28.5 0.2 collective-permute-start.5
  28.7 0.0 collective-permute-done.6.rest_0_
  28.7 0.0 collective-permute-done.8.rest_1_
  28.7 0.4 %shard_map.115 = (f32[4,16,256]{2,1,0:T(8,128)S(1)}, f32[4,16,256]{2,1,0:T(8,128)S(1)}, f32[4,16,256]{2,1,0:T(8,128)S(1)}, f32[4,16,256]{2,1,0:T(8,128)S(1)}) custom-call(f32[12,64,256]{2,1,0:T(8,128)S(1)} %get-tuple-element.31.mine.other.own_out, f32[16,64,256]{2,1,0:T(8,128)S(1)} %get-tuple-element.49.outer, ...), custom_call_target="tpu_custom_call" | custom-call | flops 1000000 | bytes 1000000 | tf_op jit(solution)/shard_map/pallas_call | solution.py:507
  29.2 1.8 %collective-permute-start.10 = (f32[4,16,256]{2,1,0:T(8,128)S(1)}, f32[4,16,256]{2,1,0:T(8,128)S(1)}, u32[]{:S(2)}, u32[]{:S(2)}) collective-permute-start(f32[4,16,256]{2,1,0:T(8,128)S(1)} %get-tuple-element.53), channel_id=1, source_target_pairs={{0,16},{8,24},{16,0},{24,8},{1,17},{9,25},{17,1},{25,9},{2,18},{10... | collective-permute-start | bytes 196616 | tf_op jit(solution)/shard_map/ppermute | solution.py:516
  30.9 2.0 %collective-permute-start.11 = (f32[4,16,256]{2,1,0:T(8,128)S(1)}, f32[4,16,256]{2,1,0:T(8,128)S(1)}, u32[]{:S(2)}, u32[]{:S(2)}) collective-permute-start(f32[4,16,256]{2,1,0:T(8,128)S(1)} %get-tuple-element.54), channel_id=1, source_target_pairs={{0,24},{8,16},{16,8},{24,0},{1,25},{9,17},{17,9},{25,1},{2,26},{10... | collective-permute-start | bytes 196616 | tf_op jit(solution)/shard_map/ppermute | solution.py:516
  32.9 0.0 collective-permute-done.3.refs_1_
  32.9 0.5 %collective-permute-start.9 = (f32[4,16,256]{2,1,0:T(8,128)S(1)}, f32[4,16,256]{2,1,0:T(8,128)S(1)}, u32[]{:S(2)}, u32[]{:S(2)}) collective-permute-start(f32[4,16,256]{2,1,0:T(8,128)S(1)} %get-tuple-element.52), channel_id=1, source_target_pairs={{0,8},{8,0},{16,24},{24,16},{1,9},{9,1},{17,25},{25,17},{2,10},{10... | collective-permute-start | bytes 196616 | tf_op jit(solution)/shard_map/ppermute | solution.py:516
  33.4 0.0 collective-permute-done.4.refs_2_
  33.4 1.5 %collective-permute-done.5.refs_3_ = f32[4,16,256]{2,1,0:T(8,128)S(1)} collective-permute-done((f32[4,16,256]{2,1,0:T(8,128)S(1)}, f32[4,16,256]{2,1,0:T(8,128)S(1)}, u32[]{:S(2)}, u32[]{:S(2)}) %collective-permute-start.5) | collective-permute-done | bytes 65568 | tf_op jit(solution)/shard_map/ppermute | solution.py:502
  34.9 5.1 %collective-permute-done.10.refs_2_ = f32[4,16,256]{2,1,0:T(8,128)S(1)} collective-permute-done((f32[4,16,256]{2,1,0:T(8,128)S(1)}, f32[4,16,256]{2,1,0:T(8,128)S(1)}, u32[]{:S(2)}, u32[]{:S(2)}) %collective-permute-start.10) | collective-permute-done | bytes 65568 | tf_op jit(solution)/shard_map/ppermute | solution.py:516
  40.0 0.0 collective-permute-done.11.refs_3_
  40.0 0.0 collective-permute-done.9.refs_1_
  40.0 0.7 %shard_map.116 = f32[8,16,256]{2,1,0:T(8,128)} custom-call(f32[4,16,256]{2,1,0:T(8,128)S(1)} %shard_map.114.inner, f32[4,16,256]{2,1,0:T(8,128)S(1)} %get-tuple-element.51.refs_0_, f32[4,16,256]{2,1,0:T(8,128)S(1)} %collective-permute-done.9.refs_1_, f32[4,16,256]{2,1,0:T(8,128)S(1)} %collective-permute-done.10.refs_2_, ...), custom_call_target="tpu_custom_call" | custom-call | flops 1000000 | bytes 1000000 | tf_op jit(solution)/shard_map/pallas_call | solution.py:518
  (1 shorter events, 0.0 us)
Async XLA Ops:
  1.7 18.6 %collective-permute-start.1 = (f32[12,64,256]{2,1,0:T(8,128)S(1)}, f32[12,64,256]{2,1,0:T(8,128)S(1)}, u32[]{:S(2)}, u32[]{:S(2)}) collective-permute-start(f32[12,64,256]{2,1,0:T(8,128)S(1)} %get-tuple-element.30.other.mine.own_in), channel_id=1, source_target_pairs={{0,1},{1,0},{2,3},{3,2},{4,5},{5,4},{6,7},{7,6},{8,9},{9,8},{10,11... | collective-permute-start | bytes 2359304 | tf_op jit(solution)/shard_map/ppermute | solution.py:435
  2.2 20.9 %collective-permute-start = (f32[12,64,256]{2,1,0:T(8,128)S(1)}, f32[12,64,256]{2,1,0:T(8,128)S(1)}, u32[]{:S(2)}, u32[]{:S(2)}) collective-permute-start(f32[12,64,256]{2,1,0:T(8,128)S(1)} %get-tuple-element.31.mine.other.own_out), channel_id=1, source_target_pairs={{1,2},{3,4},{5,6},{2,1},{4,3},{6,5},{9,10},{11,12},{13,14},{10,9},... | collective-permute-start | bytes 2359304 | tf_op jit(solution)/shard_map/ppermute | solution.py:434
  5.2 13.7 %collective-permute-start.7 = (f32[8,64,256]{2,1,0:T(8,128)S(1)}, f32[8,64,256]{2,1,0:T(8,128)S(1)}, u32[]{:S(2)}, u32[]{:S(2)}) collective-permute-start(f32[8,64,256]{2,1,0:T(8,128)S(1)} %get-tuple-element.40.late_out), channel_id=1, source_target_pairs={{3,7},{4,0},{11,15},{12,8},{19,23},{20,16},{27,31},{28,24}} | collective-permute-start | bytes 1572872 | tf_op jit(solution)/shard_map/ppermute | solution.py:451
  6.5 13.8 %copy-start.2 = (s32[1,256]{1,0:T(1,128)S(1)}, s32[1,256]{1,0:T(1,128)}, u32[]{:S(2)}) copy-start(s32[1,256]{1,0:T(1,128)} %receiver_yz.1) | copy-start | bytes 3076
  8.7 11.5 %collective-permute-start.2 = (f32[8,64,256]{2,1,0:T(8,128)S(1)}, f32[8,64,256]{2,1,0:T(8,128)S(1)}, u32[]{:S(2)}, u32[]{:S(2)}) collective-permute-start(f32[8,64,256]{2,1,0:T(8,128)S(1)} %get-tuple-element.39.late_in), channel_id=1, source_target_pairs={{0,1},{1,0},{2,3},{3,2},{4,5},{5,4},{6,7},{7,6},{8,9},{9,8},{10,11... | collective-permute-start | bytes 1572872 | tf_op jit(solution)/shard_map/ppermute | solution.py:459
  12.0 16.7 %collective-permute-start.6 = (f32[8,64,256]{2,1,0:T(8,128)S(1)}, f32[8,64,256]{2,1,0:T(8,128)S(1)}, u32[]{:S(2)}, u32[]{:S(2)}) collective-permute-start(f32[8,64,256]{2,1,0:T(8,128)S(1)} %get-tuple-element.40.late_out), channel_id=1, source_target_pairs={{1,2},{5,6},{2,1},{6,5},{9,10},{13,14},{10,9},{14,13},{17,18},{21,... | collective-permute-start | bytes 1572872 | tf_op jit(solution)/shard_map/ppermute | solution.py:453
  14.0 0.7 %copy-start.3 = (f32[1,2]{1,0:T(1,128)S(1)}, f32[1,2]{1,0:T(1,128)}, u32[]{:S(2)}) copy-start(f32[1,2]{1,0:T(1,128)} %param.18) | copy-start | bytes 28
  18.9 9.8 %collective-permute-start.8 = (f32[8,64,256]{2,1,0:T(8,128)S(1)}, f32[8,64,256]{2,1,0:T(8,128)S(1)}, u32[]{:S(2)}, u32[]{:S(2)}) collective-permute-start(f32[8,64,256]{2,1,0:T(8,128)S(1)} %collective-permute-done.7), channel_id=1, source_target_pairs={{7,4},{0,3},{15,12},{8,11},{23,20},{16,19},{31,28},{24,27}} | collective-permute-start | bytes 1572872 | tf_op jit(solution)/shard_map/ppermute | solution.py:454
  20.3 0.7 %copy-start = (f32[1,256,2]{1,2,0:T(2,128)S(1)}, f32[1,256,2]{1,2,0:T(2,128)}, u32[]{:S(2)}) copy-start(f32[1,256,2]{1,2,0:T(2,128)} %param.21) | copy-start | bytes 6148
  20.3 0.7 %copy-start.1 = (s32[1,256]{1,0:T(1,128)S(1)}, s32[1,256]{1,0:T(1,128)}, u32[]{:S(2)}) copy-start(s32[1,256]{1,0:T(1,128)} %receiver_x.1) | copy-start | bytes 3076
  24.3 8.6 %collective-permute-start.3 = (f32[4,16,256]{2,1,0:T(8,128)S(1)}, f32[4,16,256]{2,1,0:T(8,128)S(1)}, u32[]{:S(2)}, u32[]{:S(2)}) collective-permute-start(f32[4,16,256]{2,1,0:T(8,128)S(1)} %get-tuple-element.46), channel_id=1, source_target_pairs={{0,8},{8,0},{16,24},{24,16},{1,9},{9,1},{17,25},{25,17},{2,10},{10... | collective-permute-start | bytes 196616 | tf_op jit(solution)/shard_map/ppermute | solution.py:502
  25.9 7.5 %collective-permute-start.4 = (f32[4,16,256]{2,1,0:T(8,128)S(1)}, f32[4,16,256]{2,1,0:T(8,128)S(1)}, u32[]{:S(2)}, u32[]{:S(2)}) collective-permute-start(f32[4,16,256]{2,1,0:T(8,128)S(1)} %get-tuple-element.47), channel_id=1, source_target_pairs={{0,16},{8,24},{16,0},{24,8},{1,17},{9,25},{17,1},{25,9},{2,18},{10... | collective-permute-start | bytes 196616 | tf_op jit(solution)/shard_map/ppermute | solution.py:502
  28.5 6.4 %collective-permute-start.5 = (f32[4,16,256]{2,1,0:T(8,128)S(1)}, f32[4,16,256]{2,1,0:T(8,128)S(1)}, u32[]{:S(2)}, u32[]{:S(2)}) collective-permute-start(f32[4,16,256]{2,1,0:T(8,128)S(1)} %get-tuple-element.48), channel_id=1, source_target_pairs={{0,24},{8,16},{16,8},{24,0},{1,25},{9,17},{17,9},{25,1},{2,26},{10... | collective-permute-start | bytes 196616 | tf_op jit(solution)/shard_map/ppermute | solution.py:502
  29.2 10.8 %collective-permute-start.10 = (f32[4,16,256]{2,1,0:T(8,128)S(1)}, f32[4,16,256]{2,1,0:T(8,128)S(1)}, u32[]{:S(2)}, u32[]{:S(2)}) collective-permute-start(f32[4,16,256]{2,1,0:T(8,128)S(1)} %get-tuple-element.53), channel_id=1, source_target_pairs={{0,16},{8,24},{16,0},{24,8},{1,17},{9,25},{17,1},{25,9},{2,18},{10... | collective-permute-start | bytes 196616 | tf_op jit(solution)/shard_map/ppermute | solution.py:516
  30.9 9.1 %collective-permute-start.11 = (f32[4,16,256]{2,1,0:T(8,128)S(1)}, f32[4,16,256]{2,1,0:T(8,128)S(1)}, u32[]{:S(2)}, u32[]{:S(2)}) collective-permute-start(f32[4,16,256]{2,1,0:T(8,128)S(1)} %get-tuple-element.54), channel_id=1, source_target_pairs={{0,24},{8,16},{16,8},{24,0},{1,25},{9,17},{17,9},{25,1},{2,26},{10... | collective-permute-start | bytes 196616 | tf_op jit(solution)/shard_map/ppermute | solution.py:516
  32.9 7.1 %collective-permute-start.9 = (f32[4,16,256]{2,1,0:T(8,128)S(1)}, f32[4,16,256]{2,1,0:T(8,128)S(1)}, u32[]{:S(2)}, u32[]{:S(2)}) collective-permute-start(f32[4,16,256]{2,1,0:T(8,128)S(1)} %get-tuple-element.52), channel_id=1, source_target_pairs={{0,8},{8,0},{16,24},{24,16},{1,9},{9,1},{17,25},{25,17},{2,10},{10... | collective-permute-start | bytes 196616 | tf_op jit(solution)/shard_map/ppermute | solution.py:516

commit v3 on v2

v3 whole, which is shorter than its diff:
```python
import functools
import jax
import jax.numpy as jnp
from jax import lax
from jax.experimental import pallas as pl
from jax.experimental.pallas import tpu as pltpu
from jax.sharding import PartitionSpec as P

MIDDLE = 3.0 * (-205.0 / 72.0)
SIDE = (8.0 / 5.0, -1.0 / 5.0, 8.0 / 315.0, -1.0 / 560.0)
REACH = 4
EARLY_SPEEDS, INNER_SPEEDS = 3, 2
INWARD_ORDER, OUTWARD_ORDER = [2, 1, 3], [1, 2, 3]
F32 = jnp.float32
BF16 = jnp.bfloat16
VMEM_LIMIT = 32 * 1024 * 1024
MIDDLE_COST = int(6 * 10**9)
SECOND_COST = int(0.001 * 10**9)
SMALL, LARGE = 10**6, 10**10


def placed(layer, outward, odd):
    layer = layer if outward else 2 * REACH - 1 - layer
    return layer + odd * (2 * REACH - 1 - 2 * layer)


def grids(size_y, size_z):
    rows = lax.broadcasted_iota(jnp.int32, (size_y, size_z), 0)
    columns = lax.broadcasted_iota(jnp.int32, (size_y, size_z), 1)
    return rows, columns


def three_parts(values):
    high = values.astype(BF16)
    rest = values - high.astype(F32)
    middle = rest.astype(BF16)
    return high, middle, (rest - middle.astype(F32)).astype(BF16)


def exact_dot(left, right):
    def dot(a, b):
        return jnp.dot(left[a], right[b], preferred_element_type=F32)

    return dot(0, 0) + (dot(0, 1) + dot(1, 0)) + (dot(1, 1) + dot(0, 2) + dot(2, 0))


def band(size, block, middle):
    rows, columns = grids(size, size)
    distance = jnp.abs(rows - columns)
    weights = jnp.where(distance == 0, middle, 0.0)
    for offset in range(1, REACH + 1):
        weights = jnp.where(distance == offset, SIDE[offset - 1], weights)
    bits = block.bit_length() - 1
    return jnp.where(jnp.right_shift(rows, bits) == jnp.right_shift(columns, bits), weights, 0.0)


def plane_laplace(layers, along_y, along_z):
    shape = (len(layers),) + layers[0].shape
    parts = three_parts(jnp.concatenate(layers, axis=0))
    return (exact_dot(parts, along_z) + exact_dot(along_y, parts)).reshape(shape)


def weighted(terms):
    total = None
    for distance in range(1, REACH + 1):
        found = [layer() for at, layer in terms if at == distance]
        if found:
            term = SIDE[distance - 1] * functools.reduce(lambda a, b: a + b, found)
            total = term if total is None else total + term
    return total


def within(at, layers):
    return weighted([(abs(at - i), lambda i=i: layers(i)) for i in range(REACH) if i != at])


def from_other(at, layers):
    last = 2 * REACH - 1
    return weighted([(last - i - at, lambda i=i: layers(i)) for i in range(REACH)])


def across(at, layers):
    return weighted([(at + 1 + i, lambda i=i: layers(i)) for i in range(REACH)])


def add(*values):
    return functools.reduce(lambda a, b: a + b, [v for v in values if v is not None])


def early_kernel(courant, now, adjoint, packet, speeds, adjoints, sems):
    odd = lax.rem(lax.axis_index("space"), 2)
    copies = []
    for layer in range(REACH):
        at = placed(layer, True, odd)
        for source, target in ((courant, speeds), (adjoint, adjoints), (now, packet)):
            copies.append(
                pltpu.make_async_copy(source.at[at], target.at[layer], sems.at[len(copies)])
            )
            copies[-1].start()
    for copy in copies:
        copy.wait()
    for layer in range(REACH):
        speed = speeds[layer]
        packet[REACH + layer] = speed * speed * adjoints[layer]
        if layer < EARLY_SPEEDS:
            packet[2 * REACH + layer] = speed


def local_kernel(
    sent_first,
    courant,
    now,
    adjoint,
    old,
    late,
    accel,
    adjoint_mid,
    speeds,
    adjoint_now,
    bands,
    early_in,
    late_out,
    late_in,
    present,
    scaled,
    late_held,
    sem,
):
    size_y, size_z = courant.shape[1:]
    odd = lax.rem(lax.axis_index("space"), 2)
    copy = pltpu.make_async_copy(late, late_held, sem)
    copy.start()
    along_y = three_parts(band(REACH * size_y, size_y, 0.0))
    along_z = three_parts(band(size_z, size_z, MIDDLE))
    for number in range(3):
        bands[number] = along_y[number]
        bands[3 + number] = along_z[number]
    places = [placed(layer, half == 0, odd) for half in range(2) for layer in range(REACH)]
    for at, place in enumerate(places):
        speed = courant[place]
        speeds[at] = speed
        adjoint_now[at] = adjoint[place]
        present[at] = now[place]
        scaled[at] = speed * speed * adjoint[place]
    copy.wait()
    for half, packet in ((0, late_out), (1, late_in)):
        mine, other = half * REACH, (1 - half) * REACH
        flat = [
            plane_laplace([layers[mine + at] for at in range(REACH)], along_y, along_z)
            for layers in (present, scaled)
        ]
        for at in range(REACH):
            place = places[mine + at]
            speed_sq = speeds[mine + at] * speeds[mine + at]
            laplace = add(
                flat[0][at],
                within(at, lambda i: present[mine + i]),
                from_other(at, lambda i: present[other + i]),
            )
            accel[mine + at] = laplace
            packet[at] = 2.0 * now[place] - old[place] + speed_sq * laplace
            laplace = add(
                flat[1][at],
                within(at, lambda i: scaled[mine + i]),
                from_other(at, lambda i: scaled[other + i]),
            )
            field = 2.0 * adjoint[place] - late_held[place] + laplace
            adjoint_mid[mine + at] = field
            packet[REACH + at] = speed_sq * field
    for layer in range(EARLY_SPEEDS, REACH):
        late_out[2 * REACH + layer - EARLY_SPEEDS] = speeds[layer]
    for layer in range(REACH):
        early_in[layer] = present[REACH + layer]
        early_in[REACH + layer] = scaled[REACH + layer]
        if layer < INNER_SPEEDS:
            early_in[2 * REACH + layer] = speeds[REACH + layer]
        else:
            late_in[2 * REACH + layer - INNER_SPEEDS] = speeds[REACH + layer]


def next_halo(at, speed, late, own, points):
    speed_sq = speed * speed
    mid = late[at] + speed_sq * (across(at, lambda i: own[i]) + points[at])
    scaled = late[REACH + at] + speed_sq * (
        across(at, lambda i: own[REACH + i]) + points[REACH + at]
    )
    return mid, scaled


def exchange_order(shots, inward):
    if shots == 4:
        return [0] + (INWARD_ORDER if inward else OUTWARD_ORDER)
    return list(range(shots))


def scatter_rows(gradient, outputs, shots, inward):
    rows = gradient.shape[1] // shots
    me = lax.axis_index("shot")
    for number, shift in enumerate(exchange_order(shots, inward)):
        first = pl.multiple_of(jnp.bitwise_xor(me, shift) * rows, rows)
        outputs[number][...] = gradient[:, pl.ds(first, rows), :]


def inner_kernel(
    pulse,
    receiver_x,
    receiver_yz,
    residual,
    own_in,
    speeds,
    accel,
    adjoint_mid,
    late_in,
    late_out,
    adjoint_now,
    bands,
    halo_early,
    halo_late,
    inner,
    outer,
    forward,
    backward,
    points_out,
    marks,
    added,
    points_in,
    mid,
    scaled,
    next_mid,
    next_scaled,
):
    slab = 2 * REACH
    space = lax.axis_index("space")
    odd = lax.rem(space, 2)
    size_y, size_z = own_in.shape[1:]
    along_y, along_z = bands[0:3], bands[3:6]
    z_bits = size_z.bit_length() - 1

    def counted(x):
        local = x - space * slab
        return REACH + local + odd * (slab - 1 - 2 * local)

    cells = receiver_yz[...]
    layer = counted(receiver_x[...])
    inside = (layer >= 0) & (layer < 2 * slab)
    wanted = jnp.where(inside, layer * size_y + jnp.right_shift(cells, z_bits), -1)
    count = wanted.shape[1]
    line = lax.broadcasted_iota(jnp.int32, (2 * slab * size_y, count), 0)
    marks[...] = jnp.where(line == wanted, 1.0, 0.0).astype(BF16)
    depth = lax.broadcasted_iota(jnp.int32, (size_z, count), 0)
    hit = depth == jnp.bitwise_and(cells, size_z - 1)

    def received(step, first, last):
        total = None
        for part in three_parts(residual[pl.ds(step, 1), :]):
            spread = jnp.where(hit, part.astype(F32), 0.0).astype(BF16)
            term = lax.dot_general(
                marks[first * size_y : last * size_y],
                spread,
                (((1,), (1,)), ((), ())),
                preferred_element_type=F32,
            )
            total = term if total is None else total + term
        return total.reshape(last - first, size_y, size_z)

    added[0 : 2 * slab] = received(0, 0, 2 * slab)
    added[2 * slab :] = received(1, REACH, REACH + slab)

    rows, columns = grids(size_y, size_z)
    cell = rows * size_z + columns
    source_layer = counted(pulse[:, 2:3].astype(jnp.int32))
    source_cell = pulse[:, 3:4].astype(jnp.int32)

    def fired(step, at):
        spot = jnp.where(source_layer == at, source_cell, -1)
        return jnp.where(cell == spot, pulse[:, step : step + 1], 0.0)

    for at in range(REACH):
        points_out[at] = fired(0, REACH - 1 - at)
        points_out[REACH + at] = added[REACH - 1 - at]
        points_in[at] = fired(0, REACH + slab + at)
        points_in[REACH + at] = added[REACH + slab + at]
        speed = speeds[at]
        fire = fired(0, REACH + at)
        outer[at] = accel[at] + fire
        outer[REACH + at] = adjoint_mid[at] + added[REACH + at]
        outer[2 * REACH + at] = late_out[at] + speed * speed * fire
    for at in range(REACH):
        if at < INNER_SPEEDS:
            speed = halo_early[2 * REACH + at]
        else:
            speed = halo_late[2 * REACH + at - INNER_SPEEDS]
        next_mid[at], next_scaled[at] = next_halo(at, speed, halo_late, own_in, points_in)
    for at in range(REACH):
        to = REACH + slab - 1 - at
        speed = speeds[REACH + at]
        speed_sq = speed * speed
        extra = across(at, lambda i: halo_early[i]) + fired(0, to)
        adjoint = adjoint_mid[REACH + at] + across(at, lambda i: halo_early[REACH + i]) + added[to]
        inner[at] = accel[REACH + at] + extra
        inner[REACH + at] = adjoint
        mid[at] = late_in[at] + speed_sq * extra
        scaled[at] = speed_sq * adjoint
    flat_mid = plane_laplace([mid[at] for at in range(REACH)], along_y, along_z)
    flat_scaled = plane_laplace([scaled[at] for at in range(REACH)], along_y, along_z)
    for at in range(REACH):
        to = REACH + at
        forward[at] = add(fired(1, to), from_other(at, lambda i: mid[i]))
        backward[at] = add(
            added[2 * slab + at] - adjoint_now[at],
            from_other(at, lambda i: scaled[i]),
        )
        to = REACH + slab - 1 - at
        forward[REACH + at] = add(
            flat_mid[at],
            fired(1, to),
            within(at, lambda i: mid[i]),
            across(at, lambda i: next_mid[i]),
        )
        backward[REACH + at] = add(
            flat_scaled[at],
            added[2 * slab + slab - 1 - at] - adjoint_now[REACH + at],
            2.0 * inner[REACH + at],
            within(at, lambda i: scaled[i]),
            across(at, lambda i: next_scaled[i]),
        )


def middle_kernel(shots, speeds, halo, inner, outer_part, forward, backward, outer, step, *rest):
    outputs, (gradient,) = rest[:shots], rest[shots:]
    for at in range(REACH):
        speed = speeds[at]
        speed_sq = speed * speed
        extra = across(at, lambda i: halo[i])
        adjoint = outer_part[REACH + at] + across(at, lambda i: halo[REACH + i])
        outer[at] = outer_part[at] + extra
        outer[REACH + at] = adjoint
        step[at] = outer_part[2 * REACH + at] + speed_sq * extra
        step[REACH + at] = speed_sq * adjoint
    for at in range(REACH):
        ahead = add(forward[REACH + at], from_other(at, lambda i: step[i]))
        back = add(backward[REACH + at], from_other(at, lambda i: step[REACH + i]))
        speed = speeds[REACH + at]
        gradient[at] = 2.0 * speed * (back * inner[at] + inner[REACH + at] * ahead)
    scatter_rows(gradient, outputs, shots, True)


def second_kernel(bands, outer, step, forward, backward, after):
    along_y, along_z = bands[0:3], bands[3:6]
    flat_mid = plane_laplace([step[at] for at in range(REACH)], along_y, along_z)
    flat_scaled = plane_laplace([step[REACH + at] for at in range(REACH)], along_y, along_z)
    for at in range(REACH):
        after[at] = add(forward[at], flat_mid[at], within(at, lambda i: step[i]))
        after[REACH + at] = add(
            backward[at],
            2.0 * outer[REACH + at],
            flat_scaled[at],
            within(at, lambda i: step[REACH + i]),
        )


def outer_kernel(shots, relayed, own_out, speeds, outer, after, halo_early, points_out, *rest):
    lates, rest = rest[: 1 + relayed], rest[1 + relayed :]
    outputs, (late, next_mid, next_scaled, gradient) = rest[:shots], rest[shots:]
    if relayed:
        for layer in range(late.shape[0]):
            late[layer] = lates[0][layer] + lates[1][layer]
    else:
        late = lates[0]
    for at in range(REACH):
        if at < EARLY_SPEEDS:
            speed = halo_early[2 * REACH + at]
        else:
            speed = late[2 * REACH + at - EARLY_SPEEDS]
        next_mid[at], next_scaled[at] = next_halo(at, speed, late, own_out, points_out)
    for at in range(REACH):
        ahead = after[at] + across(at, lambda i: next_mid[i])
        back = after[REACH + at] + across(at, lambda i: next_scaled[i])
        speed = speeds[at]
        gradient[at] = 2.0 * speed * (back * outer[at] + outer[REACH + at] * ahead)
    scatter_rows(gradient, outputs, shots, False)


def add_kernel(*refs):
    refs[-1][...] = functools.reduce(lambda a, b: a + b, [ref[...] for ref in refs[:-1]])


def sum_kernel(inner, *refs):
    outers, out = refs[:-1], refs[-1]
    odd = lax.rem(lax.axis_index("space"), 2)
    for at in range(REACH):
        out[placed(at, True, odd)] = functools.reduce(lambda a, b: a + b, [r[at] for r in outers])
        out[placed(at, False, odd)] = inner[at]


def call(kernel, shapes, in_spaces, scratch, flops, moved):
    def shape(given):
        return jax.ShapeDtypeStruct(given, F32) if isinstance(given, tuple) else given

    many = isinstance(shapes, list)
    return pl.pallas_call(
        kernel,
        out_shape=[shape(s) for s in shapes] if many else shape(shapes),
        in_specs=[pl.BlockSpec(memory_space=space) for space in in_spaces],
        out_specs=[pl.BlockSpec(memory_space=pltpu.VMEM) for _ in shapes]
        if many
        else pl.BlockSpec(memory_space=pltpu.VMEM),
        scratch_shapes=scratch,
        compiler_params=pltpu.CompilerParams(vmem_limit_bytes=VMEM_LIMIT),
        cost_estimate=pl.CostEstimate(flops=flops, bytes_accessed=moved, transcendentals=0),
    )


def both_ways(pairs):
    return pairs + [(b, a) for a, b in pairs]


def on_device(
    courant,
    field_old,
    field_now,
    adjoint_late,
    adjoint_now,
    source_x,
    source_yz,
    wavelet,
    receiver_x,
    receiver_yz,
    residual_trace,
):
    slab, size_y, size_z = courant.shape
    if slab != 2 * REACH:
        raise ValueError("unsupported slab")
    shots = lax.axis_size("shot")
    devices = lax.axis_size("space")
    plane = size_y * size_z
    part_rows = size_y // shots
    V, H = pltpu.VMEM, pltpu.HBM

    def stack(layers):
        return (layers, size_y, size_z)

    def held(layers):
        return pltpu.VMEM(stack(layers), F32)

    def in_hbm(values):
        return pltpu.with_memory_space_constraint(values, pltpu.HBM)

    out_pairs = both_ways([(i, i + 1) for i in range(1, devices - 1, 2)])
    in_pairs = [(i, i ^ 1) for i in range(devices)]
    relayed = devices == 8
    old, now, late, adjoint = (
        field[0] for field in (field_old, field_now, adjoint_late, adjoint_now)
    )
    place = [source_x.astype(F32), source_yz.astype(F32)]
    pulse = jnp.concatenate([wavelet[0]] + place).reshape(1, 4)

    early_layers = 2 * REACH + EARLY_SPEEDS
    late_layers = 3 * REACH - EARLY_SPEEDS
    early_out = call(
        early_kernel,
        stack(early_layers),
        [H] * 3,
        [held(REACH)] * 2 + [pltpu.SemaphoreType.DMA((3 * REACH,))],
        SMALL,
        SMALL,
    )(in_hbm(courant), in_hbm(now), in_hbm(adjoint))
    halo_out = lax.ppermute(early_out, "space", out_pairs)

    bands = jax.ShapeDtypeStruct((6, size_z, size_z), BF16)
    accel, adjoint_mid, speeds, adjoint_half, bands, early_in, late_out, late_in = call(
        local_kernel,
        [stack(slab)] * 4
        + [bands, stack(2 * REACH + INNER_SPEEDS), stack(late_layers)]
        + [stack(3 * REACH - INNER_SPEEDS)],
        [pl.ANY] + [V] * 4 + [H],
        [held(slab)] * 3 + [pltpu.SemaphoreType.DMA(())],
        LARGE,
        SMALL,
    )(early_out, courant, now, adjoint, old, in_hbm(late))
    halo_in = lax.ppermute(early_in, "space", in_pairs)
    halo_late_in = lax.ppermute(late_in, "space", in_pairs)
    if relayed:
        first_hop = lax.ppermute(late_out, "space", [(3, 7), (4, 0)])
        halo_lates = [lax.ppermute(late_out, "space", both_ways([(1, 2), (5, 6)]))]
    else:
        halo_lates = [lax.ppermute(late_out, "space", out_pairs)]
    inner, outer_part, forward, backward, points_out = call(
        inner_kernel,
        [stack(2 * REACH), stack(3 * REACH)] + [stack(2 * REACH)] * 3,
        [V] * 14,
        [
            pltpu.VMEM((2 * slab * size_y, receiver_x.shape[1]), BF16),
            held(3 * slab),
            held(2 * REACH),
        ]
        + [held(REACH)] * 4,
        SMALL,
        SMALL,
    )(
        pulse,
        receiver_x,
        receiver_yz,
        residual_trace[0].T,
        early_in,
        speeds,
        accel,
        adjoint_mid,
        late_in,
        late_out,
        adjoint_half,
        bands,
        halo_in,
        halo_late_in,
    )
    if relayed:
        first_hop, inner = lax.optimization_barrier((first_hop, inner))
        halo_lates.append(lax.ppermute(first_hop, "space", [(7, 4), (0, 3)]))
    outer, step, *inner_parts = call(
        functools.partial(middle_kernel, shots),
        [stack(2 * REACH)] * 2 + [(REACH, part_rows, size_z)] * shots,
        [V] * 6,
        [held(REACH)],
        MIDDLE_COST,
        SMALL,
    )(speeds, halo_out, inner, outer_part, forward, backward)
    after = call(second_kernel, stack(2 * REACH), [V] * 5, [], SECOND_COST, SMALL)(
        bands, outer, step, forward, backward
    )
    shifts = [
        [[(i, i ^ k) for i in range(shots)] for k in exchange_order(shots, inward)]
        for inward in (True, False)
    ]
    inner_parts = inner_parts[:1] + [
        lax.ppermute(inner_parts[k], "shot", shifts[0][k]) for k in range(1, shots)
    ]
    inner_sum = call(add_kernel, (REACH, part_rows, size_z), [V] * shots, [], LARGE, SMALL)(
        *inner_parts
    )
    outer_parts = call(
        functools.partial(outer_kernel, shots, relayed),
        [(REACH, part_rows, size_z)] * shots,
        [V] * (6 + len(halo_lates)),
        [held(late_layers)] + [held(REACH)] * 3,
        SMALL,
        SMALL,
    )(early_out, speeds, outer, after, halo_out, points_out, *halo_lates)
    outer_parts = list(outer_parts[:1]) + [
        lax.ppermute(outer_parts[k], "shot", shifts[1][k]) for k in range(1, shots)
    ]
    return call(sum_kernel, (slab, part_rows, size_z), [V] * (1 + shots), [], SMALL, SMALL)(
        inner_sum, *outer_parts
    )


def solution(mesh):
    field = P("shot", "space", None, None)
    specs = (
        P("space", None, None),
        field,
        field,
        field,
        field,
        P("shot"),
        P("shot"),
        P("shot", None),
        P("shot", None),
        P("shot", None),
        P("shot", None, None),
    )
    return jax.shard_map(
        on_device, mesh=mesh, in_specs=specs, out_specs=P("space", "shot", None), check_vma=False
    )
```

time: 41.1 us -> 40.6 us (0.988)
  Pallas kernels: 10.5 us -> 9.19 us
  starting transfers between devices: 16.5 us -> 17.1 us
    ppermute x10, starting transfers between devices: 11.9 us -> 15.7 us  [the longest x3 4.45 us: on_device(): lax.ppermute(inner_parts[k], 'shot', shifts[0][k])]
    ppermute x1, starting transfers between devices: 3.29 us -> 0.08 us  [on_device(): halo_late_in = lax.ppermute(late_in, 'space', in_pairs)]
    pallas_call x4, Pallas kernels: 7.37 us -> 6.01 us  [the longest x1 3.18 us: on_device(): call(local_kernel, [stack(slab)] * 4 + [bands, stack(2 * REACH + INNER_SP...]
    ppermute x1, waiting for transfers between devices: 4.19 us -> 4.96 us  [on_device(): first_hop = lax.ppermute(late_out, 'space', [(3, 7), (4, 0)])]
    ppermute x10, waiting for transfers between devices: 6.6 us -> 6.19 us  [the longest x3 4.7 us: on_device(): lax.ppermute(outer_parts[k], 'shot', shifts[1][k])]
    unnamed x8 -> x16, local copies, waits for them, and re-layouts: 1.33 us -> 1.35 us
  transfers between devices with their start and end apart: 12 -> 12, of which waited for: 3 -> 5; matrix products, arithmetic and copies ran while one was open for 0% -> 0% of each run, Pallas kernels for 20% -> 18%
where the time goes in v3:
time: 40.6 us; the launch traced here: 40.3 us
  starting transfers between devices  17.1 us (42%)
  waiting for transfers between devices  11.1 us (27%)
  Pallas kernels  9.19 us (23%)
  between operations  1.47 us (4%)
  local copies, waits for them, and re-layouts  1.35 us (3%)
    ppermute x1, waiting for transfers between devices, on_device(): first_hop = lax.ppermute(late_out, 'space', [(3, 7), (4, 0)])  4.96 us
    ppermute x3, waiting for transfers between devices, on_device(): lax.ppermute(outer_parts[k], 'shot', shifts[1][k])  4.7 us
    ppermute x3, starting transfers between devices, on_device(): lax.ppermute(inner_parts[k], 'shot', shifts[0][k])  4.45 us
    ppermute x1, starting transfers between devices, on_device(): halo_in = lax.ppermute(early_in, 'space', in_pairs)  4.33 us
    ppermute x3, starting transfers between devices, on_device(): lax.ppermute(outer_parts[k], 'shot', shifts[1][k])  4.24 us
    pallas_call x1, Pallas kernels, on_device(): call(local_kernel, [stack(slab)] * 4 + [bands, stack(2 * REACH + INNER_SP...  3.18 us
    pallas_call x1, Pallas kernels, on_device(): call(inner_kernel, [stack(2 * REACH), stack(3 * REACH)] + [stack(2 * REAC...  2.07 us
    ppermute x1, waiting for transfers between devices, on_device(): halo_lates.append(lax.ppermute(first_hop, 'space', [(7, 4), (0, 3)]))  1.47 us
  transfers between devices with their start and end apart: 12, of which 5 were waited for; matrix products, arithmetic and copies ran while one was open for 0% of the time, Pallas kernels for 18%

profile of v3, /device:TPU:0, one launch (start us, length us, event | category | flops | bytes accessed | tf_op | source)
XLA Modules:
  0.0 40.3 jit_solution(6889943511744176691)
XLA Ops:
  0.0 0.0 copy-start
  0.0 0.0 copy-start.1
  0.0 0.0 copy-start.2
  0.0 0.0 copy-start.6
  0.0 1.4 %shard_map.109.sent_first.own_out = f32[11,64,256]{2,1,0:T(8,128)S(1)} custom-call(f32[8,64,256]{2,1,0:T(8,128)} %courant.3, f32[8,64,256]{2,1,0:T(8,128)} %bitcast.10, f32[8,64,256]{2,1,0:T(8,128)} %bitcast.12), custom_call_target="tpu_custom_call" | custom-call | flops 1000000 | bytes 1000000 | tf_op jit(solution)/shard_map/pallas_call | solution.py:460
  1.5 0.7 %collective-permute-start = (f32[11,64,256]{2,1,0:T(8,128)S(1)}, f32[11,64,256]{2,1,0:T(8,128)S(1)}, u32[]{:S(2)}, u32[]{:S(2)}) collective-permute-start(f32[11,64,256]{2,1,0:T(8,128)S(1)} %shard_map.109.sent_first.own_out), channel_id=1, source_target_pairs={{1,2},{3,4},{5,6},{2,1},{4,3},{6,5},{9,10},{11,12},{13,14},{10,9},... | collective-permute-start | bytes 2162696 | tf_op jit(solution)/shard_map/ppermute | solution.py:468
  2.2 0.0 copy-done
  2.2 0.0 copy-done.1
  2.2 0.0 copy-done.2
  2.2 0.0 copy-done.6
  2.2 0.0 copy-start.5
  2.2 3.2 %shard_map.110 = (f32[8,64,256]{2,1,0:T(8,128)S(1)}, f32[8,64,256]{2,1,0:T(8,128)S(1)}, f32[8,64,256]{2,1,0:T(8,128)S(1)}, f32[8,64,256]{2,1,0:T(8,128)S(1)}, bf...) custom-call(f32[11,64,256]{2,1,0:T(8,128)S(1)} %shard_map.109.sent_f, ...), custom_call_target="tpu_custom_call" | custom-call | flops 10000000000 | bytes 1000000 | tf_op jit(solution)/shard_map/pallas_call | solution.py:471
  5.4 4.3 %collective-permute-start.2 = (f32[10,64,256]{2,1,0:T(8,128)S(1)}, f32[10,64,256]{2,1,0:T(8,128)S(1)}, u32[]{:S(2)}, u32[]{:S(2)}) collective-permute-start(f32[10,64,256]{2,1,0:T(8,128)S(1)} %get-tuple-element.32.own_in), channel_id=1, source_target_pairs={{0,1},{1,0},{2,3},{3,2},{4,5},{5,4},{6,7},{7,6},{8,9},{9,8},{10,11... | collective-permute-start | bytes 1966088 | tf_op jit(solution)/shard_map/ppermute | solution.py:481
  9.7 0.1 collective-permute-start.3
  9.8 1.3 %collective-permute-start.1 = (f32[9,64,256]{2,1,0:T(8,128)S(1)}, f32[9,64,256]{2,1,0:T(8,128)S(1)}, u32[]{:S(2)}, u32[]{:S(2)}) collective-permute-start(f32[9,64,256]{2,1,0:T(8,128)S(1)} %get-tuple-element.31.late_out), channel_id=1, source_target_pairs={{3,7},{4,0},{11,15},{12,8},{19,23},{20,16},{27,31},{28,24}} | collective-permute-start | bytes 1769480 | tf_op jit(solution)/shard_map/ppermute | solution.py:484
  11.1 0.7 %collective-permute-start.7 = (f32[9,64,256]{2,1,0:T(8,128)S(1)}, f32[9,64,256]{2,1,0:T(8,128)S(1)}, u32[]{:S(2)}, u32[]{:S(2)}) collective-permute-start(f32[9,64,256]{2,1,0:T(8,128)S(1)} %get-tuple-element.31.late_out), channel_id=1, source_target_pairs={{1,2},{5,6},{2,1},{6,5},{9,10},{13,14},{10,9},{14,13},{17,18},{21,... | collective-permute-start | bytes 1769480 | tf_op jit(solution)/shard_map/ppermute | solution.py:485
  13.1 0.0 copy-start.7
  13.1 0.6 %copy-done.7 = f32[1,2]{1,0:T(1,128)S(1)} copy-done((f32[1,2]{1,0:T(1,128)S(1)}, f32[1,2]{1,0:T(1,128)}, u32[]{:S(2)}) %copy-start.7) | copy-done | bytes 32
  13.8 0.1 maximum_bitcast_fusion.pulse
  13.8 0.0 collective-permute-done.2.halo_early
  13.9 0.0 collective-permute-done.3.halo_late
  13.9 0.0 copy-start.3
  13.9 0.0 copy-start.4
  13.9 0.0 copy-done.5
  13.9 0.7 %copy-done.3 = f32[1,256,2]{1,2,0:T(2,128)S(1)} copy-done((f32[1,256,2]{1,2,0:T(2,128)S(1)}, f32[1,256,2]{1,2,0:T(2,128)}, u32[]{:S(2)}) %copy-start.3) | copy-done | bytes 2072
  14.5 0.0 copy-done.4
  14.6 2.1 %shard_map.111 = (f32[8,64,256]{2,1,0:T(8,128)S(1)}, f32[12,64,256]{2,1,0:T(8,128)S(1)}, f32[8,64,256]{2,1,0:T(8,128)S(1)}, f32[8,64,256]{2,1,0:T(8,128)S(1)}, f32[8,64,256]{2,1,0:T(8,128)S(1)}) custom-call(f32[1,4]{1,0:T(1,128)S(1)} %maximum_bitcast_fusion.pulse, s32[1,256]{1,0:T(1,128)S(1)} %copy-done.4, s32[1,256]{1,0:T(1,128)S(1)} %copy-done.5, ...), custom_call_target="tpu_custom_call" | custom-call | flops 1000000 | bytes 1000000 | tf_op jit(solution)/shard_map/pallas_call | solution.py:488
  16.6 5.0 %collective-permute-done.1 = f32[9,64,256]{2,1,0:T(8,128)S(1)} collective-permute-done((f32[9,64,256]{2,1,0:T(8,128)S(1)}, f32[9,64,256]{2,1,0:T(8,128)S(1)}, u32[]{:S(2)}, u32[]{:S(2)}) %collective-permute-start.1) | collective-permute-done | bytes 589856 | tf_op jit(solution)/shard_map/ppermute | solution.py:484
  21.6 1.3 %collective-permute-start.8 = (f32[9,64,256]{2,1,0:T(8,128)S(1)}, f32[9,64,256]{2,1,0:T(8,128)S(1)}, u32[]{:S(2)}, u32[]{:S(2)}) collective-permute-start(f32[9,64,256]{2,1,0:T(8,128)S(1)} %collective-permute-done.1), channel_id=1, source_target_pairs={{7,4},{0,3},{15,12},{8,11},{23,20},{16,19},{31,28},{24,27}} | collective-permute-start | bytes 1769480 | tf_op jit(solution)/shard_map/ppermute | solution.py:518
  22.9 0.0 collective-permute-done.halo.halo_early
  22.9 0.4 shard_map.112
  23.3 2.7 %collective-permute-start.4 = (f32[4,16,256]{2,1,0:T(8,128)S(1)}, f32[4,16,256]{2,1,0:T(8,128)S(1)}, u32[]{:S(2)}, u32[]{:S(2)}) collective-permute-start(f32[4,16,256]{2,1,0:T(8,128)S(1)} %get-tuple-element.44), channel_id=1, source_target_pairs={{0,16},{8,24},{16,0},{24,8},{1,17},{9,25},{17,1},{25,9},{2,18},{10... | collective-permute-start | bytes 196616 | tf_op jit(solution)/shard_map/ppermute | solution.py:535
  26.0 1.6 %collective-permute-start.5 = (f32[4,16,256]{2,1,0:T(8,128)S(1)}, f32[4,16,256]{2,1,0:T(8,128)S(1)}, u32[]{:S(2)}, u32[]{:S(2)}) collective-permute-start(f32[4,16,256]{2,1,0:T(8,128)S(1)} %get-tuple-element.45), channel_id=1, source_target_pairs={{0,8},{8,0},{16,24},{24,16},{1,9},{9,1},{17,25},{25,17},{2,10},{10... | collective-permute-start | bytes 196616 | tf_op jit(solution)/shard_map/ppermute | solution.py:535
  27.5 0.2 collective-permute-start.6
  27.8 1.0 %shard_map.114.after = f32[8,64,256]{2,1,0:T(8,128)S(1)} custom-call(bf16[6,256,256]{2,1,0:T(8,128)(2,1)S(1)} %get-tuple-element.37.bands, f32[8,64,256]{2,1,0:T(8,128)S(1)} %get-tuple-element.47.outer, f32[8,64,256]{2,1,0:T(8,128)S(1)} %get-tuple-element.48.step, f32[8,64,256]{2,1,0:T(8,128)S(1)} %get-tuple-element.41.forward, ...), custom_call_target="tpu_custom_call" | custom-call | flops 1000000 | bytes 1000000 | tf_op jit(solution)/shard_map/pallas_call | solution.py:527
  28.8 0.0 collective-permute-done.7.rest_0_
  28.8 1.5 %collective-permute-done.8.rest_1_ = f32[9,64,256]{2,1,0:T(8,128)S(1)} collective-permute-done((f32[9,64,256]{2,1,0:T(8,128)S(1)}, f32[9,64,256]{2,1,0:T(8,128)S(1)}, u32[]{:S(2)}, u32[]{:S(2)}) %collective-permute-start.8) | collective-permute-done | bytes 589856 | tf_op jit(solution)/shard_map/ppermute | solution.py:518
  30.3 0.4 %shard_map.115 = (f32[4,16,256]{2,1,0:T(8,128)S(1)}, f32[4,16,256]{2,1,0:T(8,128)S(1)}, f32[4,16,256]{2,1,0:T(8,128)S(1)}, f32[4,16,256]{2,1,0:T(8,128)S(1)}) custom-call(f32[11,64,256]{2,1,0:T(8,128)S(1)} %shard_map.109.sent_first.own_out, f32[8,64,256]{2,1,0:T(8,128)S(1)} %get-tuple-element.30.speeds, f32[8,64,256]{2,1,0:T(8,128)S(1)} %get-tuple-element.47.outer, ...), custom_call_target="tpu_custom_call" | custom-call | flops 1000000 | bytes 1000000 | tf_op jit(solution)/shard_map/pallas_call | solution.py:540
  30.7 2.7 %collective-permute-start.10 = (f32[4,16,256]{2,1,0:T(8,128)S(1)}, f32[4,16,256]{2,1,0:T(8,128)S(1)}, u32[]{:S(2)}, u32[]{:S(2)}) collective-permute-start(f32[4,16,256]{2,1,0:T(8,128)S(1)} %get-tuple-element.53), channel_id=1, source_target_pairs={{0,16},{8,24},{16,0},{24,8},{1,17},{9,25},{17,1},{25,9},{2,18},{10... | collective-permute-start | bytes 196616 | tf_op jit(solution)/shard_map/ppermute | solution.py:549
  33.3 1.3 %collective-permute-start.11 = (f32[4,16,256]{2,1,0:T(8,128)S(1)}, f32[4,16,256]{2,1,0:T(8,128)S(1)}, u32[]{:S(2)}, u32[]{:S(2)}) collective-permute-start(f32[4,16,256]{2,1,0:T(8,128)S(1)} %get-tuple-element.54), channel_id=1, source_target_pairs={{0,24},{8,16},{16,8},{24,0},{1,25},{9,17},{17,9},{25,1},{2,26},{10... | collective-permute-start | bytes 196616 | tf_op jit(solution)/shard_map/ppermute | solution.py:549
  34.7 0.0 collective-permute-done.4.refs_1_
  34.7 0.2 collective-permute-start.9
  34.9 0.0 collective-permute-done.5.refs_2_
  34.9 0.0 collective-permute-done.6.refs_3_
  35.0 1.2 %collective-permute-done.10.refs_2_ = f32[4,16,256]{2,1,0:T(8,128)S(1)} collective-permute-done((f32[4,16,256]{2,1,0:T(8,128)S(1)}, f32[4,16,256]{2,1,0:T(8,128)S(1)}, u32[]{:S(2)}, u32[]{:S(2)}) %collective-permute-start.10) | collective-permute-done | bytes 65568 | tf_op jit(solution)/shard_map/ppermute | solution.py:549
  36.1 3.4 %collective-permute-done.11.refs_3_ = f32[4,16,256]{2,1,0:T(8,128)S(1)} collective-permute-done((f32[4,16,256]{2,1,0:T(8,128)S(1)}, f32[4,16,256]{2,1,0:T(8,128)S(1)}, u32[]{:S(2)}, u32[]{:S(2)}) %collective-permute-start.11) | collective-permute-done | bytes 65568 | tf_op jit(solution)/shard_map/ppermute | solution.py:549
  39.6 0.1 collective-permute-done.9.refs_1_
  39.7 0.7 %shard_map.116 = f32[8,16,256]{2,1,0:T(8,128)} custom-call(f32[4,16,256]{2,1,0:T(8,128)S(1)} %shard_map.113.inner, f32[4,16,256]{2,1,0:T(8,128)S(1)} %get-tuple-element.51.refs_0_, f32[4,16,256]{2,1,0:T(8,128)S(1)} %collective-permute-done.9.refs_1_, f32[4,16,256]{2,1,0:T(8,128)S(1)} %collective-permute-done.10.refs_2_, ...), custom_call_target="tpu_custom_call" | custom-call | flops 1000000 | bytes 1000000 | tf_op jit(solution)/shard_map/pallas_call | solution.py:551
  (1 shorter events, 0.0 us)
Async XLA Ops:
  0.0 2.2 %copy-start = (f32[8,64,256]{2,1,0:T(8,128)S(1)}, f32[8,64,256]{2,1,0:T(8,128)}, u32[]{:S(2)}) copy-start(f32[8,64,256]{2,1,0:T(8,128)} %courant.3) | copy-start | bytes 1572868
  0.0 2.2 %copy-start.1 = (f32[1,8,64,256]{3,2,1,0:T(8,128)S(1)}, f32[1,8,64,256]{3,2,1,0:T(8,128)}, u32[]{:S(2)}) copy-start(f32[1,8,64,256]{3,2,1,0:T(8,128)} %param.13) | copy-start | bytes 1572868
  0.0 2.2 %copy-start.2 = (f32[1,8,64,256]{3,2,1,0:T(8,128)S(1)}, f32[1,8,64,256]{3,2,1,0:T(8,128)}, u32[]{:S(2)}) copy-start(f32[1,8,64,256]{3,2,1,0:T(8,128)} %param.15) | copy-start | bytes 1572868
  0.0 2.2 %copy-start.6 = (f32[1,8,64,256]{3,2,1,0:T(8,128)S(1)}, f32[1,8,64,256]{3,2,1,0:T(8,128)}, u32[]{:S(2)}) copy-start(f32[1,8,64,256]{3,2,1,0:T(8,128)} %param.12) | copy-start | bytes 1572868
  1.5 21.5 %collective-permute-start = (f32[11,64,256]{2,1,0:T(8,128)S(1)}, f32[11,64,256]{2,1,0:T(8,128)S(1)}, u32[]{:S(2)}, u32[]{:S(2)}) collective-permute-start(f32[11,64,256]{2,1,0:T(8,128)S(1)} %shard_map.109.sent_first.own_out), channel_id=1, source_target_pairs={{1,2},{3,4},{5,6},{2,1},{4,3},{6,5},{9,10},{11,12},{13,14},{10,9},... | collective-permute-start | bytes 2162696 | tf_op jit(solution)/shard_map/ppermute | solution.py:468
  2.2 11.7 %copy-start.5 = (s32[1,256]{1,0:T(1,128)S(1)}, s32[1,256]{1,0:T(1,128)}, u32[]{:S(2)}) copy-start(s32[1,256]{1,0:T(1,128)} %receiver_yz.1) | copy-start | bytes 3076
  5.4 8.4 %collective-permute-start.2 = (f32[10,64,256]{2,1,0:T(8,128)S(1)}, f32[10,64,256]{2,1,0:T(8,128)S(1)}, u32[]{:S(2)}, u32[]{:S(2)}) collective-permute-start(f32[10,64,256]{2,1,0:T(8,128)S(1)} %get-tuple-element.32.own_in), channel_id=1, source_target_pairs={{0,1},{1,0},{2,3},{3,2},{4,5},{5,4},{6,7},{7,6},{8,9},{9,8},{10,11... | collective-permute-start | bytes 1966088 | tf_op jit(solution)/shard_map/ppermute | solution.py:481
  9.7 4.1 %collective-permute-start.3 = (f32[10,64,256]{2,1,0:T(8,128)S(1)}, f32[10,64,256]{2,1,0:T(8,128)S(1)}, u32[]{:S(2)}, u32[]{:S(2)}) collective-permute-start(f32[10,64,256]{2,1,0:T(8,128)S(1)} %get-tuple-element.35.late_in), channel_id=1, source_target_pairs={{0,1},{1,0},{2,3},{3,2},{4,5},{5,4},{6,7},{7,6},{8,9},{9,8},{10,11... | collective-permute-start | bytes 1966088 | tf_op jit(solution)/shard_map/ppermute | solution.py:482
  9.8 11.8 %collective-permute-start.1 = (f32[9,64,256]{2,1,0:T(8,128)S(1)}, f32[9,64,256]{2,1,0:T(8,128)S(1)}, u32[]{:S(2)}, u32[]{:S(2)}) collective-permute-start(f32[9,64,256]{2,1,0:T(8,128)S(1)} %get-tuple-element.31.late_out), channel_id=1, source_target_pairs={{3,7},{4,0},{11,15},{12,8},{19,23},{20,16},{27,31},{28,24}} | collective-permute-start | bytes 1769480 | tf_op jit(solution)/shard_map/ppermute | solution.py:484
  11.1 17.7 %collective-permute-start.7 = (f32[9,64,256]{2,1,0:T(8,128)S(1)}, f32[9,64,256]{2,1,0:T(8,128)S(1)}, u32[]{:S(2)}, u32[]{:S(2)}) collective-permute-start(f32[9,64,256]{2,1,0:T(8,128)S(1)} %get-tuple-element.31.late_out), channel_id=1, source_target_pairs={{1,2},{5,6},{2,1},{6,5},{9,10},{13,14},{10,9},{14,13},{17,18},{21,... | collective-permute-start | bytes 1769480 | tf_op jit(solution)/shard_map/ppermute | solution.py:485
  13.1 0.7 %copy-start.7 = (f32[1,2]{1,0:T(1,128)S(1)}, f32[1,2]{1,0:T(1,128)}, u32[]{:S(2)}) copy-start(f32[1,2]{1,0:T(1,128)} %param.18) | copy-start | bytes 28
  13.9 0.7 %copy-start.3 = (f32[1,256,2]{1,2,0:T(2,128)S(1)}, f32[1,256,2]{1,2,0:T(2,128)}, u32[]{:S(2)}) copy-start(f32[1,256,2]{1,2,0:T(2,128)} %param.21) | copy-start | bytes 6148
  13.9 0.7 %copy-start.4 = (s32[1,256]{1,0:T(1,128)S(1)}, s32[1,256]{1,0:T(1,128)}, u32[]{:S(2)}) copy-start(s32[1,256]{1,0:T(1,128)} %receiver_x.1) | copy-start | bytes 3076
  21.6 8.7 %collective-permute-start.8 = (f32[9,64,256]{2,1,0:T(8,128)S(1)}, f32[9,64,256]{2,1,0:T(8,128)S(1)}, u32[]{:S(2)}, u32[]{:S(2)}) collective-permute-start(f32[9,64,256]{2,1,0:T(8,128)S(1)} %collective-permute-done.1), channel_id=1, source_target_pairs={{7,4},{0,3},{15,12},{8,11},{23,20},{16,19},{31,28},{24,27}} | collective-permute-start | bytes 1769480 | tf_op jit(solution)/shard_map/ppermute | solution.py:518
  23.3 11.4 %collective-permute-start.4 = (f32[4,16,256]{2,1,0:T(8,128)S(1)}, f32[4,16,256]{2,1,0:T(8,128)S(1)}, u32[]{:S(2)}, u32[]{:S(2)}) collective-permute-start(f32[4,16,256]{2,1,0:T(8,128)S(1)} %get-tuple-element.44), channel_id=1, source_target_pairs={{0,16},{8,24},{16,0},{24,8},{1,17},{9,25},{17,1},{25,9},{2,18},{10... | collective-permute-start | bytes 196616 | tf_op jit(solution)/shard_map/ppermute | solution.py:535
  26.0 9.0 %collective-permute-start.5 = (f32[4,16,256]{2,1,0:T(8,128)S(1)}, f32[4,16,256]{2,1,0:T(8,128)S(1)}, u32[]{:S(2)}, u32[]{:S(2)}) collective-permute-start(f32[4,16,256]{2,1,0:T(8,128)S(1)} %get-tuple-element.45), channel_id=1, source_target_pairs={{0,8},{8,0},{16,24},{24,16},{1,9},{9,1},{17,25},{25,17},{2,10},{10... | collective-permute-start | bytes 196616 | tf_op jit(solution)/shard_map/ppermute | solution.py:535
  27.5 7.4 %collective-permute-start.6 = (f32[4,16,256]{2,1,0:T(8,128)S(1)}, f32[4,16,256]{2,1,0:T(8,128)S(1)}, u32[]{:S(2)}, u32[]{:S(2)}) collective-permute-start(f32[4,16,256]{2,1,0:T(8,128)S(1)} %get-tuple-element.46), channel_id=1, source_target_pairs={{0,24},{8,16},{16,8},{24,0},{1,25},{9,17},{17,9},{25,1},{2,26},{10... | collective-permute-start | bytes 196616 | tf_op jit(solution)/shard_map/ppermute | solution.py:535
  30.7 5.5 %collective-permute-start.10 = (f32[4,16,256]{2,1,0:T(8,128)S(1)}, f32[4,16,256]{2,1,0:T(8,128)S(1)}, u32[]{:S(2)}, u32[]{:S(2)}) collective-permute-start(f32[4,16,256]{2,1,0:T(8,128)S(1)} %get-tuple-element.53), channel_id=1, source_target_pairs={{0,16},{8,24},{16,0},{24,8},{1,17},{9,25},{17,1},{25,9},{2,18},{10... | collective-permute-start | bytes 196616 | tf_op jit(solution)/shard_map/ppermute | solution.py:549
  33.3 6.2 %collective-permute-start.11 = (f32[4,16,256]{2,1,0:T(8,128)S(1)}, f32[4,16,256]{2,1,0:T(8,128)S(1)}, u32[]{:S(2)}, u32[]{:S(2)}) collective-permute-start(f32[4,16,256]{2,1,0:T(8,128)S(1)} %get-tuple-element.54), channel_id=1, source_target_pairs={{0,24},{8,16},{16,8},{24,0},{1,25},{9,17},{17,9},{25,1},{2,26},{10... | collective-permute-start | bytes 196616 | tf_op jit(solution)/shard_map/ppermute | solution.py:549
  34.7 5.0 %collective-permute-start.9 = (f32[4,16,256]{2,1,0:T(8,128)S(1)}, f32[4,16,256]{2,1,0:T(8,128)S(1)}, u32[]{:S(2)}, u32[]{:S(2)}) collective-permute-start(f32[4,16,256]{2,1,0:T(8,128)S(1)} %get-tuple-element.52), channel_id=1, source_target_pairs={{0,8},{8,0},{16,24},{24,16},{1,9},{9,1},{17,25},{25,17},{2,10},{10... | collective-permute-start | bytes 196616 | tf_op jit(solution)/shard_map/ppermute | solution.py:549

commit v4 on v3

--- a/solution.py
+++ b/solution.py
@@ -9,6 +9,8 @@
 MIDDLE = 3.0 * (-205.0 / 72.0)
 SIDE = (8.0 / 5.0, -1.0 / 5.0, 8.0 / 315.0, -1.0 / 560.0)
 REACH = 4
+SCALE = 5040.0
+WHOLE_SIDE = (8064.0, -1008.0, 128.0, -9.0)
 EARLY_SPEEDS, INNER_SPEEDS = 3, 2
 INWARD_ORDER, OUTWARD_ORDER = [2, 1, 3], [1, 2, 3]
 F32 = jnp.float32
@@ -37,27 +39,26 @@
     return high, middle, (rest - middle.astype(F32)).astype(BF16)
 
 
-def exact_dot(left, right):
-    def dot(a, b):
-        return jnp.dot(left[a], right[b], preferred_element_type=F32)
-
-    return dot(0, 0) + (dot(0, 1) + dot(1, 0)) + (dot(1, 1) + dot(0, 2) + dot(2, 0))
-
-
-def band(size, block, middle):
+def band(size, block):
     rows, columns = grids(size, size)
     distance = jnp.abs(rows - columns)
-    weights = jnp.where(distance == 0, middle, 0.0)
+    weights = jnp.zeros((size, size), F32)
     for offset in range(1, REACH + 1):
-        weights = jnp.where(distance == offset, SIDE[offset - 1], weights)
+        weights = jnp.where(distance == offset, WHOLE_SIDE[offset - 1], weights)
     bits = block.bit_length() - 1
-    return jnp.where(jnp.right_shift(rows, bits) == jnp.right_shift(columns, bits), weights, 0.0)
+    same = jnp.right_shift(rows, bits) == jnp.right_shift(columns, bits)
+    return jnp.where(same, weights, 0.0).astype(BF16)
 
 
 def plane_laplace(layers, along_y, along_z):
     shape = (len(layers),) + layers[0].shape
-    parts = three_parts(jnp.concatenate(layers, axis=0))
-    return (exact_dot(parts, along_z) + exact_dot(along_y, parts)).reshape(shape)
+    values = jnp.concatenate(layers, axis=0)
+    total = None
+    for part in three_parts(values)[::-1]:
+        term = jnp.dot(part, along_z, preferred_element_type=F32)
+        term += jnp.dot(along_y, part, preferred_element_type=F32)
+        total = term if total is None else total + term
+    return (total * (1.0 / SCALE) + MIDDLE * values).reshape(shape)
 
 
 def weighted(terms):
@@ -87,21 +88,22 @@
     return functools.reduce(lambda a, b: a + b, [v for v in values if v is not None])
 
 
-def early_kernel(courant, now, adjoint, packet, speeds, adjoints, sems):
+def early_kernel(courant, now, adjoint, packet, speeds, fields, adjoints, sems):
     odd = lax.rem(lax.axis_index("space"), 2)
-    copies = []
-    for layer in range(REACH):
-        at = placed(layer, True, odd)
-        for source, target in ((courant, speeds), (adjoint, adjoints), (now, packet)):
-            copies.append(
-                pltpu.make_async_copy(source.at[at], target.at[layer], sems.at[len(copies)])
-            )
-            copies[-1].start()
+    pairs = ((courant, speeds), (adjoint, adjoints), (now, fields))
+    copies = [
+        pltpu.make_async_copy(source.at[pl.ds(odd * REACH, REACH)], target, sems.at[number])
+        for number, (source, target) in enumerate(pairs)
+    ]
+    for copy in copies:
+        copy.start()
     for copy in copies:
         copy.wait()
     for layer in range(REACH):
-        speed = speeds[layer]
-        packet[REACH + layer] = speed * speed * adjoints[layer]
+        at = layer + odd * (REACH - 1 - 2 * layer)
+        speed = speeds[at]
+        packet[layer] = fields[at]
+        packet[REACH + layer] = speed * speed * adjoints[at]
         if layer < EARLY_SPEEDS:
             packet[2 * REACH + layer] = speed
 
@@ -130,11 +132,9 @@
     odd = lax.rem(lax.axis_index("space"), 2)
     copy = pltpu.make_async_copy(late, late_held, sem)
     copy.start()
-    along_y = three_parts(band(REACH * size_y, size_y, 0.0))
-    along_z = three_parts(band(size_z, size_z, MIDDLE))
-    for number in range(3):
-        bands[number] = along_y[number]
-        bands[3 + number] = along_z[number]
+    along_y, along_z = band(REACH * size_y, size_y), band(size_z, size_z)
+    bands[0] = along_y
+    bands[1] = along_z
     places = [placed(layer, half == 0, odd) for half in range(2) for layer in range(REACH)]
     for at, place in enumerate(places):
         speed = courant[place]
@@ -142,13 +142,14 @@
         adjoint_now[at] = adjoint[place]
         present[at] = now[place]
         scaled[at] = speed * speed * adjoint[place]
-    copy.wait()
-    for half, packet in ((0, late_out), (1, late_in)):
-        mine, other = half * REACH, (1 - half) * REACH
+    for mine, packet in ((0, late_out), (REACH, late_in)):
+        other = REACH - mine
         flat = [
             plane_laplace([layers[mine + at] for at in range(REACH)], along_y, along_z)
             for layers in (present, scaled)
         ]
+        if mine == 0:
+            copy.wait()
         for at in range(REACH):
             place = places[mine + at]
             speed_sq = speeds[mine + at] * speeds[mine + at]
@@ -233,7 +234,7 @@
     space = lax.axis_index("space")
     odd = lax.rem(space, 2)
     size_y, size_z = own_in.shape[1:]
-    along_y, along_z = bands[0:3], bands[3:6]
+    along_y, along_z = bands[0], bands[1]
     z_bits = size_z.bit_length() - 1
 
     def counted(x):
@@ -346,7 +347,7 @@
 
 
 def second_kernel(bands, outer, step, forward, backward, after):
-    along_y, along_z = bands[0:3], bands[3:6]
+    along_y, along_z = bands[0], bands[1]
     flat_mid = plane_laplace([step[at] for at in range(REACH)], along_y, along_z)
     flat_scaled = plane_laplace([step[REACH + at] for at in range(REACH)], along_y, along_z)
     for at in range(REACH):
@@ -461,13 +462,13 @@
         early_kernel,
         stack(early_layers),
         [H] * 3,
-        [held(REACH)] * 2 + [pltpu.SemaphoreType.DMA((3 * REACH,))],
+        [held(REACH)] * 3 + [pltpu.SemaphoreType.DMA((3,))],
         SMALL,
         SMALL,
     )(in_hbm(courant), in_hbm(now), in_hbm(adjoint))
     halo_out = lax.ppermute(early_out, "space", out_pairs)
 
-    bands = jax.ShapeDtypeStruct((6, size_z, size_z), BF16)
+    bands = jax.ShapeDtypeStruct((2, size_z, size_z), BF16)
     accel, adjoint_mid, speeds, adjoint_half, bands, early_in, late_out, late_in = call(
         local_kernel,
         [stack(slab)] * 4

time: 40.6 us -> 40.3 us (level)
  Pallas kernels: 9.19 us -> 7.76 us
  waiting for transfers between devices: 11.1 us -> 12.2 us
    pallas_call x1, Pallas kernels: 3.18 us -> 2.55 us  [on_device(): call(local_kernel, [stack(slab)] * 4 + [bands, stack(2 * REACH + INNER_SP...]
    ppermute x1, waiting for transfers between devices: 4.96 us -> 5.38 us  [on_device(): first_hop = lax.ppermute(late_out, 'space', [(3, 7), (4, 0)])]
    pallas_call x1, Pallas kernels: 2.07 us -> 1.65 us  [on_device(): call(inner_kernel, [stack(2 * REACH), stack(3 * REACH)] + [stack(2 * REAC...]
  transfers between devices with their start and end apart: 12 -> 12, of which waited for: 5 -> 5; matrix products, arithmetic and copies ran while one was open for 0% -> 0% of each run, Pallas kernels for 18% -> 14%
where the time goes in v4:
time: 40.3 us; the launch traced here: 40 us
  starting transfers between devices  17.1 us (42%)
  waiting for transfers between devices  12.2 us (30%)
  Pallas kernels  7.76 us (19%)
  between operations  1.47 us (4%)
  local copies, waits for them, and re-layouts  1.35 us (3%)
    ppermute x1, waiting for transfers between devices, on_device(): first_hop = lax.ppermute(late_out, 'space', [(3, 7), (4, 0)])  5.38 us
    ppermute x3, waiting for transfers between devices, on_device(): lax.ppermute(outer_parts[k], 'shot', shifts[1][k])  5.1 us
    ppermute x3, starting transfers between devices, on_device(): lax.ppermute(inner_parts[k], 'shot', shifts[0][k])  4.45 us
    ppermute x1, starting transfers between devices, on_device(): halo_in = lax.ppermute(early_in, 'space', in_pairs)  4.34 us
    ppermute x3, starting transfers between devices, on_device(): lax.ppermute(outer_parts[k], 'shot', shifts[1][k])  4.24 us
    pallas_call x1, Pallas kernels, on_device(): call(local_kernel, [stack(slab)] * 4 + [bands, stack(2 * REACH + INNER_SP...  2.55 us
    ppermute x1, waiting for transfers between devices, on_device(): halo_lates.append(lax.ppermute(first_hop, 'space', [(7, 4), (0, 3)]))  1.75 us
    pallas_call x1, Pallas kernels, on_device(): call(inner_kernel, [stack(2 * REACH), stack(3 * REACH)] + [stack(2 * REAC...  1.65 us
  transfers between devices with their start and end apart: 12, of which 5 were waited for; matrix products, arithmetic and copies ran while one was open for 0% of the time, Pallas kernels for 14%

profile of v4, /device:TPU:0, one launch (start us, length us, event | category | flops | bytes accessed | tf_op | source)
XLA Modules:
  0.0 40.0 jit_solution(12876735483954126823)
XLA Ops:
  0.0 0.0 copy-start
  0.0 0.0 copy-start.1
  0.0 0.0 copy-start.2
  0.0 0.0 copy-start.6
  0.0 1.3 %shard_map.109.sent_first.own_out = f32[11,64,256]{2,1,0:T(8,128)S(1)} custom-call(f32[8,64,256]{2,1,0:T(8,128)} %courant.3, f32[8,64,256]{2,1,0:T(8,128)} %bitcast.10, f32[8,64,256]{2,1,0:T(8,128)} %bitcast.12), custom_call_target="tpu_custom_call" | custom-call | flops 1000000 | bytes 1000000 | tf_op jit(solution)/shard_map/pallas_call | solution.py:461
  1.4 0.7 %collective-permute-start = (f32[11,64,256]{2,1,0:T(8,128)S(1)}, f32[11,64,256]{2,1,0:T(8,128)S(1)}, u32[]{:S(2)}, u32[]{:S(2)}) collective-permute-start(f32[11,64,256]{2,1,0:T(8,128)S(1)} %shard_map.109.sent_first.own_out), channel_id=1, source_target_pairs={{1,2},{3,4},{5,6},{2,1},{4,3},{6,5},{9,10},{11,12},{13,14},{10,9},... | collective-permute-start | bytes 2162696 | tf_op jit(solution)/shard_map/ppermute | solution.py:469
  2.1 0.0 copy-done
  2.1 0.0 copy-done.1
  2.1 0.0 copy-done.2
  2.1 0.0 copy-done.6
  2.1 0.0 copy-start.5
  2.1 2.6 %shard_map.110 = (f32[8,64,256]{2,1,0:T(8,128)S(1)}, f32[8,64,256]{2,1,0:T(8,128)S(1)}, f32[8,64,256]{2,1,0:T(8,128)S(1)}, f32[8,64,256]{2,1,0:T(8,128)S(1)}, bf...) custom-call(f32[11,64,256]{2,1,0:T(8,128)S(1)} %shard_map.109.sent_f, ...), custom_call_target="tpu_custom_call" | custom-call | flops 10000000000 | bytes 1000000 | tf_op jit(solution)/shard_map/pallas_call | solution.py:472
  4.7 4.3 %collective-permute-start.2 = (f32[10,64,256]{2,1,0:T(8,128)S(1)}, f32[10,64,256]{2,1,0:T(8,128)S(1)}, u32[]{:S(2)}, u32[]{:S(2)}) collective-permute-start(f32[10,64,256]{2,1,0:T(8,128)S(1)} %get-tuple-element.32.own_in), channel_id=1, source_target_pairs={{0,1},{1,0},{2,3},{3,2},{4,5},{5,4},{6,7},{7,6},{8,9},{9,8},{10,11... | collective-permute-start | bytes 1966088 | tf_op jit(solution)/shard_map/ppermute | solution.py:482
  9.0 0.1 collective-permute-start.3
  9.1 1.3 %collective-permute-start.1 = (f32[9,64,256]{2,1,0:T(8,128)S(1)}, f32[9,64,256]{2,1,0:T(8,128)S(1)}, u32[]{:S(2)}, u32[]{:S(2)}) collective-permute-start(f32[9,64,256]{2,1,0:T(8,128)S(1)} %get-tuple-element.31.late_out), channel_id=1, source_target_pairs={{3,7},{4,0},{11,15},{12,8},{19,23},{20,16},{27,31},{28,24}} | collective-permute-start | bytes 1769480 | tf_op jit(solution)/shard_map/ppermute | solution.py:485
  10.4 0.7 %collective-permute-start.7 = (f32[9,64,256]{2,1,0:T(8,128)S(1)}, f32[9,64,256]{2,1,0:T(8,128)S(1)}, u32[]{:S(2)}, u32[]{:S(2)}) collective-permute-start(f32[9,64,256]{2,1,0:T(8,128)S(1)} %get-tuple-element.31.late_out), channel_id=1, source_target_pairs={{1,2},{5,6},{2,1},{6,5},{9,10},{13,14},{10,9},{14,13},{17,18},{21,... | collective-permute-start | bytes 1769480 | tf_op jit(solution)/shard_map/ppermute | solution.py:486
  12.4 0.0 copy-start.7
  12.4 0.6 %copy-done.7 = f32[1,2]{1,0:T(1,128)S(1)} copy-done((f32[1,2]{1,0:T(1,128)S(1)}, f32[1,2]{1,0:T(1,128)}, u32[]{:S(2)}) %copy-start.7) | copy-done | bytes 32
  13.0 0.1 maximum_bitcast_fusion.pulse
  13.1 0.0 collective-permute-done.2.halo_early
  13.1 0.0 collective-permute-done.3.halo_late
  13.1 0.0 copy-start.3
  13.1 0.0 copy-start.4
  13.1 0.0 copy-done.5
  13.2 0.7 %copy-done.3 = f32[1,256,2]{1,2,0:T(2,128)S(1)} copy-done((f32[1,256,2]{1,2,0:T(2,128)S(1)}, f32[1,256,2]{1,2,0:T(2,128)}, u32[]{:S(2)}) %copy-start.3) | copy-done | bytes 2072
  13.8 0.0 copy-done.4
  13.8 1.6 %shard_map.111 = (f32[8,64,256]{2,1,0:T(8,128)S(1)}, f32[12,64,256]{2,1,0:T(8,128)S(1)}, f32[8,64,256]{2,1,0:T(8,128)S(1)}, f32[8,64,256]{2,1,0:T(8,128)S(1)}, f32[8,64,256]{2,1,0:T(8,128)S(1)}) custom-call(f32[1,4]{1,0:T(1,128)S(1)} %maximum_bitcast_fusion.pulse, s32[1,256]{1,0:T(1,128)S(1)} %copy-done.4, s32[1,256]{1,0:T(1,128)S(1)} %copy-done.5, ...), custom_call_target="tpu_custom_call" | custom-call | flops 1000000 | bytes 1000000 | tf_op jit(solution)/shard_map/pallas_call | solution.py:489
  15.5 5.4 %collective-permute-done.1 = f32[9,64,256]{2,1,0:T(8,128)S(1)} collective-permute-done((f32[9,64,256]{2,1,0:T(8,128)S(1)}, f32[9,64,256]{2,1,0:T(8,128)S(1)}, u32[]{:S(2)}, u32[]{:S(2)}) %collective-permute-start.1) | collective-permute-done | bytes 589856 | tf_op jit(solution)/shard_map/ppermute | solution.py:485
  20.9 1.3 %collective-permute-start.8 = (f32[9,64,256]{2,1,0:T(8,128)S(1)}, f32[9,64,256]{2,1,0:T(8,128)S(1)}, u32[]{:S(2)}, u32[]{:S(2)}) collective-permute-start(f32[9,64,256]{2,1,0:T(8,128)S(1)} %collective-permute-done.1), channel_id=1, source_target_pairs={{7,4},{0,3},{15,12},{8,11},{23,20},{16,19},{31,28},{24,27}} | collective-permute-start | bytes 1769480 | tf_op jit(solution)/shard_map/ppermute | solution.py:519
  22.2 0.0 collective-permute-done.halo.halo_early
  22.2 0.4 shard_map.112
  22.6 2.7 %collective-permute-start.4 = (f32[4,16,256]{2,1,0:T(8,128)S(1)}, f32[4,16,256]{2,1,0:T(8,128)S(1)}, u32[]{:S(2)}, u32[]{:S(2)}) collective-permute-start(f32[4,16,256]{2,1,0:T(8,128)S(1)} %get-tuple-element.44), channel_id=1, source_target_pairs={{0,16},{8,24},{16,0},{24,8},{1,17},{9,25},{17,1},{25,9},{2,18},{10... | collective-permute-start | bytes 196616 | tf_op jit(solution)/shard_map/ppermute | solution.py:536
  25.2 1.6 %collective-permute-start.5 = (f32[4,16,256]{2,1,0:T(8,128)S(1)}, f32[4,16,256]{2,1,0:T(8,128)S(1)}, u32[]{:S(2)}, u32[]{:S(2)}) collective-permute-start(f32[4,16,256]{2,1,0:T(8,128)S(1)} %get-tuple-element.45), channel_id=1, source_target_pairs={{0,8},{8,0},{16,24},{24,16},{1,9},{9,1},{17,25},{25,17},{2,10},{10... | collective-permute-start | bytes 196616 | tf_op jit(solution)/shard_map/ppermute | solution.py:536
  26.8 0.2 collective-permute-start.6
  27.0 0.7 %shard_map.114.after = f32[8,64,256]{2,1,0:T(8,128)S(1)} custom-call(bf16[2,256,256]{2,1,0:T(8,128)(2,1)S(1)} %get-tuple-element.37.bands, f32[8,64,256]{2,1,0:T(8,128)S(1)} %get-tuple-element.47.outer, f32[8,64,256]{2,1,0:T(8,128)S(1)} %get-tuple-element.48.step, f32[8,64,256]{2,1,0:T(8,128)S(1)} %get-tuple-element.41.forward, ...), custom_call_target="tpu_custom_call" | custom-call | flops 1000000 | bytes 1000000 | tf_op jit(solution)/shard_map/pallas_call | solution.py:528
  27.8 0.0 collective-permute-done.7.rest_0_
  27.8 1.7 %collective-permute-done.8.rest_1_ = f32[9,64,256]{2,1,0:T(8,128)S(1)} collective-permute-done((f32[9,64,256]{2,1,0:T(8,128)S(1)}, f32[9,64,256]{2,1,0:T(8,128)S(1)}, u32[]{:S(2)}, u32[]{:S(2)}) %collective-permute-start.8) | collective-permute-done | bytes 589856 | tf_op jit(solution)/shard_map/ppermute | solution.py:519
  29.5 0.4 %shard_map.115 = (f32[4,16,256]{2,1,0:T(8,128)S(1)}, f32[4,16,256]{2,1,0:T(8,128)S(1)}, f32[4,16,256]{2,1,0:T(8,128)S(1)}, f32[4,16,256]{2,1,0:T(8,128)S(1)}) custom-call(f32[11,64,256]{2,1,0:T(8,128)S(1)} %shard_map.109.sent_first.own_out, f32[8,64,256]{2,1,0:T(8,128)S(1)} %get-tuple-element.30.speeds, f32[8,64,256]{2,1,0:T(8,128)S(1)} %get-tuple-element.47.outer, ...), custom_call_target="tpu_custom_call" | custom-call | flops 1000000 | bytes 1000000 | tf_op jit(solution)/shard_map/pallas_call | solution.py:541
  30.0 2.7 %collective-permute-start.10 = (f32[4,16,256]{2,1,0:T(8,128)S(1)}, f32[4,16,256]{2,1,0:T(8,128)S(1)}, u32[]{:S(2)}, u32[]{:S(2)}) collective-permute-start(f32[4,16,256]{2,1,0:T(8,128)S(1)} %get-tuple-element.53), channel_id=1, source_target_pairs={{0,16},{8,24},{16,0},{24,8},{1,17},{9,25},{17,1},{25,9},{2,18},{10... | collective-permute-start | bytes 196616 | tf_op jit(solution)/shard_map/ppermute | solution.py:550
  32.6 1.3 %collective-permute-start.11 = (f32[4,16,256]{2,1,0:T(8,128)S(1)}, f32[4,16,256]{2,1,0:T(8,128)S(1)}, u32[]{:S(2)}, u32[]{:S(2)}) collective-permute-start(f32[4,16,256]{2,1,0:T(8,128)S(1)} %get-tuple-element.54), channel_id=1, source_target_pairs={{0,24},{8,16},{16,8},{24,0},{1,25},{9,17},{17,9},{25,1},{2,26},{10... | collective-permute-start | bytes 196616 | tf_op jit(solution)/shard_map/ppermute | solution.py:550
  34.0 0.0 collective-permute-done.4.refs_1_
  34.0 0.2 collective-permute-start.9
  34.2 0.0 collective-permute-done.5.refs_2_
  34.2 0.0 collective-permute-done.6.refs_3_
  34.2 3.5 %collective-permute-done.10.refs_2_ = f32[4,16,256]{2,1,0:T(8,128)S(1)} collective-permute-done((f32[4,16,256]{2,1,0:T(8,128)S(1)}, f32[4,16,256]{2,1,0:T(8,128)S(1)}, u32[]{:S(2)}, u32[]{:S(2)}) %collective-permute-start.10) | collective-permute-done | bytes 65568 | tf_op jit(solution)/shard_map/ppermute | solution.py:550
  37.7 1.1 %collective-permute-done.11.refs_3_ = f32[4,16,256]{2,1,0:T(8,128)S(1)} collective-permute-done((f32[4,16,256]{2,1,0:T(8,128)S(1)}, f32[4,16,256]{2,1,0:T(8,128)S(1)}, u32[]{:S(2)}, u32[]{:S(2)}) %collective-permute-start.11) | collective-permute-done | bytes 65568 | tf_op jit(solution)/shard_map/ppermute | solution.py:550
  38.8 0.5 %collective-permute-done.9.refs_1_ = f32[4,16,256]{2,1,0:T(8,128)S(1)} collective-permute-done((f32[4,16,256]{2,1,0:T(8,128)S(1)}, f32[4,16,256]{2,1,0:T(8,128)S(1)}, u32[]{:S(2)}, u32[]{:S(2)}) %collective-permute-start.9) | collective-permute-done | bytes 65568 | tf_op jit(solution)/shard_map/ppermute | solution.py:550
  39.3 0.7 %shard_map.116 = f32[8,16,256]{2,1,0:T(8,128)} custom-call(f32[4,16,256]{2,1,0:T(8,128)S(1)} %shard_map.113.inner, f32[4,16,256]{2,1,0:T(8,128)S(1)} %get-tuple-element.51.refs_0_, f32[4,16,256]{2,1,0:T(8,128)S(1)} %collective-permute-done.9.refs_1_, f32[4,16,256]{2,1,0:T(8,128)S(1)} %collective-permute-done.10.refs_2_, ...), custom_call_target="tpu_custom_call" | custom-call | flops 1000000 | bytes 1000000 | tf_op jit(solution)/shard_map/pallas_call | solution.py:552
  (1 shorter events, 0.0 us)
Async XLA Ops:
  0.0 2.1 %copy-start = (f32[8,64,256]{2,1,0:T(8,128)S(1)}, f32[8,64,256]{2,1,0:T(8,128)}, u32[]{:S(2)}) copy-start(f32[8,64,256]{2,1,0:T(8,128)} %courant.3) | copy-start | bytes 1572868
  0.0 2.1 %copy-start.1 = (f32[1,8,64,256]{3,2,1,0:T(8,128)S(1)}, f32[1,8,64,256]{3,2,1,0:T(8,128)}, u32[]{:S(2)}) copy-start(f32[1,8,64,256]{3,2,1,0:T(8,128)} %param.13) | copy-start | bytes 1572868
  0.0 2.1 %copy-start.2 = (f32[1,8,64,256]{3,2,1,0:T(8,128)S(1)}, f32[1,8,64,256]{3,2,1,0:T(8,128)}, u32[]{:S(2)}) copy-start(f32[1,8,64,256]{3,2,1,0:T(8,128)} %param.15) | copy-start | bytes 1572868
  0.0 2.1 %copy-start.6 = (f32[1,8,64,256]{3,2,1,0:T(8,128)S(1)}, f32[1,8,64,256]{3,2,1,0:T(8,128)}, u32[]{:S(2)}) copy-start(f32[1,8,64,256]{3,2,1,0:T(8,128)} %param.12) | copy-start | bytes 1572868
  1.4 20.8 %collective-permute-start = (f32[11,64,256]{2,1,0:T(8,128)S(1)}, f32[11,64,256]{2,1,0:T(8,128)S(1)}, u32[]{:S(2)}, u32[]{:S(2)}) collective-permute-start(f32[11,64,256]{2,1,0:T(8,128)S(1)} %shard_map.109.sent_first.own_out), channel_id=1, source_target_pairs={{1,2},{3,4},{5,6},{2,1},{4,3},{6,5},{9,10},{11,12},{13,14},{10,9},... | collective-permute-start | bytes 2162696 | tf_op jit(solution)/shard_map/ppermute | solution.py:469
  2.1 11.0 %copy-start.5 = (s32[1,256]{1,0:T(1,128)S(1)}, s32[1,256]{1,0:T(1,128)}, u32[]{:S(2)}) copy-start(s32[1,256]{1,0:T(1,128)} %receiver_yz.1) | copy-start | bytes 3076
  4.7 8.4 %collective-permute-start.2 = (f32[10,64,256]{2,1,0:T(8,128)S(1)}, f32[10,64,256]{2,1,0:T(8,128)S(1)}, u32[]{:S(2)}, u32[]{:S(2)}) collective-permute-start(f32[10,64,256]{2,1,0:T(8,128)S(1)} %get-tuple-element.32.own_in), channel_id=1, source_target_pairs={{0,1},{1,0},{2,3},{3,2},{4,5},{5,4},{6,7},{7,6},{8,9},{9,8},{10,11... | collective-permute-start | bytes 1966088 | tf_op jit(solution)/shard_map/ppermute | solution.py:482
  9.0 4.1 %collective-permute-start.3 = (f32[10,64,256]{2,1,0:T(8,128)S(1)}, f32[10,64,256]{2,1,0:T(8,128)S(1)}, u32[]{:S(2)}, u32[]{:S(2)}) collective-permute-start(f32[10,64,256]{2,1,0:T(8,128)S(1)} %get-tuple-element.35.late_in), channel_id=1, source_target_pairs={{0,1},{1,0},{2,3},{3,2},{4,5},{5,4},{6,7},{7,6},{8,9},{9,8},{10,11... | collective-permute-start | bytes 1966088 | tf_op jit(solution)/shard_map/ppermute | solution.py:483
  9.1 11.8 %collective-permute-start.1 = (f32[9,64,256]{2,1,0:T(8,128)S(1)}, f32[9,64,256]{2,1,0:T(8,128)S(1)}, u32[]{:S(2)}, u32[]{:S(2)}) collective-permute-start(f32[9,64,256]{2,1,0:T(8,128)S(1)} %get-tuple-element.31.late_out), channel_id=1, source_target_pairs={{3,7},{4,0},{11,15},{12,8},{19,23},{20,16},{27,31},{28,24}} | collective-permute-start | bytes 1769480 | tf_op jit(solution)/shard_map/ppermute | solution.py:485
  10.4 17.4 %collective-permute-start.7 = (f32[9,64,256]{2,1,0:T(8,128)S(1)}, f32[9,64,256]{2,1,0:T(8,128)S(1)}, u32[]{:S(2)}, u32[]{:S(2)}) collective-permute-start(f32[9,64,256]{2,1,0:T(8,128)S(1)} %get-tuple-element.31.late_out), channel_id=1, source_target_pairs={{1,2},{5,6},{2,1},{6,5},{9,10},{13,14},{10,9},{14,13},{17,18},{21,... | collective-permute-start | bytes 1769480 | tf_op jit(solution)/shard_map/ppermute | solution.py:486
  12.4 0.7 %copy-start.7 = (f32[1,2]{1,0:T(1,128)S(1)}, f32[1,2]{1,0:T(1,128)}, u32[]{:S(2)}) copy-start(f32[1,2]{1,0:T(1,128)} %param.18) | copy-start | bytes 28
  13.1 0.7 %copy-start.3 = (f32[1,256,2]{1,2,0:T(2,128)S(1)}, f32[1,256,2]{1,2,0:T(2,128)}, u32[]{:S(2)}) copy-start(f32[1,256,2]{1,2,0:T(2,128)} %param.21) | copy-start | bytes 6148
  13.1 0.7 %copy-start.4 = (s32[1,256]{1,0:T(1,128)S(1)}, s32[1,256]{1,0:T(1,128)}, u32[]{:S(2)}) copy-start(s32[1,256]{1,0:T(1,128)} %receiver_x.1) | copy-start | bytes 3076
  20.9 8.7 %collective-permute-start.8 = (f32[9,64,256]{2,1,0:T(8,128)S(1)}, f32[9,64,256]{2,1,0:T(8,128)S(1)}, u32[]{:S(2)}, u32[]{:S(2)}) collective-permute-start(f32[9,64,256]{2,1,0:T(8,128)S(1)} %collective-permute-done.1), channel_id=1, source_target_pairs={{7,4},{0,3},{15,12},{8,11},{23,20},{16,19},{31,28},{24,27}} | collective-permute-start | bytes 1769480 | tf_op jit(solution)/shard_map/ppermute | solution.py:519
  22.6 11.4 %collective-permute-start.4 = (f32[4,16,256]{2,1,0:T(8,128)S(1)}, f32[4,16,256]{2,1,0:T(8,128)S(1)}, u32[]{:S(2)}, u32[]{:S(2)}) collective-permute-start(f32[4,16,256]{2,1,0:T(8,128)S(1)} %get-tuple-element.44), channel_id=1, source_target_pairs={{0,16},{8,24},{16,0},{24,8},{1,17},{9,25},{17,1},{25,9},{2,18},{10... | collective-permute-start | bytes 196616 | tf_op jit(solution)/shard_map/ppermute | solution.py:536
  25.2 9.0 %collective-permute-start.5 = (f32[4,16,256]{2,1,0:T(8,128)S(1)}, f32[4,16,256]{2,1,0:T(8,128)S(1)}, u32[]{:S(2)}, u32[]{:S(2)}) collective-permute-start(f32[4,16,256]{2,1,0:T(8,128)S(1)} %get-tuple-element.45), channel_id=1, source_target_pairs={{0,8},{8,0},{16,24},{24,16},{1,9},{9,1},{17,25},{25,17},{2,10},{10... | collective-permute-start | bytes 196616 | tf_op jit(solution)/shard_map/ppermute | solution.py:536
  26.8 7.4 %collective-permute-start.6 = (f32[4,16,256]{2,1,0:T(8,128)S(1)}, f32[4,16,256]{2,1,0:T(8,128)S(1)}, u32[]{:S(2)}, u32[]{:S(2)}) collective-permute-start(f32[4,16,256]{2,1,0:T(8,128)S(1)} %get-tuple-element.46), channel_id=1, source_target_pairs={{0,24},{8,16},{16,8},{24,0},{1,25},{9,17},{17,9},{25,1},{2,26},{10... | collective-permute-start | bytes 196616 | tf_op jit(solution)/shard_map/ppermute | solution.py:536
  30.0 7.7 %collective-permute-start.10 = (f32[4,16,256]{2,1,0:T(8,128)S(1)}, f32[4,16,256]{2,1,0:T(8,128)S(1)}, u32[]{:S(2)}, u32[]{:S(2)}) collective-permute-start(f32[4,16,256]{2,1,0:T(8,128)S(1)} %get-tuple-element.53), channel_id=1, source_target_pairs={{0,16},{8,24},{16,0},{24,8},{1,17},{9,25},{17,1},{25,9},{2,18},{10... | collective-permute-start | bytes 196616 | tf_op jit(solution)/shard_map/ppermute | solution.py:550
  32.6 6.2 %collective-permute-start.11 = (f32[4,16,256]{2,1,0:T(8,128)S(1)}, f32[4,16,256]{2,1,0:T(8,128)S(1)}, u32[]{:S(2)}, u32[]{:S(2)}) collective-permute-start(f32[4,16,256]{2,1,0:T(8,128)S(1)} %get-tuple-element.54), channel_id=1, source_target_pairs={{0,24},{8,16},{16,8},{24,0},{1,25},{9,17},{17,9},{25,1},{2,26},{10... | collective-permute-start | bytes 196616 | tf_op jit(solution)/shard_map/ppermute | solution.py:550
  34.0 5.4 %collective-permute-start.9 = (f32[4,16,256]{2,1,0:T(8,128)S(1)}, f32[4,16,256]{2,1,0:T(8,128)S(1)}, u32[]{:S(2)}, u32[]{:S(2)}) collective-permute-start(f32[4,16,256]{2,1,0:T(8,128)S(1)} %get-tuple-element.52), channel_id=1, source_target_pairs={{0,8},{8,0},{16,24},{24,16},{1,9},{9,1},{17,25},{25,17},{2,10},{10... | collective-permute-start | bytes 196616 | tf_op jit(solution)/shard_map/ppermute | solution.py:550

commit v5 on v4

--- a/solution.py
+++ b/solution.py
@@ -11,12 +11,13 @@
 REACH = 4
 SCALE = 5040.0
 WHOLE_SIDE = (8064.0, -1008.0, 128.0, -9.0)
-EARLY_SPEEDS, INNER_SPEEDS = 3, 2
-INWARD_ORDER, OUTWARD_ORDER = [2, 1, 3], [1, 2, 3]
+EARLY_SPEEDS, INNER_SPEEDS = 2, 2
+EARLY_EXTRA, LATE_EXTRA = 16, 8
+INWARD_ORDER, OUTWARD_ORDER = [2, 3, 1], [1, 2, 3]
 F32 = jnp.float32
 BF16 = jnp.bfloat16
 VMEM_LIMIT = 32 * 1024 * 1024
-MIDDLE_COST = int(6 * 10**9)
+MIDDLE_COST = int(8 * 10**9)
 SECOND_COST = int(0.001 * 10**9)
 SMALL, LARGE = 10**6, 10**10
 
@@ -88,7 +89,12 @@
     return functools.reduce(lambda a, b: a + b, [v for v in values if v is not None])
 
 
+def layer_rows(layer, size_y):
+    return slice(layer * size_y, (layer + 1) * size_y)
+
+
 def early_kernel(courant, now, adjoint, packet, speeds, fields, adjoints, sems):
+    size_y = fields.shape[1]
     odd = lax.rem(lax.axis_index("space"), 2)
     pairs = ((courant, speeds), (adjoint, adjoints), (now, fields))
     copies = [
@@ -102,10 +108,11 @@
     for layer in range(REACH):
         at = layer + odd * (REACH - 1 - 2 * layer)
         speed = speeds[at]
-        packet[layer] = fields[at]
-        packet[REACH + layer] = speed * speed * adjoints[at]
+        packet[layer_rows(layer, size_y)] = fields[at]
+        packet[layer_rows(REACH + layer, size_y)] = speed * speed * adjoints[at]
         if layer < EARLY_SPEEDS:
-            packet[2 * REACH + layer] = speed
+            packet[layer_rows(2 * REACH + layer, size_y)] = speed
+    packet[(2 * REACH + EARLY_SPEEDS) * size_y :, :] = fields[0, 0:EARLY_EXTRA, :]
 
 
 def local_kernel(
@@ -142,7 +149,13 @@
         adjoint_now[at] = adjoint[place]
         present[at] = now[place]
         scaled[at] = speed * speed * adjoint[place]
-    for mine, packet in ((0, late_out), (REACH, late_in)):
+    def put_out(layer, value):
+        late_out[layer_rows(layer, size_y)] = value
+
+    def put_in(layer, value):
+        late_in[layer] = value
+
+    for mine, put in ((0, put_out), (REACH, put_in)):
         other = REACH - mine
         flat = [
             plane_laplace([layers[mine + at] for at in range(REACH)], along_y, along_z)
@@ -159,7 +172,7 @@
                 from_other(at, lambda i: present[other + i]),
             )
             accel[mine + at] = laplace
-            packet[at] = 2.0 * now[place] - old[place] + speed_sq * laplace
+            put(at, 2.0 * now[place] - old[place] + speed_sq * laplace)
             laplace = add(
                 flat[1][at],
                 within(at, lambda i: scaled[mine + i]),
@@ -167,9 +180,10 @@
             )
             field = 2.0 * adjoint[place] - late_held[place] + laplace
             adjoint_mid[mine + at] = field
-            packet[REACH + at] = speed_sq * field
+            put(REACH + at, speed_sq * field)
     for layer in range(EARLY_SPEEDS, REACH):
-        late_out[2 * REACH + layer - EARLY_SPEEDS] = speeds[layer]
+        put_out(2 * REACH + layer - EARLY_SPEEDS, speeds[layer])
+    late_out[(3 * REACH - EARLY_SPEEDS) * size_y :, :] = speeds[0, 0:LATE_EXTRA, :]
     for layer in range(REACH):
         early_in[layer] = present[REACH + layer]
         early_in[REACH + layer] = scaled[REACH + layer]
@@ -181,8 +195,8 @@
 
 def next_halo(at, speed, late, own, points):
     speed_sq = speed * speed
-    mid = late[at] + speed_sq * (across(at, lambda i: own[i]) + points[at])
-    scaled = late[REACH + at] + speed_sq * (
+    mid = late(at) + speed_sq * (across(at, lambda i: own[i]) + points[at])
+    scaled = late(REACH + at) + speed_sq * (
         across(at, lambda i: own[REACH + i]) + points[REACH + at]
     )
     return mid, scaled
@@ -285,13 +299,15 @@
         fire = fired(0, REACH + at)
         outer[at] = accel[at] + fire
         outer[REACH + at] = adjoint_mid[at] + added[REACH + at]
-        outer[2 * REACH + at] = late_out[at] + speed * speed * fire
+        outer[2 * REACH + at] = late_out[layer_rows(at, size_y)] + speed * speed * fire
     for at in range(REACH):
         if at < INNER_SPEEDS:
             speed = halo_early[2 * REACH + at]
         else:
             speed = halo_late[2 * REACH + at - INNER_SPEEDS]
-        next_mid[at], next_scaled[at] = next_halo(at, speed, halo_late, own_in, points_in)
+        next_mid[at], next_scaled[at] = next_halo(
+            at, speed, lambda i: halo_late[i], own_in, points_in
+        )
     for at in range(REACH):
         to = REACH + slab - 1 - at
         speed = speeds[REACH + at]
@@ -329,11 +345,12 @@
 
 def middle_kernel(shots, speeds, halo, inner, outer_part, forward, backward, outer, step, *rest):
     outputs, (gradient,) = rest[:shots], rest[shots:]
+    size_y = speeds.shape[1]
     for at in range(REACH):
         speed = speeds[at]
         speed_sq = speed * speed
-        extra = across(at, lambda i: halo[i])
-        adjoint = outer_part[REACH + at] + across(at, lambda i: halo[REACH + i])
+        extra = across(at, lambda i: halo[layer_rows(i, size_y)])
+        adjoint = outer_part[REACH + at] + across(at, lambda i: halo[layer_rows(REACH + i, size_y)])
         outer[at] = outer_part[at] + extra
         outer[REACH + at] = adjoint
         step[at] = outer_part[2 * REACH + at] + speed_sq * extra
@@ -362,18 +379,19 @@
 
 def outer_kernel(shots, relayed, own_out, speeds, outer, after, halo_early, points_out, *rest):
     lates, rest = rest[: 1 + relayed], rest[1 + relayed :]
-    outputs, (late, next_mid, next_scaled, gradient) = rest[:shots], rest[shots:]
-    if relayed:
-        for layer in range(late.shape[0]):
-            late[layer] = lates[0][layer] + lates[1][layer]
-    else:
-        late = lates[0]
+    outputs, (next_mid, next_scaled, gradient) = rest[:shots], rest[shots:]
+
+    def late(layer):
+        return add(*[packet[layer_rows(layer, size_y)] for packet in lates])
+
+    size_y = speeds.shape[1]
+    own = [own_out[layer_rows(i, size_y)] for i in range(2 * REACH)]
     for at in range(REACH):
         if at < EARLY_SPEEDS:
-            speed = halo_early[2 * REACH + at]
+            speed = halo_early[layer_rows(2 * REACH + at, size_y)]
         else:
-            speed = late[2 * REACH + at - EARLY_SPEEDS]
-        next_mid[at], next_scaled[at] = next_halo(at, speed, late, own_out, points_out)
+            speed = late(2 * REACH + at - EARLY_SPEEDS)
+        next_mid[at], next_scaled[at] = next_halo(at, speed, late, own, points_out)
     for at in range(REACH):
         ahead = after[at] + across(at, lambda i: next_mid[i])
         back = after[REACH + at] + across(at, lambda i: next_scaled[i])
@@ -460,7 +478,7 @@
     late_layers = 3 * REACH - EARLY_SPEEDS
     early_out = call(
         early_kernel,
-        stack(early_layers),
+        (early_layers * size_y + EARLY_EXTRA, size_z),
         [H] * 3,
         [held(REACH)] * 3 + [pltpu.SemaphoreType.DMA((3,))],
         SMALL,
@@ -472,7 +490,8 @@
     accel, adjoint_mid, speeds, adjoint_half, bands, early_in, late_out, late_in = call(
         local_kernel,
         [stack(slab)] * 4
-        + [bands, stack(2 * REACH + INNER_SPEEDS), stack(late_layers)]
+        + [bands, stack(2 * REACH + INNER_SPEEDS)]
+        + [(late_layers * size_y + LATE_EXTRA, size_z)]
         + [stack(3 * REACH - INNER_SPEEDS)],
         [pl.ANY] + [V] * 4 + [H],
         [held(slab)] * 3 + [pltpu.SemaphoreType.DMA(())],
@@ -542,7 +561,7 @@
         functools.partial(outer_kernel, shots, relayed),
         [(REACH, part_rows, size_z)] * shots,
         [V] * (6 + len(halo_lates)),
-        [held(late_layers)] + [held(REACH)] * 3,
+        [held(REACH)] * 3,
         SMALL,
         SMALL,
     )(early_out, speeds, outer, after, halo_out, points_out, *halo_lates)

time: 40.3 us -> 40 us (level)
  starting transfers between devices: 17.1 us -> 16.3 us
    ppermute x1, waiting for transfers between devices: 1.75 us -> 2.7 us  [on_device(): halo_lates.append(lax.ppermute(first_hop, 'space', [(7, 4), (0, 3)]))]
    ppermute x1, waiting for transfers between devices: 5.38 us -> 4.61 us  [on_device(): first_hop = lax.ppermute(late_out, 'space', [(3, 7), (4, 0)])]
    ppermute x1, starting transfers between devices: 4.34 us -> 3.75 us  [on_device(): halo_in = lax.ppermute(early_in, 'space', in_pairs)]
  transfers between devices with their start and end apart: 12 -> 12, of which waited for: 5 -> 5; matrix products, arithmetic and copies ran while one was open for 0% -> 0% of each run, Pallas kernels for 14% -> 15%
where the time goes in v5:
time: 40 us; the launch traced here: 39.7 us
  starting transfers between devices  16.3 us (41%)
  waiting for transfers between devices  12.5 us (31%)
  Pallas kernels  8.04 us (20%)
  between operations  1.47 us (4%)
  local copies, waits for them, and re-layouts  1.35 us (3%)
    ppermute x3, waiting for transfers between devices, on_device(): lax.ppermute(outer_parts[k], 'shot', shifts[1][k])  5.16 us
    ppermute x1, waiting for transfers between devices, on_device(): first_hop = lax.ppermute(late_out, 'space', [(3, 7), (4, 0)])  4.61 us
    ppermute x3, starting transfers between devices, on_device(): lax.ppermute(outer_parts[k], 'shot', shifts[1][k])  4.24 us
    ppermute x3, starting transfers between devices, on_device(): lax.ppermute(inner_parts[k], 'shot', shifts[0][k])  4.24 us
    ppermute x1, starting transfers between devices, on_device(): halo_in = lax.ppermute(early_in, 'space', in_pairs)  3.75 us
    ppermute x1, waiting for transfers between devices, on_device(): halo_lates.append(lax.ppermute(first_hop, 'space', [(7, 4), (0, 3)]))  2.7 us
    pallas_call x1, Pallas kernels, on_device(): call(local_kernel, [stack(slab)] * 4 + [bands, stack(2 * REACH + INNER_SP...  2.6 us
    pallas_call x1, Pallas kernels, on_device(): call(inner_kernel, [stack(2 * REACH), stack(3 * REACH)] + [stack(2 * REAC...  1.8 us
  transfers between devices with their start and end apart: 12, of which 5 were waited for; matrix products, arithmetic and copies ran while one was open for 0% of the time, Pallas kernels for 15%

profile of v5, /device:TPU:0, one launch (start us, length us, event | category | flops | bytes accessed | tf_op | source)
XLA Modules:
  0.0 39.7 jit_solution(3678332937983459885)
XLA Ops:
  0.0 0.0 copy-start
  0.0 0.0 copy-start.1
  0.0 0.0 copy-start.2
  0.0 0.0 copy-start.6
  0.0 1.3 %shard_map.109.sent_first.own_out = f32[656,256]{1,0:T(8,128)S(1)} custom-call(f32[8,64,256]{2,1,0:T(8,128)} %courant.3, f32[8,64,256]{2,1,0:T(8,128)} %bitcast.10, f32[8,64,256]{2,1,0:T(8,128)} %bitcast.12), custom_call_target="tpu_custom_call" | custom-call | flops 1000000 | bytes 1000000 | tf_op jit(solution)/shard_map/pallas_call | solution.py:479
  1.4 0.7 %collective-permute-start = (f32[656,256]{1,0:T(8,128)S(1)}, f32[656,256]{1,0:T(8,128)S(1)}, u32[]{:S(2)}, u32[]{:S(2)}) collective-permute-start(f32[656,256]{1,0:T(8,128)S(1)} %shard_map.109.sent_first.own_out), channel_id=1, source_target_pairs={{1,2},{3,4},{5,6},{2,1},{4,3},{6,5},{9,10},{11,12},{13,14},{10,9},... | collective-permute-start | bytes 2015240 | tf_op jit(solution)/shard_map/ppermute | solution.py:487
  2.1 0.0 copy-done
  2.1 0.0 copy-done.1
  2.1 0.0 copy-done.2
  2.1 0.0 copy-done.6
  2.1 0.0 copy-start.5
  2.1 2.6 %shard_map.110 = (f32[8,64,256]{2,1,0:T(8,128)S(1)}, f32[8,64,256]{2,1,0:T(8,128)S(1)}, f32[8,64,256]{2,1,0:T(8,128)S(1)}, f32[8,64,256]{2,1,0:T(8,128)S(1)}, bf...) custom-call(f32[656,256]{1,0:T(8,128)S(1)} %shard_map.109.sent_first, ...), custom_call_target="tpu_custom_call" | custom-call | flops 10000000000 | bytes 1000000 | tf_op jit(solution)/shard_map/pallas_call | solution.py:490
  4.7 1.3 %collective-permute-start.1 = (f32[648,256]{1,0:T(8,128)S(1)}, f32[648,256]{1,0:T(8,128)S(1)}, u32[]{:S(2)}, u32[]{:S(2)}) collective-permute-start(f32[648,256]{1,0:T(8,128)S(1)} %get-tuple-element.31.late_out), channel_id=1, source_target_pairs={{3,7},{4,0},{11,15},{12,8},{19,23},{20,16},{27,31},{28,24}} | collective-permute-start | bytes 1990664 | tf_op jit(solution)/shard_map/ppermute | solution.py:504
  6.0 3.7 %collective-permute-start.2 = (f32[10,64,256]{2,1,0:T(8,128)S(1)}, f32[10,64,256]{2,1,0:T(8,128)S(1)}, u32[]{:S(2)}, u32[]{:S(2)}) collective-permute-start(f32[10,64,256]{2,1,0:T(8,128)S(1)} %get-tuple-element.32.own_in), channel_id=1, source_target_pairs={{0,1},{1,0},{2,3},{3,2},{4,5},{5,4},{6,7},{7,6},{8,9},{9,8},{10,11... | collective-permute-start | bytes 1966088 | tf_op jit(solution)/shard_map/ppermute | solution.py:501
  9.8 0.1 collective-permute-start.3
  9.9 0.7 %collective-permute-start.7 = (f32[648,256]{1,0:T(8,128)S(1)}, f32[648,256]{1,0:T(8,128)S(1)}, u32[]{:S(2)}, u32[]{:S(2)}) collective-permute-start(f32[648,256]{1,0:T(8,128)S(1)} %get-tuple-element.31.late_out), channel_id=1, source_target_pairs={{1,2},{5,6},{2,1},{6,5},{9,10},{13,14},{10,9},{14,13},{17,18},{21,... | collective-permute-start | bytes 1990664 | tf_op jit(solution)/shard_map/ppermute | solution.py:505
  11.8 0.0 copy-start.7
  11.9 0.6 %copy-done.7 = f32[1,2]{1,0:T(1,128)S(1)} copy-done((f32[1,2]{1,0:T(1,128)S(1)}, f32[1,2]{1,0:T(1,128)}, u32[]{:S(2)}) %copy-start.7) | copy-done | bytes 32
  12.5 0.1 maximum_bitcast_fusion.pulse
  12.6 0.0 collective-permute-done.2.halo_early
  12.6 0.0 collective-permute-done.3.halo_late
  12.6 0.0 copy-start.3
  12.6 0.0 copy-start.4
  12.6 0.0 copy-done.5
  12.6 0.7 %copy-done.3 = f32[1,256,2]{1,2,0:T(2,128)S(1)} copy-done((f32[1,256,2]{1,2,0:T(2,128)S(1)}, f32[1,256,2]{1,2,0:T(2,128)}, u32[]{:S(2)}) %copy-start.3) | copy-done | bytes 2072
  13.3 0.0 copy-done.4
  13.3 1.8 %shard_map.111 = (f32[8,64,256]{2,1,0:T(8,128)S(1)}, f32[12,64,256]{2,1,0:T(8,128)S(1)}, f32[8,64,256]{2,1,0:T(8,128)S(1)}, f32[8,64,256]{2,1,0:T(8,128)S(1)}, f32[8,64,256]{2,1,0:T(8,128)S(1)}) custom-call(f32[1,4]{1,0:T(1,128)S(1)} %maximum_bitcast_fusion.pulse, s32[1,256]{1,0:T(1,128)S(1)} %copy-done.4, s32[1,256]{1,0:T(1,128)S(1)} %copy-done.5, ...), custom_call_target="tpu_custom_call" | custom-call | flops 1000000 | bytes 1000000 | tf_op jit(solution)/shard_map/pallas_call | solution.py:508
  15.1 4.6 %collective-permute-done.1 = f32[648,256]{1,0:T(8,128)S(1)} collective-permute-done((f32[648,256]{1,0:T(8,128)S(1)}, f32[648,256]{1,0:T(8,128)S(1)}, u32[]{:S(2)}, u32[]{:S(2)}) %collective-permute-start.1) | collective-permute-done | bytes 663584 | tf_op jit(solution)/shard_map/ppermute | solution.py:504
  19.7 1.3 %collective-permute-start.8 = (f32[648,256]{1,0:T(8,128)S(1)}, f32[648,256]{1,0:T(8,128)S(1)}, u32[]{:S(2)}, u32[]{:S(2)}) collective-permute-start(f32[648,256]{1,0:T(8,128)S(1)} %collective-permute-done.1), channel_id=1, source_target_pairs={{7,4},{0,3},{15,12},{8,11},{23,20},{16,19},{31,28},{24,27}} | collective-permute-start | bytes 1990664 | tf_op jit(solution)/shard_map/ppermute | solution.py:538
  21.0 0.0 collective-permute-done.halo.halo_early
  21.0 0.4 %shard_map.112 = (f32[8,64,256]{2,1,0:T(8,128)S(1)}, f32[8,64,256]{2,1,0:T(8,128)S(1)}, f32[4,16,256]{2,1,0:T(8,128)S(1)}, f32[4,16,256]{2,1,0:T(8,128)S(1)}, f3...) custom-call(f32[8,64,256]{2,1,0:T(8,128)S(1)} %get-tuple-element.30.speeds, ...), custom_call_target="tpu_custom_call" | custom-call | flops 8000000000 | bytes 1000000 | tf_op jit(solution)/shard_map/pallas_call | solution.py:539
  21.5 2.7 %collective-permute-start.4 = (f32[4,16,256]{2,1,0:T(8,128)S(1)}, f32[4,16,256]{2,1,0:T(8,128)S(1)}, u32[]{:S(2)}, u32[]{:S(2)}) collective-permute-start(f32[4,16,256]{2,1,0:T(8,128)S(1)} %get-tuple-element.44), channel_id=1, source_target_pairs={{0,16},{8,24},{16,0},{24,8},{1,17},{9,25},{17,1},{25,9},{2,18},{10... | collective-permute-start | bytes 196616 | tf_op jit(solution)/shard_map/ppermute | solution.py:555
  24.1 1.3 %collective-permute-start.5 = (f32[4,16,256]{2,1,0:T(8,128)S(1)}, f32[4,16,256]{2,1,0:T(8,128)S(1)}, u32[]{:S(2)}, u32[]{:S(2)}) collective-permute-start(f32[4,16,256]{2,1,0:T(8,128)S(1)} %get-tuple-element.45), channel_id=1, source_target_pairs={{0,24},{8,16},{16,8},{24,0},{1,25},{9,17},{17,9},{25,1},{2,26},{10... | collective-permute-start | bytes 196616 | tf_op jit(solution)/shard_map/ppermute | solution.py:555
  25.5 0.2 collective-permute-start.6
  25.7 0.8 %shard_map.114.after = f32[8,64,256]{2,1,0:T(8,128)S(1)} custom-call(bf16[2,256,256]{2,1,0:T(8,128)(2,1)S(1)} %get-tuple-element.37.bands, f32[8,64,256]{2,1,0:T(8,128)S(1)} %get-tuple-element.47.outer, f32[8,64,256]{2,1,0:T(8,128)S(1)} %get-tuple-element.48.step, f32[8,64,256]{2,1,0:T(8,128)S(1)} %get-tuple-element.41.forward, ...), custom_call_target="tpu_custom_call" | custom-call | flops 1000000 | bytes 1000000 | tf_op jit(solution)/shard_map/pallas_call | solution.py:547
  26.5 0.0 collective-permute-done.7.rest_0_
  26.5 2.7 %collective-permute-done.8.rest_1_ = f32[648,256]{1,0:T(8,128)S(1)} collective-permute-done((f32[648,256]{1,0:T(8,128)S(1)}, f32[648,256]{1,0:T(8,128)S(1)}, u32[]{:S(2)}, u32[]{:S(2)}) %collective-permute-start.8) | collective-permute-done | bytes 663584 | tf_op jit(solution)/shard_map/ppermute | solution.py:538
  29.2 0.4 %shard_map.115 = (f32[4,16,256]{2,1,0:T(8,128)S(1)}, f32[4,16,256]{2,1,0:T(8,128)S(1)}, f32[4,16,256]{2,1,0:T(8,128)S(1)}, f32[4,16,256]{2,1,0:T(8,128)S(1)}) custom-call(f32[656,256]{1,0:T(8,128)S(1)} %shard_map.109.sent_first.own_out, f32[8,64,256]{2,1,0:T(8,128)S(1)} %get-tuple-element.30.speeds, f32[8,64,256]{2,1,0:T(8,128)S(1)} %get-tuple-element.47.outer, ...), custom_call_target="tpu_custom_call" | custom-call | flops 1000000 | bytes 1000000 | tf_op jit(solution)/shard_map/pallas_call | solution.py:560
  29.6 2.7 %collective-permute-start.10 = (f32[4,16,256]{2,1,0:T(8,128)S(1)}, f32[4,16,256]{2,1,0:T(8,128)S(1)}, u32[]{:S(2)}, u32[]{:S(2)}) collective-permute-start(f32[4,16,256]{2,1,0:T(8,128)S(1)} %get-tuple-element.53), channel_id=1, source_target_pairs={{0,16},{8,24},{16,0},{24,8},{1,17},{9,25},{17,1},{25,9},{2,18},{10... | collective-permute-start | bytes 196616 | tf_op jit(solution)/shard_map/ppermute | solution.py:569
  32.3 1.3 %collective-permute-start.11 = (f32[4,16,256]{2,1,0:T(8,128)S(1)}, f32[4,16,256]{2,1,0:T(8,128)S(1)}, u32[]{:S(2)}, u32[]{:S(2)}) collective-permute-start(f32[4,16,256]{2,1,0:T(8,128)S(1)} %get-tuple-element.54), channel_id=1, source_target_pairs={{0,24},{8,16},{16,8},{24,0},{1,25},{9,17},{17,9},{25,1},{2,26},{10... | collective-permute-start | bytes 196616 | tf_op jit(solution)/shard_map/ppermute | solution.py:569
  33.6 0.0 collective-permute-done.4.refs_1_
  33.6 0.2 collective-permute-start.9
  33.9 0.0 collective-permute-done.5.refs_2_
  33.9 0.0 collective-permute-done.6.refs_3_
  33.9 3.4 %collective-permute-done.10.refs_2_ = f32[4,16,256]{2,1,0:T(8,128)S(1)} collective-permute-done((f32[4,16,256]{2,1,0:T(8,128)S(1)}, f32[4,16,256]{2,1,0:T(8,128)S(1)}, u32[]{:S(2)}, u32[]{:S(2)}) %collective-permute-start.10) | collective-permute-done | bytes 65568 | tf_op jit(solution)/shard_map/ppermute | solution.py:569
  37.3 1.3 %collective-permute-done.11.refs_3_ = f32[4,16,256]{2,1,0:T(8,128)S(1)} collective-permute-done((f32[4,16,256]{2,1,0:T(8,128)S(1)}, f32[4,16,256]{2,1,0:T(8,128)S(1)}, u32[]{:S(2)}, u32[]{:S(2)}) %collective-permute-start.11) | collective-permute-done | bytes 65568 | tf_op jit(solution)/shard_map/ppermute | solution.py:569
  38.6 0.4 %collective-permute-done.9.refs_1_ = f32[4,16,256]{2,1,0:T(8,128)S(1)} collective-permute-done((f32[4,16,256]{2,1,0:T(8,128)S(1)}, f32[4,16,256]{2,1,0:T(8,128)S(1)}, u32[]{:S(2)}, u32[]{:S(2)}) %collective-permute-start.9) | collective-permute-done | bytes 65568 | tf_op jit(solution)/shard_map/ppermute | solution.py:569
  39.0 0.7 %shard_map.116 = f32[8,16,256]{2,1,0:T(8,128)} custom-call(f32[4,16,256]{2,1,0:T(8,128)S(1)} %shard_map.113.inner, f32[4,16,256]{2,1,0:T(8,128)S(1)} %get-tuple-element.51.refs_0_, f32[4,16,256]{2,1,0:T(8,128)S(1)} %collective-permute-done.9.refs_1_, f32[4,16,256]{2,1,0:T(8,128)S(1)} %collective-permute-done.10.refs_2_, ...), custom_call_target="tpu_custom_call" | custom-call | flops 1000000 | bytes 1000000 | tf_op jit(solution)/shard_map/pallas_call | solution.py:571
  (1 shorter events, 0.0 us)
Async XLA Ops:
  0.0 2.1 %copy-start = (f32[8,64,256]{2,1,0:T(8,128)S(1)}, f32[8,64,256]{2,1,0:T(8,128)}, u32[]{:S(2)}) copy-start(f32[8,64,256]{2,1,0:T(8,128)} %courant.3) | copy-start | bytes 1572868
  0.0 2.1 %copy-start.1 = (f32[1,8,64,256]{3,2,1,0:T(8,128)S(1)}, f32[1,8,64,256]{3,2,1,0:T(8,128)}, u32[]{:S(2)}) copy-start(f32[1,8,64,256]{3,2,1,0:T(8,128)} %param.13) | copy-start | bytes 1572868
  0.0 2.1 %copy-start.2 = (f32[1,8,64,256]{3,2,1,0:T(8,128)S(1)}, f32[1,8,64,256]{3,2,1,0:T(8,128)}, u32[]{:S(2)}) copy-start(f32[1,8,64,256]{3,2,1,0:T(8,128)} %param.15) | copy-start | bytes 1572868
  0.0 2.1 %copy-start.6 = (f32[1,8,64,256]{3,2,1,0:T(8,128)S(1)}, f32[1,8,64,256]{3,2,1,0:T(8,128)}, u32[]{:S(2)}) copy-start(f32[1,8,64,256]{3,2,1,0:T(8,128)} %param.12) | copy-start | bytes 1572868
  1.4 19.7 %collective-permute-start = (f32[656,256]{1,0:T(8,128)S(1)}, f32[656,256]{1,0:T(8,128)S(1)}, u32[]{:S(2)}, u32[]{:S(2)}) collective-permute-start(f32[656,256]{1,0:T(8,128)S(1)} %shard_map.109.sent_first.own_out), channel_id=1, source_target_pairs={{1,2},{3,4},{5,6},{2,1},{4,3},{6,5},{9,10},{11,12},{13,14},{10,9},... | collective-permute-start | bytes 2015240 | tf_op jit(solution)/shard_map/ppermute | solution.py:487
  2.1 10.5 %copy-start.5 = (s32[1,256]{1,0:T(1,128)S(1)}, s32[1,256]{1,0:T(1,128)}, u32[]{:S(2)}) copy-start(s32[1,256]{1,0:T(1,128)} %receiver_yz.1) | copy-start | bytes 3076
  4.7 15.0 %collective-permute-start.1 = (f32[648,256]{1,0:T(8,128)S(1)}, f32[648,256]{1,0:T(8,128)S(1)}, u32[]{:S(2)}, u32[]{:S(2)}) collective-permute-start(f32[648,256]{1,0:T(8,128)S(1)} %get-tuple-element.31.late_out), channel_id=1, source_target_pairs={{3,7},{4,0},{11,15},{12,8},{19,23},{20,16},{27,31},{28,24}} | collective-permute-start | bytes 1990664 | tf_op jit(solution)/shard_map/ppermute | solution.py:504
  6.0 6.6 %collective-permute-start.2 = (f32[10,64,256]{2,1,0:T(8,128)S(1)}, f32[10,64,256]{2,1,0:T(8,128)S(1)}, u32[]{:S(2)}, u32[]{:S(2)}) collective-permute-start(f32[10,64,256]{2,1,0:T(8,128)S(1)} %get-tuple-element.32.own_in), channel_id=1, source_target_pairs={{0,1},{1,0},{2,3},{3,2},{4,5},{5,4},{6,7},{7,6},{8,9},{9,8},{10,11... | collective-permute-start | bytes 1966088 | tf_op jit(solution)/shard_map/ppermute | solution.py:501
  9.8 2.8 %collective-permute-start.3 = (f32[10,64,256]{2,1,0:T(8,128)S(1)}, f32[10,64,256]{2,1,0:T(8,128)S(1)}, u32[]{:S(2)}, u32[]{:S(2)}) collective-permute-start(f32[10,64,256]{2,1,0:T(8,128)S(1)} %get-tuple-element.35.late_in), channel_id=1, source_target_pairs={{0,1},{1,0},{2,3},{3,2},{4,5},{5,4},{6,7},{7,6},{8,9},{9,8},{10,11... | collective-permute-start | bytes 1966088 | tf_op jit(solution)/shard_map/ppermute | solution.py:502
  9.9 16.6 %collective-permute-start.7 = (f32[648,256]{1,0:T(8,128)S(1)}, f32[648,256]{1,0:T(8,128)S(1)}, u32[]{:S(2)}, u32[]{:S(2)}) collective-permute-start(f32[648,256]{1,0:T(8,128)S(1)} %get-tuple-element.31.late_out), channel_id=1, source_target_pairs={{1,2},{5,6},{2,1},{6,5},{9,10},{13,14},{10,9},{14,13},{17,18},{21,... | collective-permute-start | bytes 1990664 | tf_op jit(solution)/shard_map/ppermute | solution.py:505
  11.8 0.7 %copy-start.7 = (f32[1,2]{1,0:T(1,128)S(1)}, f32[1,2]{1,0:T(1,128)}, u32[]{:S(2)}) copy-start(f32[1,2]{1,0:T(1,128)} %param.18) | copy-start | bytes 28
  12.6 0.7 %copy-start.3 = (f32[1,256,2]{1,2,0:T(2,128)S(1)}, f32[1,256,2]{1,2,0:T(2,128)}, u32[]{:S(2)}) copy-start(f32[1,256,2]{1,2,0:T(2,128)} %param.21) | copy-start | bytes 6148
  12.6 0.7 %copy-start.4 = (s32[1,256]{1,0:T(1,128)S(1)}, s32[1,256]{1,0:T(1,128)}, u32[]{:S(2)}) copy-start(s32[1,256]{1,0:T(1,128)} %receiver_x.1) | copy-start | bytes 3076
  19.7 9.5 %collective-permute-start.8 = (f32[648,256]{1,0:T(8,128)S(1)}, f32[648,256]{1,0:T(8,128)S(1)}, u32[]{:S(2)}, u32[]{:S(2)}) collective-permute-start(f32[648,256]{1,0:T(8,128)S(1)} %collective-permute-done.1), channel_id=1, source_target_pairs={{7,4},{0,3},{15,12},{8,11},{23,20},{16,19},{31,28},{24,27}} | collective-permute-start | bytes 1990664 | tf_op jit(solution)/shard_map/ppermute | solution.py:538
  21.5 12.2 %collective-permute-start.4 = (f32[4,16,256]{2,1,0:T(8,128)S(1)}, f32[4,16,256]{2,1,0:T(8,128)S(1)}, u32[]{:S(2)}, u32[]{:S(2)}) collective-permute-start(f32[4,16,256]{2,1,0:T(8,128)S(1)} %get-tuple-element.44), channel_id=1, source_target_pairs={{0,16},{8,24},{16,0},{24,8},{1,17},{9,25},{17,1},{25,9},{2,18},{10... | collective-permute-start | bytes 196616 | tf_op jit(solution)/shard_map/ppermute | solution.py:555
  24.1 9.7 %collective-permute-start.5 = (f32[4,16,256]{2,1,0:T(8,128)S(1)}, f32[4,16,256]{2,1,0:T(8,128)S(1)}, u32[]{:S(2)}, u32[]{:S(2)}) collective-permute-start(f32[4,16,256]{2,1,0:T(8,128)S(1)} %get-tuple-element.45), channel_id=1, source_target_pairs={{0,24},{8,16},{16,8},{24,0},{1,25},{9,17},{17,9},{25,1},{2,26},{10... | collective-permute-start | bytes 196616 | tf_op jit(solution)/shard_map/ppermute | solution.py:555
  25.5 8.4 %collective-permute-start.6 = (f32[4,16,256]{2,1,0:T(8,128)S(1)}, f32[4,16,256]{2,1,0:T(8,128)S(1)}, u32[]{:S(2)}, u32[]{:S(2)}) collective-permute-start(f32[4,16,256]{2,1,0:T(8,128)S(1)} %get-tuple-element.46), channel_id=1, source_target_pairs={{0,8},{8,0},{16,24},{24,16},{1,9},{9,1},{17,25},{25,17},{2,10},{10... | collective-permute-start | bytes 196616 | tf_op jit(solution)/shard_map/ppermute | solution.py:555
  29.6 7.7 %collective-permute-start.10 = (f32[4,16,256]{2,1,0:T(8,128)S(1)}, f32[4,16,256]{2,1,0:T(8,128)S(1)}, u32[]{:S(2)}, u32[]{:S(2)}) collective-permute-start(f32[4,16,256]{2,1,0:T(8,128)S(1)} %get-tuple-element.53), channel_id=1, source_target_pairs={{0,16},{8,24},{16,0},{24,8},{1,17},{9,25},{17,1},{25,9},{2,18},{10... | collective-permute-start | bytes 196616 | tf_op jit(solution)/shard_map/ppermute | solution.py:569
  32.3 6.4 %collective-permute-start.11 = (f32[4,16,256]{2,1,0:T(8,128)S(1)}, f32[4,16,256]{2,1,0:T(8,128)S(1)}, u32[]{:S(2)}, u32[]{:S(2)}) collective-permute-start(f32[4,16,256]{2,1,0:T(8,128)S(1)} %get-tuple-element.54), channel_id=1, source_target_pairs={{0,24},{8,16},{16,8},{24,0},{1,25},{9,17},{17,9},{25,1},{2,26},{10... | collective-permute-start | bytes 196616 | tf_op jit(solution)/shard_map/ppermute | solution.py:569
  33.6 5.4 %collective-permute-start.9 = (f32[4,16,256]{2,1,0:T(8,128)S(1)}, f32[4,16,256]{2,1,0:T(8,128)S(1)}, u32[]{:S(2)}, u32[]{:S(2)}) collective-permute-start(f32[4,16,256]{2,1,0:T(8,128)S(1)} %get-tuple-element.52), channel_id=1, source_target_pairs={{0,8},{8,0},{16,24},{24,16},{1,9},{9,1},{17,25},{25,17},{2,10},{10... | collective-permute-start | bytes 196616 | tf_op jit(solution)/shard_map/ppermute | solution.py:569

commit v6 on v5

--- a/solution.py
+++ b/solution.py
@@ -11,9 +11,9 @@
 REACH = 4
 SCALE = 5040.0
 WHOLE_SIDE = (8064.0, -1008.0, 128.0, -9.0)
-EARLY_SPEEDS, INNER_SPEEDS = 2, 2
-EARLY_EXTRA, LATE_EXTRA = 16, 8
-INWARD_ORDER, OUTWARD_ORDER = [2, 3, 1], [1, 2, 3]
+EARLY_SPEEDS, INNER_SPEEDS = REACH // 2, REACH // 2
+EARLY_EXTRA = 8
+INWARD_ORDER, OUTWARD_ORDER = [2, 3, 1], [2, 3, 1]
 F32 = jnp.float32
 BF16 = jnp.bfloat16
 VMEM_LIMIT = 32 * 1024 * 1024
@@ -110,8 +110,11 @@
         speed = speeds[at]
         packet[layer_rows(layer, size_y)] = fields[at]
         packet[layer_rows(REACH + layer, size_y)] = speed * speed * adjoints[at]
-        if layer < EARLY_SPEEDS:
-            packet[layer_rows(2 * REACH + layer, size_y)] = speed
+    parity = lax.rem(lax.axis_index("shot"), 2)
+    for number in range(EARLY_SPEEDS):
+        layer = parity * EARLY_SPEEDS + number
+        at = layer + odd * (REACH - 1 - 2 * layer)
+        packet[layer_rows(2 * REACH + number, size_y)] = speeds[at]
     packet[(2 * REACH + EARLY_SPEEDS) * size_y :, :] = fields[0, 0:EARLY_EXTRA, :]
 
 
@@ -181,9 +184,6 @@
             field = 2.0 * adjoint[place] - late_held[place] + laplace
             adjoint_mid[mine + at] = field
             put(REACH + at, speed_sq * field)
-    for layer in range(EARLY_SPEEDS, REACH):
-        put_out(2 * REACH + layer - EARLY_SPEEDS, speeds[layer])
-    late_out[(3 * REACH - EARLY_SPEEDS) * size_y :, :] = speeds[0, 0:LATE_EXTRA, :]
     for layer in range(REACH):
         early_in[layer] = present[REACH + layer]
         early_in[REACH + layer] = scaled[REACH + layer]
@@ -344,7 +344,7 @@
 
 
 def middle_kernel(shots, speeds, halo, inner, outer_part, forward, backward, outer, step, *rest):
-    outputs, (gradient,) = rest[:shots], rest[shots:]
+    shared, outputs, (gradient,) = rest[0], rest[1 : 1 + shots], rest[1 + shots :]
     size_y = speeds.shape[1]
     for at in range(REACH):
         speed = speeds[at]
@@ -361,6 +361,8 @@
         speed = speeds[REACH + at]
         gradient[at] = 2.0 * speed * (back * inner[at] + inner[REACH + at] * ahead)
     scatter_rows(gradient, outputs, shots, True)
+    for number in range(EARLY_SPEEDS):
+        shared[number] = halo[layer_rows(2 * REACH + number, size_y)]
 
 
 def second_kernel(bands, outer, step, forward, backward, after):
@@ -377,7 +379,9 @@
         )
 
 
-def outer_kernel(shots, relayed, own_out, speeds, outer, after, halo_early, points_out, *rest):
+def outer_kernel(
+    shots, relayed, own_out, speeds, outer, after, shared, passed, points_out, *rest
+):
     lates, rest = rest[: 1 + relayed], rest[1 + relayed :]
     outputs, (next_mid, next_scaled, gradient) = rest[:shots], rest[shots:]
 
@@ -386,11 +390,10 @@
 
     size_y = speeds.shape[1]
     own = [own_out[layer_rows(i, size_y)] for i in range(2 * REACH)]
-    for at in range(REACH):
-        if at < EARLY_SPEEDS:
-            speed = halo_early[layer_rows(2 * REACH + at, size_y)]
-        else:
-            speed = late(2 * REACH + at - EARLY_SPEEDS)
+    parity = lax.rem(lax.axis_index("shot"), 2)
+    for at in range(REACH):
+        mine, number = parity == at // EARLY_SPEEDS, at % EARLY_SPEEDS
+        speed = jnp.where(mine, shared[number], passed[number])
         next_mid[at], next_scaled[at] = next_halo(at, speed, late, own, points_out)
     for at in range(REACH):
         ahead = after[at] + across(at, lambda i: next_mid[i])
@@ -404,12 +407,12 @@
     refs[-1][...] = functools.reduce(lambda a, b: a + b, [ref[...] for ref in refs[:-1]])
 
 
-def sum_kernel(inner, *refs):
+def sum_kernel(inner, inner_near, *refs):
     outers, out = refs[:-1], refs[-1]
     odd = lax.rem(lax.axis_index("space"), 2)
     for at in range(REACH):
         out[placed(at, True, odd)] = functools.reduce(lambda a, b: a + b, [r[at] for r in outers])
-        out[placed(at, False, odd)] = inner[at]
+        out[placed(at, False, odd)] = inner[at] + inner_near[at]
 
 
 def call(kernel, shapes, in_spaces, scratch, flops, moved):
@@ -448,9 +451,9 @@
     residual_trace,
 ):
     slab, size_y, size_z = courant.shape
-    if slab != 2 * REACH:
+    shots = lax.axis_size("shot")
+    if slab != 2 * REACH or shots % 2:
         raise ValueError("unsupported slab")
-    shots = lax.axis_size("shot")
     devices = lax.axis_size("space")
     plane = size_y * size_z
     part_rows = size_y // shots
@@ -475,7 +478,6 @@
     pulse = jnp.concatenate([wavelet[0]] + place).reshape(1, 4)
 
     early_layers = 2 * REACH + EARLY_SPEEDS
-    late_layers = 3 * REACH - EARLY_SPEEDS
     early_out = call(
         early_kernel,
         (early_layers * size_y + EARLY_EXTRA, size_z),
@@ -491,7 +493,7 @@
         local_kernel,
         [stack(slab)] * 4
         + [bands, stack(2 * REACH + INNER_SPEEDS)]
-        + [(late_layers * size_y + LATE_EXTRA, size_z)]
+        + [(2 * REACH * size_y, size_z)]
         + [stack(3 * REACH - INNER_SPEEDS)],
         [pl.ANY] + [V] * 4 + [H],
         [held(slab)] * 3 + [pltpu.SemaphoreType.DMA(())],
@@ -536,9 +538,9 @@
     if relayed:
         first_hop, inner = lax.optimization_barrier((first_hop, inner))
         halo_lates.append(lax.ppermute(first_hop, "space", [(7, 4), (0, 3)]))
-    outer, step, *inner_parts = call(
+    outer, step, shared, *inner_parts = call(
         functools.partial(middle_kernel, shots),
-        [stack(2 * REACH)] * 2 + [(REACH, part_rows, size_z)] * shots,
+        [stack(2 * REACH)] * 2 + [stack(EARLY_SPEEDS)] + [(REACH, part_rows, size_z)] * shots,
         [V] * 6,
         [held(REACH)],
         MIDDLE_COST,
@@ -547,30 +549,43 @@
     after = call(second_kernel, stack(2 * REACH), [V] * 5, [], SECOND_COST, SMALL)(
         bands, outer, step, forward, backward
     )
-    shifts = [
-        [[(i, i ^ k) for i in range(shots)] for k in exchange_order(shots, inward)]
-        for inward in (True, False)
+    passed = lax.ppermute(shared, "shot", [(i, i ^ 1) for i in range(shots)])
+
+    def exchanged(part, shift):
+        return lax.ppermute(part, "shot", [(i, i ^ shift) for i in range(shots)])
+
+    order = exchange_order(shots, True)
+    inner_near = inner_parts[order.index(1)]
+    early_parts = [
+        exchanged(part, shift) if shift else part
+        for part, shift in zip(inner_parts, order)
+        if shift != 1
     ]
-    inner_parts = inner_parts[:1] + [
-        lax.ppermute(inner_parts[k], "shot", shifts[0][k]) for k in range(1, shots)
-    ]
-    inner_sum = call(add_kernel, (REACH, part_rows, size_z), [V] * shots, [], LARGE, SMALL)(
-        *inner_parts
-    )
+    inner_sum = call(
+        add_kernel, (REACH, part_rows, size_z), [V] * (shots - 1), [], LARGE, SMALL
+    )(*early_parts)
+    order = exchange_order(shots, False)
     outer_parts = call(
         functools.partial(outer_kernel, shots, relayed),
         [(REACH, part_rows, size_z)] * shots,
-        [V] * (6 + len(halo_lates)),
+        [V] * (7 + len(halo_lates)),
         [held(REACH)] * 3,
         SMALL,
         SMALL,
-    )(early_out, speeds, outer, after, halo_out, points_out, *halo_lates)
-    outer_parts = list(outer_parts[:1]) + [
-        lax.ppermute(outer_parts[k], "shot", shifts[1][k]) for k in range(1, shots)
+    )(early_out, speeds, outer, after, shared, passed, points_out, *halo_lates)
+    inner_near, *outer_parts = lax.optimization_barrier((inner_near, *outer_parts))
+    inner_near = exchanged(inner_near, 1)
+    outer_parts = [
+        exchanged(part, shift) if shift else part for part, shift in zip(outer_parts, order)
     ]
-    return call(sum_kernel, (slab, part_rows, size_z), [V] * (1 + shots), [], SMALL, SMALL)(
-        inner_sum, *outer_parts
-    )
+    return call(
+        sum_kernel,
+        (slab, part_rows, size_z),
+        [V] * (2 + shots),
+        [],
+        SMALL,
+        SMALL,
+    )(inner_sum, inner_near, *outer_parts)
 
 
 def solution(mesh):

time: 40 us -> 39.6 us (0.990)
  waiting for transfers between devices: 12.5 us -> 9.53 us
  starting transfers between devices: 16.3 us -> 18.9 us
    ppermute x1, waiting for transfers between devices: 2.7 us -> 0.5 us  [on_device(): halo_lates.append(lax.ppermute(first_hop, 'space', [(7, 4), (0, 3)]))]
    ppermute x6 -> x7, starting transfers between devices: 8.48 us -> 10.5 us  [the longest x6 8.87 us: exchanged(): return lax.ppermute(part, 'shot', [(i, i ^ shift) for i in range(shots)])]
    ppermute x6 -> x7, waiting for transfers between devices: 5.17 us -> 4.45 us  [the longest x6 3.92 us: exchanged(): return lax.ppermute(part, 'shot', [(i, i ^ shift) for i in range(shots)])]
    ppermute x1, starting transfers between devices: 3.75 us -> 4.34 us  [on_device(): halo_in = lax.ppermute(early_in, 'space', in_pairs)]
  transfers between devices with their start and end apart: 12 -> 13, of which waited for: 5 -> 7; matrix products, arithmetic and copies ran while one was open for 0% -> 0% of each run, Pallas kernels for 15% -> 15%
where the time goes in v6:
time: 39.6 us; the launch traced here: 39.4 us
  starting transfers between devices  18.9 us (48%)
  waiting for transfers between devices  9.53 us (24%)
  Pallas kernels  8.02 us (20%)
  between operations  1.47 us (4%)
  local copies, waits for them, and re-layouts  1.35 us (3%)
    ppermute x6, starting transfers between devices, exchanged(): return lax.ppermute(part, 'shot', [(i, i ^ shift) for i in range(shots)])  8.87 us
    ppermute x1, waiting for transfers between devices, on_device(): first_hop = lax.ppermute(late_out, 'space', [(3, 7), (4, 0)])  4.57 us
    ppermute x1, starting transfers between devices, on_device(): halo_in = lax.ppermute(early_in, 'space', in_pairs)  4.34 us
    ppermute x6, waiting for transfers between devices, exchanged(): return lax.ppermute(part, 'shot', [(i, i ^ shift) for i in range(shots)])  3.92 us
    pallas_call x1, Pallas kernels, on_device(): call(local_kernel, [stack(slab)] * 4 + [bands, stack(2 * REACH + INNER_SP...  2.61 us
    pallas_call x1, Pallas kernels, on_device(): call(inner_kernel, [stack(2 * REACH), stack(3 * REACH)] + [stack(2 * REAC...  1.76 us
    ppermute x1, starting transfers between devices, on_device(): passed = lax.ppermute(shared, 'shot', [(i, i ^ 1) for i in range(shots)])  1.64 us
    unnamed x16, local copies, waits for them, and re-layouts  1.35 us
  transfers between devices with their start and end apart: 13, of which 7 were waited for; matrix products, arithmetic and copies ran while one was open for 0% of the time, Pallas kernels for 15%

profile of v6, /device:TPU:0, one launch (start us, length us, event | category | flops | bytes accessed | tf_op | source)
XLA Modules:
  0.0 39.4 jit_solution(5413057158695299278)
XLA Ops:
  0.0 0.0 copy-start
  0.0 0.0 copy-start.1
  0.0 0.0 copy-start.2
  0.0 0.0 copy-start.6
  0.0 1.3 %shard_map.109.sent_first.own_out = f32[648,256]{1,0:T(8,128)S(1)} custom-call(f32[8,64,256]{2,1,0:T(8,128)} %courant.3, f32[8,64,256]{2,1,0:T(8,128)} %bitcast.10, f32[8,64,256]{2,1,0:T(8,128)} %bitcast.12), custom_call_target="tpu_custom_call" | custom-call | flops 1000000 | bytes 1000000 | tf_op jit(solution)/shard_map/pallas_call | solution.py:481
  1.4 0.7 %collective-permute-start = (f32[648,256]{1,0:T(8,128)S(1)}, f32[648,256]{1,0:T(8,128)S(1)}, u32[]{:S(2)}, u32[]{:S(2)}) collective-permute-start(f32[648,256]{1,0:T(8,128)S(1)} %shard_map.109.sent_first.own_out), channel_id=1, source_target_pairs={{1,2},{3,4},{5,6},{2,1},{4,3},{6,5},{9,10},{11,12},{13,14},{10,9},... | collective-permute-start | bytes 1990664 | tf_op jit(solution)/shard_map/ppermute | solution.py:489
  2.1 0.0 copy-done
  2.1 0.0 copy-done.1
  2.1 0.0 copy-done.2
  2.1 0.0 copy-done.6
  2.1 0.0 copy-start.5
  2.1 2.6 %shard_map.110 = (f32[8,64,256]{2,1,0:T(8,128)S(1)}, f32[8,64,256]{2,1,0:T(8,128)S(1)}, f32[8,64,256]{2,1,0:T(8,128)S(1)}, f32[8,64,256]{2,1,0:T(8,128)S(1)}, bf...) custom-call(f32[648,256]{1,0:T(8,128)S(1)} %shard_map.109.sent_first, ...), custom_call_target="tpu_custom_call" | custom-call | flops 10000000000 | bytes 1000000 | tf_op jit(solution)/shard_map/pallas_call | solution.py:492
  4.7 4.3 %collective-permute-start.2 = (f32[10,64,256]{2,1,0:T(8,128)S(1)}, f32[10,64,256]{2,1,0:T(8,128)S(1)}, u32[]{:S(2)}, u32[]{:S(2)}) collective-permute-start(f32[10,64,256]{2,1,0:T(8,128)S(1)} %get-tuple-element.38.own_in), channel_id=1, source_target_pairs={{0,1},{1,0},{2,3},{3,2},{4,5},{5,4},{6,7},{7,6},{8,9},{9,8},{10,11... | collective-permute-start | bytes 1966088 | tf_op jit(solution)/shard_map/ppermute | solution.py:503
  9.1 0.1 collective-permute-start.3
  9.2 1.3 %collective-permute-start.1 = (f32[512,256]{1,0:T(8,128)S(1)}, f32[512,256]{1,0:T(8,128)S(1)}, u32[]{:S(2)}, u32[]{:S(2)}) collective-permute-start(f32[512,256]{1,0:T(8,128)S(1)} %get-tuple-element.37.late_out), channel_id=1, source_target_pairs={{3,7},{4,0},{11,15},{12,8},{19,23},{20,16},{27,31},{28,24}} | collective-permute-start | bytes 1572872 | tf_op jit(solution)/shard_map/ppermute | solution.py:506
  10.4 0.7 %collective-permute-start.7 = (f32[512,256]{1,0:T(8,128)S(1)}, f32[512,256]{1,0:T(8,128)S(1)}, u32[]{:S(2)}, u32[]{:S(2)}) collective-permute-start(f32[512,256]{1,0:T(8,128)S(1)} %get-tuple-element.37.late_out), channel_id=1, source_target_pairs={{1,2},{5,6},{2,1},{6,5},{9,10},{13,14},{10,9},{14,13},{17,18},{21,... | collective-permute-start | bytes 1572872 | tf_op jit(solution)/shard_map/ppermute | solution.py:507
  12.4 0.0 copy-start.7
  12.5 0.6 %copy-done.7 = f32[1,2]{1,0:T(1,128)S(1)} copy-done((f32[1,2]{1,0:T(1,128)S(1)}, f32[1,2]{1,0:T(1,128)}, u32[]{:S(2)}) %copy-start.7) | copy-done | bytes 32
  13.1 0.1 maximum_bitcast_fusion.pulse
  13.2 0.0 collective-permute-done.2.halo_early
  13.2 0.0 collective-permute-done.3.halo_late
  13.2 0.0 copy-start.3
  13.2 0.0 copy-start.4
  13.2 0.0 copy-done.5
  13.2 0.7 %copy-done.3 = f32[1,256,2]{1,2,0:T(2,128)S(1)} copy-done((f32[1,256,2]{1,2,0:T(2,128)S(1)}, f32[1,256,2]{1,2,0:T(2,128)}, u32[]{:S(2)}) %copy-start.3) | copy-done | bytes 2072
  13.9 0.0 copy-done.4
  13.9 1.8 %shard_map.111 = (f32[8,64,256]{2,1,0:T(8,128)S(1)}, f32[12,64,256]{2,1,0:T(8,128)S(1)}, f32[8,64,256]{2,1,0:T(8,128)S(1)}, f32[8,64,256]{2,1,0:T(8,128)S(1)}, f32[8,64,256]{2,1,0:T(8,128)S(1)}) custom-call(f32[1,4]{1,0:T(1,128)S(1)} %maximum_bitcast_fusion.pulse, s32[1,256]{1,0:T(1,128)S(1)} %copy-done.4, s32[1,256]{1,0:T(1,128)S(1)} %copy-done.5, ...), custom_call_target="tpu_custom_call" | custom-call | flops 1000000 | bytes 1000000 | tf_op jit(solution)/shard_map/pallas_call | solution.py:510
  15.7 4.6 %collective-permute-done.1 = f32[512,256]{1,0:T(8,128)S(1)} collective-permute-done((f32[512,256]{1,0:T(8,128)S(1)}, f32[512,256]{1,0:T(8,128)S(1)}, u32[]{:S(2)}, u32[]{:S(2)}) %collective-permute-start.1) | collective-permute-done | bytes 524320 | tf_op jit(solution)/shard_map/ppermute | solution.py:506
  20.2 1.3 %collective-permute-start.8 = (f32[512,256]{1,0:T(8,128)S(1)}, f32[512,256]{1,0:T(8,128)S(1)}, u32[]{:S(2)}, u32[]{:S(2)}) collective-permute-start(f32[512,256]{1,0:T(8,128)S(1)} %collective-permute-done.1), channel_id=1, source_target_pairs={{7,4},{0,3},{15,12},{8,11},{23,20},{16,19},{31,28},{24,27}} | collective-permute-start | bytes 1572872 | tf_op jit(solution)/shard_map/ppermute | solution.py:540
  21.5 0.0 collective-permute-done.halo
  21.6 0.4 %shard_map.112 = (f32[8,64,256]{2,1,0:T(8,128)S(1)}, f32[8,64,256]{2,1,0:T(8,128)S(1)}, f32[2,64,256]{2,1,0:T(8,128)S(1)}, f32[4,16,256]{2,1,0:T(8,128)S(1)}, f3...) custom-call(f32[8,64,256]{2,1,0:T(8,128)S(1)} %get-tuple-element.36.speeds, ...), custom_call_target="tpu_custom_call" | custom-call | flops 8000000000 | bytes 1000000 | tf_op jit(solution)/shard_map/pallas_call | solution.py:541
  22.0 1.6 %collective-permute-start.6 = (f32[2,64,256]{2,1,0:T(8,128)S(1)}, f32[2,64,256]{2,1,0:T(8,128)S(1)}, u32[]{:S(2)}, u32[]{:S(2)}) collective-permute-start(f32[2,64,256]{2,1,0:T(8,128)S(1)} %get-tuple-element.55.shared), channel_id=1, source_target_pairs={{0,8},{8,0},{16,24},{24,16},{1,9},{9,1},{17,25},{25,17},{2,10},{10... | collective-permute-start | bytes 393224 | tf_op jit(solution)/shard_map/ppermute | solution.py:552
  23.6 2.6 %collective-permute-start.4 = (f32[4,16,256]{2,1,0:T(8,128)S(1)}, f32[4,16,256]{2,1,0:T(8,128)S(1)}, u32[]{:S(2)}, u32[]{:S(2)}) collective-permute-start(f32[4,16,256]{2,1,0:T(8,128)S(1)} %get-tuple-element.50), channel_id=1, source_target_pairs={{0,16},{8,24},{16,0},{24,8},{1,17},{9,25},{17,1},{25,9},{2,18},{10... | collective-permute-start | bytes 196616 | tf_op jit(solution)/shard_map/ppermute | solution.py:555
  26.2 0.2 collective-permute-start.5
  26.4 0.7 %shard_map.114.after = f32[8,64,256]{2,1,0:T(8,128)S(1)} custom-call(bf16[2,256,256]{2,1,0:T(8,128)(2,1)S(1)} %get-tuple-element.43.bands, f32[8,64,256]{2,1,0:T(8,128)S(1)} %get-tuple-element.53.outer, f32[8,64,256]{2,1,0:T(8,128)S(1)} %get-tuple-element.54.step, f32[8,64,256]{2,1,0:T(8,128)S(1)} %get-tuple-element.47.forward, ...), custom_call_target="tpu_custom_call" | custom-call | flops 1000000 | bytes 1000000 | tf_op jit(solution)/shard_map/pallas_call | solution.py:549
  27.2 0.0 collective-permute-done.7.rest_0_
  27.2 0.5 %collective-permute-done.6.passed = f32[2,64,256]{2,1,0:T(8,128)S(1)} collective-permute-done((f32[2,64,256]{2,1,0:T(8,128)S(1)}, f32[2,64,256]{2,1,0:T(8,128)S(1)}, u32[]{:S(2)}, u32[]{:S(2)}) %collective-permute-start.6) | collective-permute-done | bytes 131104 | tf_op jit(solution)/shard_map/ppermute | solution.py:552
  27.7 0.5 %collective-permute-done.8.rest_1_ = f32[512,256]{1,0:T(8,128)S(1)} collective-permute-done((f32[512,256]{1,0:T(8,128)S(1)}, f32[512,256]{1,0:T(8,128)S(1)}, u32[]{:S(2)}, u32[]{:S(2)}) %collective-permute-start.8) | collective-permute-done | bytes 524320 | tf_op jit(solution)/shard_map/ppermute | solution.py:540
  28.2 0.5 %shard_map.115 = (f32[4,16,256]{2,1,0:T(8,128)S(1)}, f32[4,16,256]{2,1,0:T(8,128)S(1)}, f32[4,16,256]{2,1,0:T(8,128)S(1)}, f32[4,16,256]{2,1,0:T(8,128)S(1)}) custom-call(f32[648,256]{1,0:T(8,128)S(1)} %shard_map.109.sent_first.own_out, f32[8,64,256]{2,1,0:T(8,128)S(1)} %get-tuple-element.36.speeds, f32[8,64,256]{2,1,0:T(8,128)S(1)} %get-tuple-element.53.outer, ...), custom_call_target="tpu_custom_call" | custom-call | flops 1000000 | bytes 1000000 | tf_op jit(solution)/shard_map/pallas_call | solution.py:568
  28.7 2.7 %collective-permute-start.10 = (f32[4,16,256]{2,1,0:T(8,128)S(1)}, f32[4,16,256]{2,1,0:T(8,128)S(1)}, u32[]{:S(2)}, u32[]{:S(2)}) collective-permute-start(f32[4,16,256]{2,1,0:T(8,128)S(1)} %get-tuple-element.64), channel_id=1, source_target_pairs={{0,16},{8,24},{16,0},{24,8},{1,17},{9,25},{17,1},{25,9},{2,18},{10... | collective-permute-start | bytes 196616 | tf_op jit(solution)/shard_map/ppermute | solution.py:555
  31.3 1.4 %collective-permute-start.11 = (f32[4,16,256]{2,1,0:T(8,128)S(1)}, f32[4,16,256]{2,1,0:T(8,128)S(1)}, u32[]{:S(2)}, u32[]{:S(2)}) collective-permute-start(f32[4,16,256]{2,1,0:T(8,128)S(1)} %get-tuple-element.65), channel_id=1, source_target_pairs={{0,24},{8,16},{16,8},{24,0},{1,25},{9,17},{17,9},{25,1},{2,26},{10... | collective-permute-start | bytes 196616 | tf_op jit(solution)/shard_map/ppermute | solution.py:555
  32.7 0.5 %collective-permute-start.12 = (f32[4,16,256]{2,1,0:T(8,128)S(1)}, f32[4,16,256]{2,1,0:T(8,128)S(1)}, u32[]{:S(2)}, u32[]{:S(2)}) collective-permute-start(f32[4,16,256]{2,1,0:T(8,128)S(1)} %get-tuple-element.66), channel_id=1, source_target_pairs={{0,8},{8,0},{16,24},{24,16},{1,9},{9,1},{17,25},{25,17},{2,10},{10... | collective-permute-start | bytes 196616 | tf_op jit(solution)/shard_map/ppermute | solution.py:555
  33.2 0.0 collective-permute-done.4.refs_1_
  33.2 1.5 %collective-permute-start.9 = (f32[4,16,256]{2,1,0:T(8,128)S(1)}, f32[4,16,256]{2,1,0:T(8,128)S(1)}, u32[]{:S(2)}, u32[]{:S(2)}) collective-permute-start(f32[4,16,256]{2,1,0:T(8,128)S(1)} %get-tuple-element.62), channel_id=1, source_target_pairs={{0,8},{8,0},{16,24},{24,16},{1,9},{9,1},{17,25},{25,17},{2,10},{10... | collective-permute-start | bytes 196616 | tf_op jit(solution)/shard_map/ppermute | solution.py:555
  34.7 0.0 collective-permute-done.5.refs_2_
  34.8 1.3 %collective-permute-done.10.refs_1_ = f32[4,16,256]{2,1,0:T(8,128)S(1)} collective-permute-done((f32[4,16,256]{2,1,0:T(8,128)S(1)}, f32[4,16,256]{2,1,0:T(8,128)S(1)}, u32[]{:S(2)}, u32[]{:S(2)}) %collective-permute-start.10) | collective-permute-done | bytes 65568 | tf_op jit(solution)/shard_map/ppermute | solution.py:555
  36.1 1.9 %collective-permute-done.11.refs_2_ = f32[4,16,256]{2,1,0:T(8,128)S(1)} collective-permute-done((f32[4,16,256]{2,1,0:T(8,128)S(1)}, f32[4,16,256]{2,1,0:T(8,128)S(1)}, u32[]{:S(2)}, u32[]{:S(2)}) %collective-permute-start.11) | collective-permute-done | bytes 65568 | tf_op jit(solution)/shard_map/ppermute | solution.py:555
  37.9 0.1 collective-permute-done.12.refs_3_
  38.0 0.7 %collective-permute-done.9.inner_near = f32[4,16,256]{2,1,0:T(8,128)S(1)} collective-permute-done((f32[4,16,256]{2,1,0:T(8,128)S(1)}, f32[4,16,256]{2,1,0:T(8,128)S(1)}, u32[]{:S(2)}, u32[]{:S(2)}) %collective-permute-start.9) | collective-permute-done | bytes 65568 | tf_op jit(solution)/shard_map/ppermute | solution.py:555
  38.7 0.7 %shard_map.116 = f32[8,16,256]{2,1,0:T(8,128)} custom-call(f32[4,16,256]{2,1,0:T(8,128)S(1)} %shard_map.113.inner, f32[4,16,256]{2,1,0:T(8,128)S(1)} %collective-permute-done.9.inner_near, f32[4,16,256]{2,1,0:T(8,128)S(1)} %get-tuple-element.63.refs_0_, f32[4,16,256]{2,1,0:T(8,128)S(1)} %collective-permute-done.10.refs_1_, ...), custom_call_target="tpu_custom_call" | custom-call | flops 1000000 | bytes 1000000 | tf_op jit(solution)/shard_map/pallas_call | solution.py:581
  (1 shorter events, 0.0 us)
Async XLA Ops:
  0.0 2.1 %copy-start = (f32[8,64,256]{2,1,0:T(8,128)S(1)}, f32[8,64,256]{2,1,0:T(8,128)}, u32[]{:S(2)}) copy-start(f32[8,64,256]{2,1,0:T(8,128)} %courant.3) | copy-start | bytes 1572868
  0.0 2.1 %copy-start.1 = (f32[1,8,64,256]{3,2,1,0:T(8,128)S(1)}, f32[1,8,64,256]{3,2,1,0:T(8,128)}, u32[]{:S(2)}) copy-start(f32[1,8,64,256]{3,2,1,0:T(8,128)} %param.13) | copy-start | bytes 1572868
  0.0 2.1 %copy-start.2 = (f32[1,8,64,256]{3,2,1,0:T(8,128)S(1)}, f32[1,8,64,256]{3,2,1,0:T(8,128)}, u32[]{:S(2)}) copy-start(f32[1,8,64,256]{3,2,1,0:T(8,128)} %param.15) | copy-start | bytes 1572868
  0.0 2.1 %copy-start.6 = (f32[1,8,64,256]{3,2,1,0:T(8,128)S(1)}, f32[1,8,64,256]{3,2,1,0:T(8,128)}, u32[]{:S(2)}) copy-start(f32[1,8,64,256]{3,2,1,0:T(8,128)} %param.12) | copy-start | bytes 1572868
  1.4 20.2 %collective-permute-start = (f32[648,256]{1,0:T(8,128)S(1)}, f32[648,256]{1,0:T(8,128)S(1)}, u32[]{:S(2)}, u32[]{:S(2)}) collective-permute-start(f32[648,256]{1,0:T(8,128)S(1)} %shard_map.109.sent_first.own_out), channel_id=1, source_target_pairs={{1,2},{3,4},{5,6},{2,1},{4,3},{6,5},{9,10},{11,12},{13,14},{10,9},... | collective-permute-start | bytes 1990664 | tf_op jit(solution)/shard_map/ppermute | solution.py:489
  2.1 11.1 %copy-start.5 = (s32[1,256]{1,0:T(1,128)S(1)}, s32[1,256]{1,0:T(1,128)}, u32[]{:S(2)}) copy-start(s32[1,256]{1,0:T(1,128)} %receiver_yz.1) | copy-start | bytes 3076
  4.7 8.4 %collective-permute-start.2 = (f32[10,64,256]{2,1,0:T(8,128)S(1)}, f32[10,64,256]{2,1,0:T(8,128)S(1)}, u32[]{:S(2)}, u32[]{:S(2)}) collective-permute-start(f32[10,64,256]{2,1,0:T(8,128)S(1)} %get-tuple-element.38.own_in), channel_id=1, source_target_pairs={{0,1},{1,0},{2,3},{3,2},{4,5},{5,4},{6,7},{7,6},{8,9},{9,8},{10,11... | collective-permute-start | bytes 1966088 | tf_op jit(solution)/shard_map/ppermute | solution.py:503
  9.1 4.1 %collective-permute-start.3 = (f32[10,64,256]{2,1,0:T(8,128)S(1)}, f32[10,64,256]{2,1,0:T(8,128)S(1)}, u32[]{:S(2)}, u32[]{:S(2)}) collective-permute-start(f32[10,64,256]{2,1,0:T(8,128)S(1)} %get-tuple-element.41.late_in), channel_id=1, source_target_pairs={{0,1},{1,0},{2,3},{3,2},{4,5},{5,4},{6,7},{7,6},{8,9},{9,8},{10,11... | collective-permute-start | bytes 1966088 | tf_op jit(solution)/shard_map/ppermute | solution.py:504
  9.2 11.1 %collective-permute-start.1 = (f32[512,256]{1,0:T(8,128)S(1)}, f32[512,256]{1,0:T(8,128)S(1)}, u32[]{:S(2)}, u32[]{:S(2)}) collective-permute-start(f32[512,256]{1,0:T(8,128)S(1)} %get-tuple-element.37.late_out), channel_id=1, source_target_pairs={{3,7},{4,0},{11,15},{12,8},{19,23},{20,16},{27,31},{28,24}} | collective-permute-start | bytes 1572872 | tf_op jit(solution)/shard_map/ppermute | solution.py:506
  10.4 16.7 %collective-permute-start.7 = (f32[512,256]{1,0:T(8,128)S(1)}, f32[512,256]{1,0:T(8,128)S(1)}, u32[]{:S(2)}, u32[]{:S(2)}) collective-permute-start(f32[512,256]{1,0:T(8,128)S(1)} %get-tuple-element.37.late_out), channel_id=1, source_target_pairs={{1,2},{5,6},{2,1},{6,5},{9,10},{13,14},{10,9},{14,13},{17,18},{21,... | collective-permute-start | bytes 1572872 | tf_op jit(solution)/shard_map/ppermute | solution.py:507
  12.4 0.7 %copy-start.7 = (f32[1,2]{1,0:T(1,128)S(1)}, f32[1,2]{1,0:T(1,128)}, u32[]{:S(2)}) copy-start(f32[1,2]{1,0:T(1,128)} %param.18) | copy-start | bytes 28
  13.2 0.7 %copy-start.3 = (f32[1,256,2]{1,2,0:T(2,128)S(1)}, f32[1,256,2]{1,2,0:T(2,128)}, u32[]{:S(2)}) copy-start(f32[1,256,2]{1,2,0:T(2,128)} %param.21) | copy-start | bytes 6148
  13.2 0.7 %copy-start.4 = (s32[1,256]{1,0:T(1,128)S(1)}, s32[1,256]{1,0:T(1,128)}, u32[]{:S(2)}) copy-start(s32[1,256]{1,0:T(1,128)} %receiver_x.1) | copy-start | bytes 3076
  20.2 8.0 %collective-permute-start.8 = (f32[512,256]{1,0:T(8,128)S(1)}, f32[512,256]{1,0:T(8,128)S(1)}, u32[]{:S(2)}, u32[]{:S(2)}) collective-permute-start(f32[512,256]{1,0:T(8,128)S(1)} %collective-permute-done.1), channel_id=1, source_target_pairs={{7,4},{0,3},{15,12},{8,11},{23,20},{16,19},{31,28},{24,27}} | collective-permute-start | bytes 1572872 | tf_op jit(solution)/shard_map/ppermute | solution.py:540
  22.0 5.7 %collective-permute-start.6 = (f32[2,64,256]{2,1,0:T(8,128)S(1)}, f32[2,64,256]{2,1,0:T(8,128)S(1)}, u32[]{:S(2)}, u32[]{:S(2)}) collective-permute-start(f32[2,64,256]{2,1,0:T(8,128)S(1)} %get-tuple-element.55.shared), channel_id=1, source_target_pairs={{0,8},{8,0},{16,24},{24,16},{1,9},{9,1},{17,25},{25,17},{2,10},{10... | collective-permute-start | bytes 393224 | tf_op jit(solution)/shard_map/ppermute | solution.py:552
  23.6 9.6 %collective-permute-start.4 = (f32[4,16,256]{2,1,0:T(8,128)S(1)}, f32[4,16,256]{2,1,0:T(8,128)S(1)}, u32[]{:S(2)}, u32[]{:S(2)}) collective-permute-start(f32[4,16,256]{2,1,0:T(8,128)S(1)} %get-tuple-element.50), channel_id=1, source_target_pairs={{0,16},{8,24},{16,0},{24,8},{1,17},{9,25},{17,1},{25,9},{2,18},{10... | collective-permute-start | bytes 196616 | tf_op jit(solution)/shard_map/ppermute | solution.py:555
  26.2 8.6 %collective-permute-start.5 = (f32[4,16,256]{2,1,0:T(8,128)S(1)}, f32[4,16,256]{2,1,0:T(8,128)S(1)}, u32[]{:S(2)}, u32[]{:S(2)}) collective-permute-start(f32[4,16,256]{2,1,0:T(8,128)S(1)} %get-tuple-element.51), channel_id=1, source_target_pairs={{0,24},{8,16},{16,8},{24,0},{1,25},{9,17},{17,9},{25,1},{2,26},{10... | collective-permute-start | bytes 196616 | tf_op jit(solution)/shard_map/ppermute | solution.py:555
  28.7 7.4 %collective-permute-start.10 = (f32[4,16,256]{2,1,0:T(8,128)S(1)}, f32[4,16,256]{2,1,0:T(8,128)S(1)}, u32[]{:S(2)}, u32[]{:S(2)}) collective-permute-start(f32[4,16,256]{2,1,0:T(8,128)S(1)} %get-tuple-element.64), channel_id=1, source_target_pairs={{0,16},{8,24},{16,0},{24,8},{1,17},{9,25},{17,1},{25,9},{2,18},{10... | collective-permute-start | bytes 196616 | tf_op jit(solution)/shard_map/ppermute | solution.py:555
  31.3 6.6 %collective-permute-start.11 = (f32[4,16,256]{2,1,0:T(8,128)S(1)}, f32[4,16,256]{2,1,0:T(8,128)S(1)}, u32[]{:S(2)}, u32[]{:S(2)}) collective-permute-start(f32[4,16,256]{2,1,0:T(8,128)S(1)} %get-tuple-element.65), channel_id=1, source_target_pairs={{0,24},{8,16},{16,8},{24,0},{1,25},{9,17},{17,9},{25,1},{2,26},{10... | collective-permute-start | bytes 196616 | tf_op jit(solution)/shard_map/ppermute | solution.py:555
  32.7 5.3 %collective-permute-start.12 = (f32[4,16,256]{2,1,0:T(8,128)S(1)}, f32[4,16,256]{2,1,0:T(8,128)S(1)}, u32[]{:S(2)}, u32[]{:S(2)}) collective-permute-start(f32[4,16,256]{2,1,0:T(8,128)S(1)} %get-tuple-element.66), channel_id=1, source_target_pairs={{0,8},{8,0},{16,24},{24,16},{1,9},{9,1},{17,25},{25,17},{2,10},{10... | collective-permute-start | bytes 196616 | tf_op jit(solution)/shard_map/ppermute | solution.py:555
  33.2 5.5 %collective-permute-start.9 = (f32[4,16,256]{2,1,0:T(8,128)S(1)}, f32[4,16,256]{2,1,0:T(8,128)S(1)}, u32[]{:S(2)}, u32[]{:S(2)}) collective-permute-start(f32[4,16,256]{2,1,0:T(8,128)S(1)} %get-tuple-element.62), channel_id=1, source_target_pairs={{0,8},{8,0},{16,24},{24,16},{1,9},{9,1},{17,25},{25,17},{2,10},{10... | collective-permute-start | bytes 196616 | tf_op jit(solution)/shard_map/ppermute | solution.py:555

commit v7 on v6

--- a/solution.py
+++ b/solution.py
@@ -549,7 +549,13 @@
     after = call(second_kernel, stack(2 * REACH), [V] * 5, [], SECOND_COST, SMALL)(
         bands, outer, step, forward, backward
     )
-    passed = lax.ppermute(shared, "shot", [(i, i ^ 1) for i in range(shots)])
+    passed = lax.ppermute(
+        lax.slice_in_dim(halo_out, 2 * REACH * size_y, early_layers * size_y).reshape(
+            stack(EARLY_SPEEDS)
+        ),
+        "shot",
+        [(i, i ^ 1) for i in range(shots)],
+    )
 
     def exchanged(part, shift):
         return lax.ppermute(part, "shot", [(i, i ^ shift) for i in range(shots)])

time: 39.6 us -> 39.4 us (level)
    ppermute x1, waiting for transfers between devices: 0.53 us -> 0.06 us  [on_device(): lax.ppermute(lax.slice_in_dim(halo_out, 2 * REACH * size_y, early_layers...]
  transfers between devices with their start and end apart: 13 -> 13, of which waited for: 7 -> 6; matrix products, arithmetic and copies ran while one was open for 0% -> 0% of each run, Pallas kernels for 15% -> 15%
where the time goes in v7:
time: 39.4 us; the launch traced here: 39.2 us
  starting transfers between devices  19 us (48%)
  waiting for transfers between devices  9.3 us (24%)
  Pallas kernels  8.02 us (20%)
  between operations  1.47 us (4%)
  local copies, waits for them, and re-layouts  1.36 us (3%)
    ppermute x6, starting transfers between devices, exchanged(): return lax.ppermute(part, 'shot', [(i, i ^ shift) for i in range(shots)])  8.91 us
    ppermute x1, waiting for transfers between devices, on_device(): first_hop = lax.ppermute(late_out, 'space', [(3, 7), (4, 0)])  4.57 us
    ppermute x1, starting transfers between devices, on_device(): halo_in = lax.ppermute(early_in, 'space', in_pairs)  4.34 us
    ppermute x6, waiting for transfers between devices, exchanged(): return lax.ppermute(part, 'shot', [(i, i ^ shift) for i in range(shots)])  3.78 us
    pallas_call x1, Pallas kernels, on_device(): call(local_kernel, [stack(slab)] * 4 + [bands, stack(2 * REACH + INNER_SP...  2.61 us
    pallas_call x1, Pallas kernels, on_device(): call(inner_kernel, [stack(2 * REACH), stack(3 * REACH)] + [stack(2 * REAC...  1.76 us
    ppermute x1, starting transfers between devices, on_device(): lax.ppermute(lax.slice_in_dim(halo_out, 2 * REACH * size_y, early_layers...  1.64 us
    unnamed x16, local copies, waits for them, and re-layouts  1.35 us
  transfers between devices with their start and end apart: 13, of which 6 were waited for; matrix products, arithmetic and copies ran while one was open for 0% of the time, Pallas kernels for 15%

profile of v7, /device:TPU:0, one launch (start us, length us, event | category | flops | bytes accessed | tf_op | source)
XLA Modules:
  0.0 39.2 jit_solution(10958803300553891110)
XLA Ops:
  0.0 0.0 copy-start
  0.0 0.0 copy-start.1
  0.0 0.0 copy-start.2
  0.0 0.0 copy-start.6
  0.0 1.3 %shard_map.109.sent_first.own_out = f32[648,256]{1,0:T(8,128)S(1)} custom-call(f32[8,64,256]{2,1,0:T(8,128)} %courant.3, f32[8,64,256]{2,1,0:T(8,128)} %bitcast.11, f32[8,64,256]{2,1,0:T(8,128)} %bitcast.13), custom_call_target="tpu_custom_call" | custom-call | flops 1000000 | bytes 1000000 | tf_op jit(solution)/shard_map/pallas_call | solution.py:481
  1.4 0.7 %collective-permute-start = (f32[648,256]{1,0:T(8,128)S(1)}, f32[648,256]{1,0:T(8,128)S(1)}, u32[]{:S(2)}, u32[]{:S(2)}) collective-permute-start(f32[648,256]{1,0:T(8,128)S(1)} %shard_map.109.sent_first.own_out), channel_id=1, source_target_pairs={{1,2},{3,4},{5,6},{2,1},{4,3},{6,5},{9,10},{11,12},{13,14},{10,9},... | collective-permute-start | bytes 1990664 | tf_op jit(solution)/shard_map/ppermute | solution.py:489
  2.1 0.0 copy-done
  2.1 0.0 copy-done.1
  2.1 0.0 copy-done.2
  2.1 0.0 copy-done.6
  2.1 0.0 copy-start.5
  2.1 2.6 %shard_map.110 = (f32[8,64,256]{2,1,0:T(8,128)S(1)}, f32[8,64,256]{2,1,0:T(8,128)S(1)}, f32[8,64,256]{2,1,0:T(8,128)S(1)}, f32[8,64,256]{2,1,0:T(8,128)S(1)}, bf...) custom-call(f32[648,256]{1,0:T(8,128)S(1)} %shard_map.109.sent_first, ...), custom_call_target="tpu_custom_call" | custom-call | flops 10000000000 | bytes 1000000 | tf_op jit(solution)/shard_map/pallas_call | solution.py:492
  4.7 4.3 %collective-permute-start.2 = (f32[10,64,256]{2,1,0:T(8,128)S(1)}, f32[10,64,256]{2,1,0:T(8,128)S(1)}, u32[]{:S(2)}, u32[]{:S(2)}) collective-permute-start(f32[10,64,256]{2,1,0:T(8,128)S(1)} %get-tuple-element.38.own_in), channel_id=1, source_target_pairs={{0,1},{1,0},{2,3},{3,2},{4,5},{5,4},{6,7},{7,6},{8,9},{9,8},{10,11... | collective-permute-start | bytes 1966088 | tf_op jit(solution)/shard_map/ppermute | solution.py:503
  9.1 0.1 collective-permute-start.3
  9.2 1.3 %collective-permute-start.1 = (f32[512,256]{1,0:T(8,128)S(1)}, f32[512,256]{1,0:T(8,128)S(1)}, u32[]{:S(2)}, u32[]{:S(2)}) collective-permute-start(f32[512,256]{1,0:T(8,128)S(1)} %get-tuple-element.37.late_out), channel_id=1, source_target_pairs={{3,7},{4,0},{11,15},{12,8},{19,23},{20,16},{27,31},{28,24}} | collective-permute-start | bytes 1572872 | tf_op jit(solution)/shard_map/ppermute | solution.py:506
  10.4 0.7 %collective-permute-start.7 = (f32[512,256]{1,0:T(8,128)S(1)}, f32[512,256]{1,0:T(8,128)S(1)}, u32[]{:S(2)}, u32[]{:S(2)}) collective-permute-start(f32[512,256]{1,0:T(8,128)S(1)} %get-tuple-element.37.late_out), channel_id=1, source_target_pairs={{1,2},{5,6},{2,1},{6,5},{9,10},{13,14},{10,9},{14,13},{17,18},{21,... | collective-permute-start | bytes 1572872 | tf_op jit(solution)/shard_map/ppermute | solution.py:507
  12.4 0.0 copy-start.7
  12.5 0.6 %copy-done.7 = f32[1,2]{1,0:T(1,128)S(1)} copy-done((f32[1,2]{1,0:T(1,128)S(1)}, f32[1,2]{1,0:T(1,128)}, u32[]{:S(2)}) %copy-start.7) | copy-done | bytes 32
  13.1 0.1 maximum_bitcast_fusion.pulse
  13.2 0.0 collective-permute-done.2.halo_early
  13.2 0.0 collective-permute-done.3.halo_late
  13.2 0.0 copy-start.3
  13.2 0.0 copy-start.4
  13.2 0.0 copy-done.5
  13.2 0.7 %copy-done.3 = f32[1,256,2]{1,2,0:T(2,128)S(1)} copy-done((f32[1,256,2]{1,2,0:T(2,128)S(1)}, f32[1,256,2]{1,2,0:T(2,128)}, u32[]{:S(2)}) %copy-start.3) | copy-done | bytes 2072
  13.9 0.0 copy-done.4
  13.9 1.8 %shard_map.111 = (f32[8,64,256]{2,1,0:T(8,128)S(1)}, f32[12,64,256]{2,1,0:T(8,128)S(1)}, f32[8,64,256]{2,1,0:T(8,128)S(1)}, f32[8,64,256]{2,1,0:T(8,128)S(1)}, f32[8,64,256]{2,1,0:T(8,128)S(1)}) custom-call(f32[1,4]{1,0:T(1,128)S(1)} %maximum_bitcast_fusion.pulse, s32[1,256]{1,0:T(1,128)S(1)} %copy-done.4, s32[1,256]{1,0:T(1,128)S(1)} %copy-done.5, ...), custom_call_target="tpu_custom_call" | custom-call | flops 1000000 | bytes 1000000 | tf_op jit(solution)/shard_map/pallas_call | solution.py:510
  15.7 4.6 %collective-permute-done.1 = f32[512,256]{1,0:T(8,128)S(1)} collective-permute-done((f32[512,256]{1,0:T(8,128)S(1)}, f32[512,256]{1,0:T(8,128)S(1)}, u32[]{:S(2)}, u32[]{:S(2)}) %collective-permute-start.1) | collective-permute-done | bytes 524320 | tf_op jit(solution)/shard_map/ppermute | solution.py:506
  20.2 1.3 %collective-permute-start.8 = (f32[512,256]{1,0:T(8,128)S(1)}, f32[512,256]{1,0:T(8,128)S(1)}, u32[]{:S(2)}, u32[]{:S(2)}) collective-permute-start(f32[512,256]{1,0:T(8,128)S(1)} %collective-permute-done.1), channel_id=1, source_target_pairs={{7,4},{0,3},{15,12},{8,11},{23,20},{16,19},{31,28},{24,27}} | collective-permute-start | bytes 1572872 | tf_op jit(solution)/shard_map/ppermute | solution.py:540
  21.5 0.0 collective-permute-done.halo
  21.6 1.6 %collective-permute-start.6 = (f32[2,64,256]{2,1,0:T(8,128)S(1)}, f32[2,64,256]{2,1,0:T(8,128)S(1)}, u32[]{:S(2)}, u32[]{:S(2)}) collective-permute-start(f32[2,64,256]{2,1,0:T(8,128)S(1)} %bitcast.17), channel_id=1, source_target_pairs={{0,8},{8,0},{16,24},{24,16},{1,9},{9,1},{17,25},{25,17},{2,10},{10... | collective-permute-start | bytes 393224 | tf_op jit(solution)/shard_map/ppermute | solution.py:552
  23.2 0.4 %shard_map.112 = (f32[8,64,256]{2,1,0:T(8,128)S(1)}, f32[8,64,256]{2,1,0:T(8,128)S(1)}, f32[2,64,256]{2,1,0:T(8,128)S(1)}, f32[4,16,256]{2,1,0:T(8,128)S(1)}, f3...) custom-call(f32[8,64,256]{2,1,0:T(8,128)S(1)} %get-tuple-element.36.speeds, ...), custom_call_target="tpu_custom_call" | custom-call | flops 8000000000 | bytes 1000000 | tf_op jit(solution)/shard_map/pallas_call | solution.py:541
  23.6 2.7 %collective-permute-start.4 = (f32[4,16,256]{2,1,0:T(8,128)S(1)}, f32[4,16,256]{2,1,0:T(8,128)S(1)}, u32[]{:S(2)}, u32[]{:S(2)}) collective-permute-start(f32[4,16,256]{2,1,0:T(8,128)S(1)} %get-tuple-element.50), channel_id=1, source_target_pairs={{0,16},{8,24},{16,0},{24,8},{1,17},{9,25},{17,1},{25,9},{2,18},{10... | collective-permute-start | bytes 196616 | tf_op jit(solution)/shard_map/ppermute | solution.py:561
  26.3 0.2 collective-permute-start.5
  26.5 0.7 %shard_map.114.after = f32[8,64,256]{2,1,0:T(8,128)S(1)} custom-call(bf16[2,256,256]{2,1,0:T(8,128)(2,1)S(1)} %get-tuple-element.43.bands, f32[8,64,256]{2,1,0:T(8,128)S(1)} %get-tuple-element.53.outer, f32[8,64,256]{2,1,0:T(8,128)S(1)} %get-tuple-element.54.step, f32[8,64,256]{2,1,0:T(8,128)S(1)} %get-tuple-element.47.forward, ...), custom_call_target="tpu_custom_call" | custom-call | flops 1000000 | bytes 1000000 | tf_op jit(solution)/shard_map/pallas_call | solution.py:549
  27.2 0.0 collective-permute-done.7.rest_0_
  27.3 0.1 collective-permute-done.6.passed
  27.3 0.9 %collective-permute-done.8.rest_1_ = f32[512,256]{1,0:T(8,128)S(1)} collective-permute-done((f32[512,256]{1,0:T(8,128)S(1)}, f32[512,256]{1,0:T(8,128)S(1)}, u32[]{:S(2)}, u32[]{:S(2)}) %collective-permute-start.8) | collective-permute-done | bytes 524320 | tf_op jit(solution)/shard_map/ppermute | solution.py:540
  28.2 0.5 %shard_map.115 = (f32[4,16,256]{2,1,0:T(8,128)S(1)}, f32[4,16,256]{2,1,0:T(8,128)S(1)}, f32[4,16,256]{2,1,0:T(8,128)S(1)}, f32[4,16,256]{2,1,0:T(8,128)S(1)}) custom-call(f32[648,256]{1,0:T(8,128)S(1)} %shard_map.109.sent_first.own_out, f32[8,64,256]{2,1,0:T(8,128)S(1)} %get-tuple-element.36.speeds, f32[8,64,256]{2,1,0:T(8,128)S(1)} %get-tuple-element.53.outer, ...), custom_call_target="tpu_custom_call" | custom-call | flops 1000000 | bytes 1000000 | tf_op jit(solution)/shard_map/pallas_call | solution.py:574
  28.7 2.7 %collective-permute-start.10 = (f32[4,16,256]{2,1,0:T(8,128)S(1)}, f32[4,16,256]{2,1,0:T(8,128)S(1)}, u32[]{:S(2)}, u32[]{:S(2)}) collective-permute-start(f32[4,16,256]{2,1,0:T(8,128)S(1)} %get-tuple-element.64), channel_id=1, source_target_pairs={{0,16},{8,24},{16,0},{24,8},{1,17},{9,25},{17,1},{25,9},{2,18},{10... | collective-permute-start | bytes 196616 | tf_op jit(solution)/shard_map/ppermute | solution.py:561
  31.3 1.3 %collective-permute-start.11 = (f32[4,16,256]{2,1,0:T(8,128)S(1)}, f32[4,16,256]{2,1,0:T(8,128)S(1)}, u32[]{:S(2)}, u32[]{:S(2)}) collective-permute-start(f32[4,16,256]{2,1,0:T(8,128)S(1)} %get-tuple-element.65), channel_id=1, source_target_pairs={{0,24},{8,16},{16,8},{24,0},{1,25},{9,17},{17,9},{25,1},{2,26},{10... | collective-permute-start | bytes 196616 | tf_op jit(solution)/shard_map/ppermute | solution.py:561
  32.7 0.2 collective-permute-start.12
  32.9 0.0 collective-permute-done.4.refs_1_
  32.9 1.8 %collective-permute-start.9 = (f32[4,16,256]{2,1,0:T(8,128)S(1)}, f32[4,16,256]{2,1,0:T(8,128)S(1)}, u32[]{:S(2)}, u32[]{:S(2)}) collective-permute-start(f32[4,16,256]{2,1,0:T(8,128)S(1)} %get-tuple-element.62), channel_id=1, source_target_pairs={{0,8},{8,0},{16,24},{24,16},{1,9},{9,1},{17,25},{25,17},{2,10},{10... | collective-permute-start | bytes 196616 | tf_op jit(solution)/shard_map/ppermute | solution.py:561
  34.7 0.0 collective-permute-done.5.refs_2_
  34.7 1.3 %collective-permute-done.10.refs_1_ = f32[4,16,256]{2,1,0:T(8,128)S(1)} collective-permute-done((f32[4,16,256]{2,1,0:T(8,128)S(1)}, f32[4,16,256]{2,1,0:T(8,128)S(1)}, u32[]{:S(2)}, u32[]{:S(2)}) %collective-permute-start.10) | collective-permute-done | bytes 65568 | tf_op jit(solution)/shard_map/ppermute | solution.py:561
  36.0 1.9 %collective-permute-done.11.refs_2_ = f32[4,16,256]{2,1,0:T(8,128)S(1)} collective-permute-done((f32[4,16,256]{2,1,0:T(8,128)S(1)}, f32[4,16,256]{2,1,0:T(8,128)S(1)}, u32[]{:S(2)}, u32[]{:S(2)}) %collective-permute-start.11) | collective-permute-done | bytes 65568 | tf_op jit(solution)/shard_map/ppermute | solution.py:561
  37.9 0.0 collective-permute-done.12.refs_3_
  37.9 0.6 %collective-permute-done.9.inner_near = f32[4,16,256]{2,1,0:T(8,128)S(1)} collective-permute-done((f32[4,16,256]{2,1,0:T(8,128)S(1)}, f32[4,16,256]{2,1,0:T(8,128)S(1)}, u32[]{:S(2)}, u32[]{:S(2)}) %collective-permute-start.9) | collective-permute-done | bytes 65568 | tf_op jit(solution)/shard_map/ppermute | solution.py:561
  38.5 0.7 %shard_map.116 = f32[8,16,256]{2,1,0:T(8,128)} custom-call(f32[4,16,256]{2,1,0:T(8,128)S(1)} %shard_map.113.inner, f32[4,16,256]{2,1,0:T(8,128)S(1)} %collective-permute-done.9.inner_near, f32[4,16,256]{2,1,0:T(8,128)S(1)} %get-tuple-element.63.refs_0_, f32[4,16,256]{2,1,0:T(8,128)S(1)} %collective-permute-done.10.refs_1_, ...), custom_call_target="tpu_custom_call" | custom-call | flops 1000000 | bytes 1000000 | tf_op jit(solution)/shard_map/pallas_call | solution.py:587
  (2 shorter events, 0.0 us)
Async XLA Ops:
  0.0 2.1 %copy-start = (f32[8,64,256]{2,1,0:T(8,128)S(1)}, f32[8,64,256]{2,1,0:T(8,128)}, u32[]{:S(2)}) copy-start(f32[8,64,256]{2,1,0:T(8,128)} %courant.3) | copy-start | bytes 1572868
  0.0 2.1 %copy-start.1 = (f32[1,8,64,256]{3,2,1,0:T(8,128)S(1)}, f32[1,8,64,256]{3,2,1,0:T(8,128)}, u32[]{:S(2)}) copy-start(f32[1,8,64,256]{3,2,1,0:T(8,128)} %param.13) | copy-start | bytes 1572868
  0.0 2.1 %copy-start.2 = (f32[1,8,64,256]{3,2,1,0:T(8,128)S(1)}, f32[1,8,64,256]{3,2,1,0:T(8,128)}, u32[]{:S(2)}) copy-start(f32[1,8,64,256]{3,2,1,0:T(8,128)} %param.15) | copy-start | bytes 1572868
  0.0 2.1 %copy-start.6 = (f32[1,8,64,256]{3,2,1,0:T(8,128)S(1)}, f32[1,8,64,256]{3,2,1,0:T(8,128)}, u32[]{:S(2)}) copy-start(f32[1,8,64,256]{3,2,1,0:T(8,128)} %param.12) | copy-start | bytes 1572868
  1.4 20.2 %collective-permute-start = (f32[648,256]{1,0:T(8,128)S(1)}, f32[648,256]{1,0:T(8,128)S(1)}, u32[]{:S(2)}, u32[]{:S(2)}) collective-permute-start(f32[648,256]{1,0:T(8,128)S(1)} %shard_map.109.sent_first.own_out), channel_id=1, source_target_pairs={{1,2},{3,4},{5,6},{2,1},{4,3},{6,5},{9,10},{11,12},{13,14},{10,9},... | collective-permute-start | bytes 1990664 | tf_op jit(solution)/shard_map/ppermute | solution.py:489
  2.1 11.1 %copy-start.5 = (s32[1,256]{1,0:T(1,128)S(1)}, s32[1,256]{1,0:T(1,128)}, u32[]{:S(2)}) copy-start(s32[1,256]{1,0:T(1,128)} %receiver_yz.1) | copy-start | bytes 3076
  4.7 8.4 %collective-permute-start.2 = (f32[10,64,256]{2,1,0:T(8,128)S(1)}, f32[10,64,256]{2,1,0:T(8,128)S(1)}, u32[]{:S(2)}, u32[]{:S(2)}) collective-permute-start(f32[10,64,256]{2,1,0:T(8,128)S(1)} %get-tuple-element.38.own_in), channel_id=1, source_target_pairs={{0,1},{1,0},{2,3},{3,2},{4,5},{5,4},{6,7},{7,6},{8,9},{9,8},{10,11... | collective-permute-start | bytes 1966088 | tf_op jit(solution)/shard_map/ppermute | solution.py:503
  9.1 4.1 %collective-permute-start.3 = (f32[10,64,256]{2,1,0:T(8,128)S(1)}, f32[10,64,256]{2,1,0:T(8,128)S(1)}, u32[]{:S(2)}, u32[]{:S(2)}) collective-permute-start(f32[10,64,256]{2,1,0:T(8,128)S(1)} %get-tuple-element.41.late_in), channel_id=1, source_target_pairs={{0,1},{1,0},{2,3},{3,2},{4,5},{5,4},{6,7},{7,6},{8,9},{9,8},{10,11... | collective-permute-start | bytes 1966088 | tf_op jit(solution)/shard_map/ppermute | solution.py:504
  9.2 11.1 %collective-permute-start.1 = (f32[512,256]{1,0:T(8,128)S(1)}, f32[512,256]{1,0:T(8,128)S(1)}, u32[]{:S(2)}, u32[]{:S(2)}) collective-permute-start(f32[512,256]{1,0:T(8,128)S(1)} %get-tuple-element.37.late_out), channel_id=1, source_target_pairs={{3,7},{4,0},{11,15},{12,8},{19,23},{20,16},{27,31},{28,24}} | collective-permute-start | bytes 1572872 | tf_op jit(solution)/shard_map/ppermute | solution.py:506
  10.4 16.8 %collective-permute-start.7 = (f32[512,256]{1,0:T(8,128)S(1)}, f32[512,256]{1,0:T(8,128)S(1)}, u32[]{:S(2)}, u32[]{:S(2)}) collective-permute-start(f32[512,256]{1,0:T(8,128)S(1)} %get-tuple-element.37.late_out), channel_id=1, source_target_pairs={{1,2},{5,6},{2,1},{6,5},{9,10},{13,14},{10,9},{14,13},{17,18},{21,... | collective-permute-start | bytes 1572872 | tf_op jit(solution)/shard_map/ppermute | solution.py:507
  12.4 0.7 %copy-start.7 = (f32[1,2]{1,0:T(1,128)S(1)}, f32[1,2]{1,0:T(1,128)}, u32[]{:S(2)}) copy-start(f32[1,2]{1,0:T(1,128)} %param.18) | copy-start | bytes 28
  13.2 0.7 %copy-start.3 = (f32[1,256,2]{1,2,0:T(2,128)S(1)}, f32[1,256,2]{1,2,0:T(2,128)}, u32[]{:S(2)}) copy-start(f32[1,256,2]{1,2,0:T(2,128)} %param.21) | copy-start | bytes 6148
  13.2 0.7 %copy-start.4 = (s32[1,256]{1,0:T(1,128)S(1)}, s32[1,256]{1,0:T(1,128)}, u32[]{:S(2)}) copy-start(s32[1,256]{1,0:T(1,128)} %receiver_x.1) | copy-start | bytes 3076
  20.2 8.0 %collective-permute-start.8 = (f32[512,256]{1,0:T(8,128)S(1)}, f32[512,256]{1,0:T(8,128)S(1)}, u32[]{:S(2)}, u32[]{:S(2)}) collective-permute-start(f32[512,256]{1,0:T(8,128)S(1)} %collective-permute-done.1), channel_id=1, source_target_pairs={{7,4},{0,3},{15,12},{8,11},{23,20},{16,19},{31,28},{24,27}} | collective-permute-start | bytes 1572872 | tf_op jit(solution)/shard_map/ppermute | solution.py:540
  21.6 5.7 %collective-permute-start.6 = (f32[2,64,256]{2,1,0:T(8,128)S(1)}, f32[2,64,256]{2,1,0:T(8,128)S(1)}, u32[]{:S(2)}, u32[]{:S(2)}) collective-permute-start(f32[2,64,256]{2,1,0:T(8,128)S(1)} %bitcast.17), channel_id=1, source_target_pairs={{0,8},{8,0},{16,24},{24,16},{1,9},{9,1},{17,25},{25,17},{2,10},{10... | collective-permute-start | bytes 393224 | tf_op jit(solution)/shard_map/ppermute | solution.py:552
  23.6 9.3 %collective-permute-start.4 = (f32[4,16,256]{2,1,0:T(8,128)S(1)}, f32[4,16,256]{2,1,0:T(8,128)S(1)}, u32[]{:S(2)}, u32[]{:S(2)}) collective-permute-start(f32[4,16,256]{2,1,0:T(8,128)S(1)} %get-tuple-element.50), channel_id=1, source_target_pairs={{0,16},{8,24},{16,0},{24,8},{1,17},{9,25},{17,1},{25,9},{2,18},{10... | collective-permute-start | bytes 196616 | tf_op jit(solution)/shard_map/ppermute | solution.py:561
  26.3 8.4 %collective-permute-start.5 = (f32[4,16,256]{2,1,0:T(8,128)S(1)}, f32[4,16,256]{2,1,0:T(8,128)S(1)}, u32[]{:S(2)}, u32[]{:S(2)}) collective-permute-start(f32[4,16,256]{2,1,0:T(8,128)S(1)} %get-tuple-element.51), channel_id=1, source_target_pairs={{0,24},{8,16},{16,8},{24,0},{1,25},{9,17},{17,9},{25,1},{2,26},{10... | collective-permute-start | bytes 196616 | tf_op jit(solution)/shard_map/ppermute | solution.py:561
  28.7 7.3 %collective-permute-start.10 = (f32[4,16,256]{2,1,0:T(8,128)S(1)}, f32[4,16,256]{2,1,0:T(8,128)S(1)}, u32[]{:S(2)}, u32[]{:S(2)}) collective-permute-start(f32[4,16,256]{2,1,0:T(8,128)S(1)} %get-tuple-element.64), channel_id=1, source_target_pairs={{0,16},{8,24},{16,0},{24,8},{1,17},{9,25},{17,1},{25,9},{2,18},{10... | collective-permute-start | bytes 196616 | tf_op jit(solution)/shard_map/ppermute | solution.py:561
  31.3 6.5 %collective-permute-start.11 = (f32[4,16,256]{2,1,0:T(8,128)S(1)}, f32[4,16,256]{2,1,0:T(8,128)S(1)}, u32[]{:S(2)}, u32[]{:S(2)}) collective-permute-start(f32[4,16,256]{2,1,0:T(8,128)S(1)} %get-tuple-element.65), channel_id=1, source_target_pairs={{0,24},{8,16},{16,8},{24,0},{1,25},{9,17},{17,9},{25,1},{2,26},{10... | collective-permute-start | bytes 196616 | tf_op jit(solution)/shard_map/ppermute | solution.py:561
  32.7 5.2 %collective-permute-start.12 = (f32[4,16,256]{2,1,0:T(8,128)S(1)}, f32[4,16,256]{2,1,0:T(8,128)S(1)}, u32[]{:S(2)}, u32[]{:S(2)}) collective-permute-start(f32[4,16,256]{2,1,0:T(8,128)S(1)} %get-tuple-element.66), channel_id=1, source_target_pairs={{0,8},{8,0},{16,24},{24,16},{1,9},{9,1},{17,25},{25,17},{2,10},{10... | collective-permute-start | bytes 196616 | tf_op jit(solution)/shard_map/ppermute | solution.py:561
  32.9 5.6 %collective-permute-start.9 = (f32[4,16,256]{2,1,0:T(8,128)S(1)}, f32[4,16,256]{2,1,0:T(8,128)S(1)}, u32[]{:S(2)}, u32[]{:S(2)}) collective-permute-start(f32[4,16,256]{2,1,0:T(8,128)S(1)} %get-tuple-element.62), channel_id=1, source_target_pairs={{0,8},{8,0},{16,24},{24,16},{1,9},{9,1},{17,25},{25,17},{2,10},{10... | collective-permute-start | bytes 196616 | tf_op jit(solution)/shard_map/ppermute | solution.py:561

commit v8 on v7

--- a/solution.py
+++ b/solution.py
@@ -344,7 +344,7 @@
 
 
 def middle_kernel(shots, speeds, halo, inner, outer_part, forward, backward, outer, step, *rest):
-    shared, outputs, (gradient,) = rest[0], rest[1 : 1 + shots], rest[1 + shots :]
+    outputs, (gradient,) = rest[:shots], rest[shots:]
     size_y = speeds.shape[1]
     for at in range(REACH):
         speed = speeds[at]
@@ -361,8 +361,6 @@
         speed = speeds[REACH + at]
         gradient[at] = 2.0 * speed * (back * inner[at] + inner[REACH + at] * ahead)
     scatter_rows(gradient, outputs, shots, True)
-    for number in range(EARLY_SPEEDS):
-        shared[number] = halo[layer_rows(2 * REACH + number, size_y)]
 
 
 def second_kernel(bands, outer, step, forward, backward, after):
@@ -380,7 +378,7 @@
 
 
 def outer_kernel(
-    shots, relayed, own_out, speeds, outer, after, shared, passed, points_out, *rest
+    shots, relayed, own_out, speeds, outer, after, halo, passed, points_out, *rest
 ):
     lates, rest = rest[: 1 + relayed], rest[1 + relayed :]
     outputs, (next_mid, next_scaled, gradient) = rest[:shots], rest[shots:]
@@ -393,7 +391,8 @@
     parity = lax.rem(lax.axis_index("shot"), 2)
     for at in range(REACH):
         mine, number = parity == at // EARLY_SPEEDS, at % EARLY_SPEEDS
-        speed = jnp.where(mine, shared[number], passed[number])
+        arrived = halo[layer_rows(2 * REACH + number, size_y)]
+        speed = jnp.where(mine, arrived, passed[number])
         next_mid[at], next_scaled[at] = next_halo(at, speed, late, own, points_out)
     for at in range(REACH):
         ahead = after[at] + across(at, lambda i: next_mid[i])
@@ -538,9 +537,9 @@
     if relayed:
         first_hop, inner = lax.optimization_barrier((first_hop, inner))
         halo_lates.append(lax.ppermute(first_hop, "space", [(7, 4), (0, 3)]))
-    outer, step, shared, *inner_parts = call(
+    outer, step, *inner_parts = call(
         functools.partial(middle_kernel, shots),
-        [stack(2 * REACH)] * 2 + [stack(EARLY_SPEEDS)] + [(REACH, part_rows, size_z)] * shots,
+        [stack(2 * REACH)] * 2 + [(REACH, part_rows, size_z)] * shots,
         [V] * 6,
         [held(REACH)],
         MIDDLE_COST,
@@ -578,7 +577,7 @@
         [held(REACH)] * 3,
         SMALL,
         SMALL,
-    )(early_out, speeds, outer, after, shared, passed, points_out, *halo_lates)
+    )(early_out, speeds, outer, after, halo_out, passed, points_out, *halo_lates)
     inner_near, *outer_parts = lax.optimization_barrier((inner_near, *outer_parts))
     inner_near = exchanged(inner_near, 1)
     outer_parts = [

time: 39.4 us -> 39.4 us (level)
  no operation moved by 1% of the time
where the time goes in v8:
time: 39.4 us; the launch traced here: 39.1 us
  starting transfers between devices  19 us (48%)
  waiting for transfers between devices  9.38 us (24%)
  Pallas kernels  7.88 us (20%)
  between operations  1.48 us (4%)
  local copies, waits for them, and re-layouts  1.36 us (3%)
    ppermute x6, starting transfers between devices, exchanged(): return lax.ppermute(part, 'shot', [(i, i ^ shift) for i in range(shots)])  8.91 us
    ppermute x1, waiting for transfers between devices, on_device(): first_hop = lax.ppermute(late_out, 'space', [(3, 7), (4, 0)])  4.6 us
    ppermute x1, starting transfers between devices, on_device(): halo_in = lax.ppermute(early_in, 'space', in_pairs)  4.34 us
    ppermute x6, waiting for transfers between devices, exchanged(): return lax.ppermute(part, 'shot', [(i, i ^ shift) for i in range(shots)])  3.81 us
    pallas_call x1, Pallas kernels, on_device(): call(local_kernel, [stack(slab)] * 4 + [bands, stack(2 * REACH + INNER_SP...  2.57 us
    pallas_call x1, Pallas kernels, on_device(): call(inner_kernel, [stack(2 * REACH), stack(3 * REACH)] + [stack(2 * REAC...  1.73 us
    ppermute x1, starting transfers between devices, on_device(): lax.ppermute(lax.slice_in_dim(halo_out, 2 * REACH * size_y, early_layers...  1.64 us
    unnamed x16, local copies, waits for them, and re-layouts  1.35 us
  transfers between devices with their start and end apart: 13, of which 6 were waited for; matrix products, arithmetic and copies ran while one was open for 0% of the time, Pallas kernels for 15%

profile of v8, /device:TPU:0, one launch (start us, length us, event | category | flops | bytes accessed | tf_op | source)
XLA Modules:
  0.0 39.1 jit_solution(7726409902689480697)
XLA Ops:
  0.0 0.0 copy-start
  0.0 0.0 copy-start.1
  0.0 0.0 copy-start.2
  0.0 0.0 copy-start.6
  0.0 1.3 %shard_map.109.sent_first.own_out = f32[648,256]{1,0:T(8,128)S(1)} custom-call(f32[8,64,256]{2,1,0:T(8,128)} %courant.3, f32[8,64,256]{2,1,0:T(8,128)} %bitcast.11, f32[8,64,256]{2,1,0:T(8,128)} %bitcast.13), custom_call_target="tpu_custom_call" | custom-call | flops 1000000 | bytes 1000000 | tf_op jit(solution)/shard_map/pallas_call | solution.py:480
  1.4 0.7 %collective-permute-start = (f32[648,256]{1,0:T(8,128)S(1)}, f32[648,256]{1,0:T(8,128)S(1)}, u32[]{:S(2)}, u32[]{:S(2)}) collective-permute-start(f32[648,256]{1,0:T(8,128)S(1)} %shard_map.109.sent_first.own_out), channel_id=1, source_target_pairs={{1,2},{3,4},{5,6},{2,1},{4,3},{6,5},{9,10},{11,12},{13,14},{10,9},... | collective-permute-start | bytes 1990664 | tf_op jit(solution)/shard_map/ppermute | solution.py:488
  2.1 0.0 copy-done
  2.1 0.0 copy-done.1
  2.1 0.0 copy-done.2
  2.1 0.0 copy-done.6
  2.1 0.0 copy-start.5
  2.1 2.6 %shard_map.110 = (f32[8,64,256]{2,1,0:T(8,128)S(1)}, f32[8,64,256]{2,1,0:T(8,128)S(1)}, f32[8,64,256]{2,1,0:T(8,128)S(1)}, f32[8,64,256]{2,1,0:T(8,128)S(1)}, bf...) custom-call(f32[648,256]{1,0:T(8,128)S(1)} %shard_map.109.sent_first, ...), custom_call_target="tpu_custom_call" | custom-call | flops 10000000000 | bytes 1000000 | tf_op jit(solution)/shard_map/pallas_call | solution.py:491
  4.7 4.3 %collective-permute-start.2 = (f32[10,64,256]{2,1,0:T(8,128)S(1)}, f32[10,64,256]{2,1,0:T(8,128)S(1)}, u32[]{:S(2)}, u32[]{:S(2)}) collective-permute-start(f32[10,64,256]{2,1,0:T(8,128)S(1)} %get-tuple-element.37.own_in), channel_id=1, source_target_pairs={{0,1},{1,0},{2,3},{3,2},{4,5},{5,4},{6,7},{7,6},{8,9},{9,8},{10,11... | collective-permute-start | bytes 1966088 | tf_op jit(solution)/shard_map/ppermute | solution.py:502
  9.0 0.1 collective-permute-start.3
  9.1 1.3 %collective-permute-start.1 = (f32[512,256]{1,0:T(8,128)S(1)}, f32[512,256]{1,0:T(8,128)S(1)}, u32[]{:S(2)}, u32[]{:S(2)}) collective-permute-start(f32[512,256]{1,0:T(8,128)S(1)} %get-tuple-element.36.late_out), channel_id=1, source_target_pairs={{3,7},{4,0},{11,15},{12,8},{19,23},{20,16},{27,31},{28,24}} | collective-permute-start | bytes 1572872 | tf_op jit(solution)/shard_map/ppermute | solution.py:505
  10.4 0.7 %collective-permute-start.7 = (f32[512,256]{1,0:T(8,128)S(1)}, f32[512,256]{1,0:T(8,128)S(1)}, u32[]{:S(2)}, u32[]{:S(2)}) collective-permute-start(f32[512,256]{1,0:T(8,128)S(1)} %get-tuple-element.36.late_out), channel_id=1, source_target_pairs={{1,2},{5,6},{2,1},{6,5},{9,10},{13,14},{10,9},{14,13},{17,18},{21,... | collective-permute-start | bytes 1572872 | tf_op jit(solution)/shard_map/ppermute | solution.py:506
  12.4 0.0 copy-start.7
  12.4 0.6 %copy-done.7 = f32[1,2]{1,0:T(1,128)S(1)} copy-done((f32[1,2]{1,0:T(1,128)S(1)}, f32[1,2]{1,0:T(1,128)}, u32[]{:S(2)}) %copy-start.7) | copy-done | bytes 32
  13.1 0.1 maximum_bitcast_fusion.pulse
  13.1 0.0 collective-permute-done.2.halo_early
  13.1 0.0 collective-permute-done.3.halo_late
  13.1 0.0 copy-start.3
  13.1 0.0 copy-start.4
  13.2 0.0 copy-done.5
  13.2 0.7 %copy-done.3 = f32[1,256,2]{1,2,0:T(2,128)S(1)} copy-done((f32[1,256,2]{1,2,0:T(2,128)S(1)}, f32[1,256,2]{1,2,0:T(2,128)}, u32[]{:S(2)}) %copy-start.3) | copy-done | bytes 2072
  13.8 0.0 copy-done.4
  13.8 1.7 %shard_map.111 = (f32[8,64,256]{2,1,0:T(8,128)S(1)}, f32[12,64,256]{2,1,0:T(8,128)S(1)}, f32[8,64,256]{2,1,0:T(8,128)S(1)}, f32[8,64,256]{2,1,0:T(8,128)S(1)}, f32[8,64,256]{2,1,0:T(8,128)S(1)}) custom-call(f32[1,4]{1,0:T(1,128)S(1)} %maximum_bitcast_fusion.pulse, s32[1,256]{1,0:T(1,128)S(1)} %copy-done.4, s32[1,256]{1,0:T(1,128)S(1)} %copy-done.5, ...), custom_call_target="tpu_custom_call" | custom-call | flops 1000000 | bytes 1000000 | tf_op jit(solution)/shard_map/pallas_call | solution.py:509
  15.6 4.6 %collective-permute-done.1 = f32[512,256]{1,0:T(8,128)S(1)} collective-permute-done((f32[512,256]{1,0:T(8,128)S(1)}, f32[512,256]{1,0:T(8,128)S(1)}, u32[]{:S(2)}, u32[]{:S(2)}) %collective-permute-start.1) | collective-permute-done | bytes 524320 | tf_op jit(solution)/shard_map/ppermute | solution.py:505
  20.2 1.3 %collective-permute-start.8 = (f32[512,256]{1,0:T(8,128)S(1)}, f32[512,256]{1,0:T(8,128)S(1)}, u32[]{:S(2)}, u32[]{:S(2)}) collective-permute-start(f32[512,256]{1,0:T(8,128)S(1)} %collective-permute-done.1), channel_id=1, source_target_pairs={{7,4},{0,3},{15,12},{8,11},{23,20},{16,19},{31,28},{24,27}} | collective-permute-start | bytes 1572872 | tf_op jit(solution)/shard_map/ppermute | solution.py:539
  21.5 0.0 collective-permute-done.halo
  21.5 1.6 %collective-permute-start.6 = (f32[2,64,256]{2,1,0:T(8,128)S(1)}, f32[2,64,256]{2,1,0:T(8,128)S(1)}, u32[]{:S(2)}, u32[]{:S(2)}) collective-permute-start(f32[2,64,256]{2,1,0:T(8,128)S(1)} %bitcast.17), channel_id=1, source_target_pairs={{0,8},{8,0},{16,24},{24,16},{1,9},{9,1},{17,25},{25,17},{2,10},{10... | collective-permute-start | bytes 393224 | tf_op jit(solution)/shard_map/ppermute | solution.py:551
  23.2 0.4 shard_map.112
  23.6 2.7 %collective-permute-start.4 = (f32[4,16,256]{2,1,0:T(8,128)S(1)}, f32[4,16,256]{2,1,0:T(8,128)S(1)}, u32[]{:S(2)}, u32[]{:S(2)}) collective-permute-start(f32[4,16,256]{2,1,0:T(8,128)S(1)} %get-tuple-element.49), channel_id=1, source_target_pairs={{0,16},{8,24},{16,0},{24,8},{1,17},{9,25},{17,1},{25,9},{2,18},{10... | collective-permute-start | bytes 196616 | tf_op jit(solution)/shard_map/ppermute | solution.py:560
  26.2 0.2 collective-permute-start.5
  26.4 0.7 %shard_map.114.after = f32[8,64,256]{2,1,0:T(8,128)S(1)} custom-call(bf16[2,256,256]{2,1,0:T(8,128)(2,1)S(1)} %get-tuple-element.42.bands, f32[8,64,256]{2,1,0:T(8,128)S(1)} %get-tuple-element.52.outer, f32[8,64,256]{2,1,0:T(8,128)S(1)} %get-tuple-element.53.step, f32[8,64,256]{2,1,0:T(8,128)S(1)} %get-tuple-element.46.forward, ...), custom_call_target="tpu_custom_call" | custom-call | flops 1000000 | bytes 1000000 | tf_op jit(solution)/shard_map/pallas_call | solution.py:548
  27.2 0.0 collective-permute-done.7.rest_0_
  27.2 0.1 collective-permute-done.6.passed
  27.3 0.9 %collective-permute-done.8.rest_1_ = f32[512,256]{1,0:T(8,128)S(1)} collective-permute-done((f32[512,256]{1,0:T(8,128)S(1)}, f32[512,256]{1,0:T(8,128)S(1)}, u32[]{:S(2)}, u32[]{:S(2)}) %collective-permute-start.8) | collective-permute-done | bytes 524320 | tf_op jit(solution)/shard_map/ppermute | solution.py:539
  28.1 0.4 %shard_map.115 = (f32[4,16,256]{2,1,0:T(8,128)S(1)}, f32[4,16,256]{2,1,0:T(8,128)S(1)}, f32[4,16,256]{2,1,0:T(8,128)S(1)}, f32[4,16,256]{2,1,0:T(8,128)S(1)}) custom-call(f32[648,256]{1,0:T(8,128)S(1)} %shard_map.109.sent_first.own_out, f32[8,64,256]{2,1,0:T(8,128)S(1)} %get-tuple-element.35.speeds, f32[8,64,256]{2,1,0:T(8,128)S(1)} %get-tuple-element.52.outer, ...), custom_call_target="tpu_custom_call" | custom-call | flops 1000000 | bytes 1000000 | tf_op jit(solution)/shard_map/pallas_call | solution.py:573
  28.6 2.7 %collective-permute-start.10 = (f32[4,16,256]{2,1,0:T(8,128)S(1)}, f32[4,16,256]{2,1,0:T(8,128)S(1)}, u32[]{:S(2)}, u32[]{:S(2)}) collective-permute-start(f32[4,16,256]{2,1,0:T(8,128)S(1)} %get-tuple-element.62), channel_id=1, source_target_pairs={{0,16},{8,24},{16,0},{24,8},{1,17},{9,25},{17,1},{25,9},{2,18},{10... | collective-permute-start | bytes 196616 | tf_op jit(solution)/shard_map/ppermute | solution.py:560
  31.2 1.3 %collective-permute-start.11 = (f32[4,16,256]{2,1,0:T(8,128)S(1)}, f32[4,16,256]{2,1,0:T(8,128)S(1)}, u32[]{:S(2)}, u32[]{:S(2)}) collective-permute-start(f32[4,16,256]{2,1,0:T(8,128)S(1)} %get-tuple-element.63), channel_id=1, source_target_pairs={{0,24},{8,16},{16,8},{24,0},{1,25},{9,17},{17,9},{25,1},{2,26},{10... | collective-permute-start | bytes 196616 | tf_op jit(solution)/shard_map/ppermute | solution.py:560
  32.6 0.2 collective-permute-start.12
  32.8 0.0 collective-permute-done.4.refs_1_
  32.8 1.8 %collective-permute-start.9 = (f32[4,16,256]{2,1,0:T(8,128)S(1)}, f32[4,16,256]{2,1,0:T(8,128)S(1)}, u32[]{:S(2)}, u32[]{:S(2)}) collective-permute-start(f32[4,16,256]{2,1,0:T(8,128)S(1)} %get-tuple-element.60), channel_id=1, source_target_pairs={{0,8},{8,0},{16,24},{24,16},{1,9},{9,1},{17,25},{25,17},{2,10},{10... | collective-permute-start | bytes 196616 | tf_op jit(solution)/shard_map/ppermute | solution.py:560
  34.6 0.0 collective-permute-done.5.refs_2_
  34.6 1.3 %collective-permute-done.10.refs_1_ = f32[4,16,256]{2,1,0:T(8,128)S(1)} collective-permute-done((f32[4,16,256]{2,1,0:T(8,128)S(1)}, f32[4,16,256]{2,1,0:T(8,128)S(1)}, u32[]{:S(2)}, u32[]{:S(2)}) %collective-permute-start.10) | collective-permute-done | bytes 65568 | tf_op jit(solution)/shard_map/ppermute | solution.py:560
  35.9 1.9 %collective-permute-done.11.refs_2_ = f32[4,16,256]{2,1,0:T(8,128)S(1)} collective-permute-done((f32[4,16,256]{2,1,0:T(8,128)S(1)}, f32[4,16,256]{2,1,0:T(8,128)S(1)}, u32[]{:S(2)}, u32[]{:S(2)}) %collective-permute-start.11) | collective-permute-done | bytes 65568 | tf_op jit(solution)/shard_map/ppermute | solution.py:560
  37.8 0.0 collective-permute-done.12.refs_3_
  37.8 0.6 %collective-permute-done.9.inner_near = f32[4,16,256]{2,1,0:T(8,128)S(1)} collective-permute-done((f32[4,16,256]{2,1,0:T(8,128)S(1)}, f32[4,16,256]{2,1,0:T(8,128)S(1)}, u32[]{:S(2)}, u32[]{:S(2)}) %collective-permute-start.9) | collective-permute-done | bytes 65568 | tf_op jit(solution)/shard_map/ppermute | solution.py:560
  38.4 0.7 %shard_map.116 = f32[8,16,256]{2,1,0:T(8,128)} custom-call(f32[4,16,256]{2,1,0:T(8,128)S(1)} %shard_map.113.inner, f32[4,16,256]{2,1,0:T(8,128)S(1)} %collective-permute-done.9.inner_near, f32[4,16,256]{2,1,0:T(8,128)S(1)} %get-tuple-element.61.refs_0_, f32[4,16,256]{2,1,0:T(8,128)S(1)} %collective-permute-done.10.refs_1_, ...), custom_call_target="tpu_custom_call" | custom-call | flops 1000000 | bytes 1000000 | tf_op jit(solution)/shard_map/pallas_call | solution.py:586
  (2 shorter events, 0.0 us)
Async XLA Ops:
  0.0 2.1 %copy-start = (f32[8,64,256]{2,1,0:T(8,128)S(1)}, f32[8,64,256]{2,1,0:T(8,128)}, u32[]{:S(2)}) copy-start(f32[8,64,256]{2,1,0:T(8,128)} %courant.3) | copy-start | bytes 1572868
  0.0 2.1 %copy-start.1 = (f32[1,8,64,256]{3,2,1,0:T(8,128)S(1)}, f32[1,8,64,256]{3,2,1,0:T(8,128)}, u32[]{:S(2)}) copy-start(f32[1,8,64,256]{3,2,1,0:T(8,128)} %param.13) | copy-start | bytes 1572868
  0.0 2.1 %copy-start.2 = (f32[1,8,64,256]{3,2,1,0:T(8,128)S(1)}, f32[1,8,64,256]{3,2,1,0:T(8,128)}, u32[]{:S(2)}) copy-start(f32[1,8,64,256]{3,2,1,0:T(8,128)} %param.15) | copy-start | bytes 1572868
  0.0 2.1 %copy-start.6 = (f32[1,8,64,256]{3,2,1,0:T(8,128)S(1)}, f32[1,8,64,256]{3,2,1,0:T(8,128)}, u32[]{:S(2)}) copy-start(f32[1,8,64,256]{3,2,1,0:T(8,128)} %param.12) | copy-start | bytes 1572868
  1.4 20.1 %collective-permute-start = (f32[648,256]{1,0:T(8,128)S(1)}, f32[648,256]{1,0:T(8,128)S(1)}, u32[]{:S(2)}, u32[]{:S(2)}) collective-permute-start(f32[648,256]{1,0:T(8,128)S(1)} %shard_map.109.sent_first.own_out), channel_id=1, source_target_pairs={{1,2},{3,4},{5,6},{2,1},{4,3},{6,5},{9,10},{11,12},{13,14},{10,9},... | collective-permute-start | bytes 1990664 | tf_op jit(solution)/shard_map/ppermute | solution.py:488
  2.1 11.1 %copy-start.5 = (s32[1,256]{1,0:T(1,128)S(1)}, s32[1,256]{1,0:T(1,128)}, u32[]{:S(2)}) copy-start(s32[1,256]{1,0:T(1,128)} %receiver_yz.1) | copy-start | bytes 3076
  4.7 8.4 %collective-permute-start.2 = (f32[10,64,256]{2,1,0:T(8,128)S(1)}, f32[10,64,256]{2,1,0:T(8,128)S(1)}, u32[]{:S(2)}, u32[]{:S(2)}) collective-permute-start(f32[10,64,256]{2,1,0:T(8,128)S(1)} %get-tuple-element.37.own_in), channel_id=1, source_target_pairs={{0,1},{1,0},{2,3},{3,2},{4,5},{5,4},{6,7},{7,6},{8,9},{9,8},{10,11... | collective-permute-start | bytes 1966088 | tf_op jit(solution)/shard_map/ppermute | solution.py:502
  9.0 4.1 %collective-permute-start.3 = (f32[10,64,256]{2,1,0:T(8,128)S(1)}, f32[10,64,256]{2,1,0:T(8,128)S(1)}, u32[]{:S(2)}, u32[]{:S(2)}) collective-permute-start(f32[10,64,256]{2,1,0:T(8,128)S(1)} %get-tuple-element.40.late_in), channel_id=1, source_target_pairs={{0,1},{1,0},{2,3},{3,2},{4,5},{5,4},{6,7},{7,6},{8,9},{9,8},{10,11... | collective-permute-start | bytes 1966088 | tf_op jit(solution)/shard_map/ppermute | solution.py:503
  9.1 11.1 %collective-permute-start.1 = (f32[512,256]{1,0:T(8,128)S(1)}, f32[512,256]{1,0:T(8,128)S(1)}, u32[]{:S(2)}, u32[]{:S(2)}) collective-permute-start(f32[512,256]{1,0:T(8,128)S(1)} %get-tuple-element.36.late_out), channel_id=1, source_target_pairs={{3,7},{4,0},{11,15},{12,8},{19,23},{20,16},{27,31},{28,24}} | collective-permute-start | bytes 1572872 | tf_op jit(solution)/shard_map/ppermute | solution.py:505
  10.4 16.8 %collective-permute-start.7 = (f32[512,256]{1,0:T(8,128)S(1)}, f32[512,256]{1,0:T(8,128)S(1)}, u32[]{:S(2)}, u32[]{:S(2)}) collective-permute-start(f32[512,256]{1,0:T(8,128)S(1)} %get-tuple-element.36.late_out), channel_id=1, source_target_pairs={{1,2},{5,6},{2,1},{6,5},{9,10},{13,14},{10,9},{14,13},{17,18},{21,... | collective-permute-start | bytes 1572872 | tf_op jit(solution)/shard_map/ppermute | solution.py:506
  12.4 0.7 %copy-start.7 = (f32[1,2]{1,0:T(1,128)S(1)}, f32[1,2]{1,0:T(1,128)}, u32[]{:S(2)}) copy-start(f32[1,2]{1,0:T(1,128)} %param.18) | copy-start | bytes 28
  13.1 0.7 %copy-start.3 = (f32[1,256,2]{1,2,0:T(2,128)S(1)}, f32[1,256,2]{1,2,0:T(2,128)}, u32[]{:S(2)}) copy-start(f32[1,256,2]{1,2,0:T(2,128)} %param.21) | copy-start | bytes 6148
  13.1 0.7 %copy-start.4 = (s32[1,256]{1,0:T(1,128)S(1)}, s32[1,256]{1,0:T(1,128)}, u32[]{:S(2)}) copy-start(s32[1,256]{1,0:T(1,128)} %receiver_x.1) | copy-start | bytes 3076
  20.2 8.0 %collective-permute-start.8 = (f32[512,256]{1,0:T(8,128)S(1)}, f32[512,256]{1,0:T(8,128)S(1)}, u32[]{:S(2)}, u32[]{:S(2)}) collective-permute-start(f32[512,256]{1,0:T(8,128)S(1)} %collective-permute-done.1), channel_id=1, source_target_pairs={{7,4},{0,3},{15,12},{8,11},{23,20},{16,19},{31,28},{24,27}} | collective-permute-start | bytes 1572872 | tf_op jit(solution)/shard_map/ppermute | solution.py:539
  21.5 5.7 %collective-permute-start.6 = (f32[2,64,256]{2,1,0:T(8,128)S(1)}, f32[2,64,256]{2,1,0:T(8,128)S(1)}, u32[]{:S(2)}, u32[]{:S(2)}) collective-permute-start(f32[2,64,256]{2,1,0:T(8,128)S(1)} %bitcast.17), channel_id=1, source_target_pairs={{0,8},{8,0},{16,24},{24,16},{1,9},{9,1},{17,25},{25,17},{2,10},{10... | collective-permute-start | bytes 393224 | tf_op jit(solution)/shard_map/ppermute | solution.py:551
  23.6 9.3 %collective-permute-start.4 = (f32[4,16,256]{2,1,0:T(8,128)S(1)}, f32[4,16,256]{2,1,0:T(8,128)S(1)}, u32[]{:S(2)}, u32[]{:S(2)}) collective-permute-start(f32[4,16,256]{2,1,0:T(8,128)S(1)} %get-tuple-element.49), channel_id=1, source_target_pairs={{0,16},{8,24},{16,0},{24,8},{1,17},{9,25},{17,1},{25,9},{2,18},{10... | collective-permute-start | bytes 196616 | tf_op jit(solution)/shard_map/ppermute | solution.py:560
  26.2 8.4 %collective-permute-start.5 = (f32[4,16,256]{2,1,0:T(8,128)S(1)}, f32[4,16,256]{2,1,0:T(8,128)S(1)}, u32[]{:S(2)}, u32[]{:S(2)}) collective-permute-start(f32[4,16,256]{2,1,0:T(8,128)S(1)} %get-tuple-element.50), channel_id=1, source_target_pairs={{0,24},{8,16},{16,8},{24,0},{1,25},{9,17},{17,9},{25,1},{2,26},{10... | collective-permute-start | bytes 196616 | tf_op jit(solution)/shard_map/ppermute | solution.py:560
  28.6 7.4 %collective-permute-start.10 = (f32[4,16,256]{2,1,0:T(8,128)S(1)}, f32[4,16,256]{2,1,0:T(8,128)S(1)}, u32[]{:S(2)}, u32[]{:S(2)}) collective-permute-start(f32[4,16,256]{2,1,0:T(8,128)S(1)} %get-tuple-element.62), channel_id=1, source_target_pairs={{0,16},{8,24},{16,0},{24,8},{1,17},{9,25},{17,1},{25,9},{2,18},{10... | collective-permute-start | bytes 196616 | tf_op jit(solution)/shard_map/ppermute | solution.py:560
  31.2 6.6 %collective-permute-start.11 = (f32[4,16,256]{2,1,0:T(8,128)S(1)}, f32[4,16,256]{2,1,0:T(8,128)S(1)}, u32[]{:S(2)}, u32[]{:S(2)}) collective-permute-start(f32[4,16,256]{2,1,0:T(8,128)S(1)} %get-tuple-element.63), channel_id=1, source_target_pairs={{0,24},{8,16},{16,8},{24,0},{1,25},{9,17},{17,9},{25,1},{2,26},{10... | collective-permute-start | bytes 196616 | tf_op jit(solution)/shard_map/ppermute | solution.py:560
  32.6 5.2 %collective-permute-start.12 = (f32[4,16,256]{2,1,0:T(8,128)S(1)}, f32[4,16,256]{2,1,0:T(8,128)S(1)}, u32[]{:S(2)}, u32[]{:S(2)}) collective-permute-start(f32[4,16,256]{2,1,0:T(8,128)S(1)} %get-tuple-element.64), channel_id=1, source_target_pairs={{0,8},{8,0},{16,24},{24,16},{1,9},{9,1},{17,25},{25,17},{2,10},{10... | collective-permute-start | bytes 196616 | tf_op jit(solution)/shard_map/ppermute | solution.py:560
  32.8 5.6 %collective-permute-start.9 = (f32[4,16,256]{2,1,0:T(8,128)S(1)}, f32[4,16,256]{2,1,0:T(8,128)S(1)}, u32[]{:S(2)}, u32[]{:S(2)}) collective-permute-start(f32[4,16,256]{2,1,0:T(8,128)S(1)} %get-tuple-element.60), channel_id=1, source_target_pairs={{0,8},{8,0},{16,24},{24,16},{1,9},{9,1},{17,25},{25,17},{2,10},{10... | collective-permute-start | bytes 196616 | tf_op jit(solution)/shard_map/ppermute | solution.py:560
